TPU v7x, 128 devices: a whole 4x4x4 slice. The times are simulated.
128 devices in a mesh: section: 2 (over x_lo), ctx: 16 (over x_hi, y, core), wshard: 4 (over z).
Axes of the slice: x: 4 (x_hi: 2, x_lo: 2; x = x_hi * 2 + x_lo), y: 4, z: 4, core: 2. Of those that a mesh axis runs over, the one named last changes fastest.
Arguments:
- inputs: bfloat16 [2, 4, 2048, 768], P(None, 'wshard', 'ctx'), may hold values from -6 to 6
- cotangent: bfloat16 [2, 4, 2048, 768], P(None, 'wshard', 'ctx'), may hold values from -6 to 6
- attn_gain: bfloat16 [2, 768], P('section', 'wshard'), may hold values from 0.099609375 to 1.8984375
- qkv_weight: bfloat16 [2, 768, 2304], P('section', 'wshard'), may hold values from -0.21875 to 0.21875
- out_weight: bfloat16 [2, 768, 768], P('section', 'wshard'), may hold values from -6 to 6
- mlp_gain: bfloat16 [2, 768], P('section', 'wshard'), may hold values from 0.099609375 to 1.8984375
- up_weight: bfloat16 [2, 768, 2304], P('section', 'wshard'), may hold values from -0.21875 to 0.21875
- down_weight: bfloat16 [2, 1152, 768], P('section', 'wshard'), may hold values from -0.1875 to 0.1875
Outputs:
- activations: bfloat16 [2, 2, 4, 2048, 768], P('section', None, 'wshard', 'ctx')
- input_grads: bfloat16 [2, 2, 4, 2048, 768], P('section', None, 'wshard', 'ctx')
- grad_attn_gain: float32 [2, 768], P('section', 'wshard')
- grad_qkv: float32 [2, 768, 2304], P('section', 'wshard')
- grad_out: float32 [2, 768, 768], P('section', 'wshard')
- grad_mlp_gain: float32 [2, 768], P('section', 'wshard')
- grad_up: float32 [2, 768, 2304], P('section', 'wshard')
- grad_down: float32 [2, 1152, 768], P('section', 'wshard')
All inputs are finite; a program needn't handle non-finite values.
Results may differ from a plain program's by a relative error of at most 0.023.
Values may be sent and summed in bfloat16 or wider, within the bound.
A program may use at most 192 MiB of HBM per device.

v0:
```python
import jax
import jax.numpy as jnp
from jax import lax
from jax.sharding import PartitionSpec as P

D = 768
HEADS = 12
HEAD_DIM = 64
FF = 1152


def passed_along(block, axis, distance):
    devices = range(lax.axis_size(axis))
    route = [(i - distance, i) for i in devices if i - distance in devices]
    return lax.ppermute(block, axis, route)


def for_sending(x):

    def short(part):
        return part.astype(jnp.bfloat16) if part.dtype == jnp.float32 else part

    return jax.tree.map(short, x)


def norm_rows(source):
    centered = source - jnp.mean(source, axis=-1, keepdims=True)
    variance = jnp.mean(centered * centered, axis=-1, keepdims=True)
    return centered * lax.rsqrt(variance + 1e-05)


def scaled_norm(source, scales):
    return norm_rows(source) * scales


def gated_units(gate_up):
    return jax.nn.gelu(gate_up[:, :FF], approximate=False) * gate_up[:, FF:]


def rope_tables(first_row, row_total):
    half_width = HEAD_DIM // 2
    positions = (first_row + lax.iota(jnp.int32, row_total)).astype(jnp.float32)
    frequency = 1.0 / 160000.0 ** (jnp.arange(half_width, dtype=jnp.float32) * 2.0 / HEAD_DIM)
    angles = positions[:, None] * frequency[None, :]
    return (jnp.cos(angles)[:, None, :], jnp.sin(angles)[:, None, :])


def split_heads(matrix):
    return matrix.reshape(matrix.shape[0], HEADS, HEAD_DIM)


def rotate(matrix, cosine_table, sine_table):
    half_width = HEAD_DIM // 2
    heads_in = split_heads(matrix)
    first_half = heads_in[..., :half_width]
    second_half = heads_in[..., half_width:]
    turned = jnp.concatenate(
        [
            first_half * cosine_table - second_half * sine_table,
            second_half * cosine_table + first_half * sine_table,
        ],
        axis=-1,
    )
    return turned.reshape(matrix.shape)


def rotate_back(matrix, cosine_table, sine_table):
    half_width = HEAD_DIM // 2
    heads_in = split_heads(matrix)
    first_half = heads_in[..., :half_width]
    second_half = heads_in[..., half_width:]
    turned = jnp.concatenate(
        [
            first_half * cosine_table + second_half * sine_table,
            second_half * cosine_table - first_half * sine_table,
        ],
        axis=-1,
    )
    return turned.reshape(matrix.shape)


def forward_layer(source, weights, cosine_table, sine_table):
    gain_one, qkv_weight, out_weight, gain_two, up_weight, down_weight = weights
    rows_here = source.shape[0]
    score_scale = HEAD_DIM ** (-0.5)
    source_wide = source.astype(jnp.float32)
    normed = scaled_norm(source_wide, gain_one.astype(jnp.float32)).astype(jnp.bfloat16)
    projected = jnp.dot(normed, qkv_weight, preferred_element_type=jnp.float32)
    queries = rotate(projected[:, :D], cosine_table, sine_table).astype(jnp.bfloat16)
    key_rows = rotate(projected[:, D : 2 * D], cosine_table, sine_table).astype(jnp.bfloat16)
    values = projected[:, 2 * D :].astype(jnp.bfloat16)
    keys_all, values_all = (
        lax.all_gather(key_rows, "ctx", axis=0, tiled=True),
        lax.all_gather(values, "ctx", axis=0, tiled=True),
    )
    scores = (
        jnp.einsum(
            "qhd,khd->hqk",
            split_heads(queries),
            split_heads(keys_all),
            preferred_element_type=jnp.float32,
        )
        * score_scale
    )
    totals = jax.nn.logsumexp(scores, axis=-1)
    probs = jnp.exp(scores - totals[..., None]).astype(jnp.bfloat16)
    attended = jnp.einsum(
        "hqk,khd->qhd", probs, split_heads(values_all), preferred_element_type=jnp.float32
    ).reshape(rows_here, D)
    attended_low = attended.astype(jnp.bfloat16)
    hidden = source_wide + jnp.dot(attended_low, out_weight, preferred_element_type=jnp.float32)
    normed_two = scaled_norm(hidden, gain_two.astype(jnp.float32)).astype(jnp.bfloat16)
    gate_up = jnp.dot(normed_two, up_weight, preferred_element_type=jnp.float32)
    product = gated_units(gate_up).astype(jnp.bfloat16)
    output = (hidden + jnp.dot(product, down_weight, preferred_element_type=jnp.float32)).astype(
        jnp.bfloat16
    )
    stored = (
        source_wide,
        normed,
        queries,
        key_rows,
        values,
        attended,
        attended_low,
        totals,
        hidden,
        normed_two,
        gate_up,
        product,
        keys_all,
        values_all,
    )
    return (output, stored)


def attention_back(queries, key_rows, values, grad_attended, totals, row_delta):
    rows_here = queries.shape[0]
    score_scale = HEAD_DIM ** (-0.5)
    keys_all, values_all = (
        lax.all_gather(key_rows, "ctx", axis=0, tiled=True),
        lax.all_gather(values, "ctx", axis=0, tiled=True),
    )
    length_all = keys_all.shape[0]
    scores = (
        jnp.einsum(
            "qhd,khd->hqk",
            split_heads(queries),
            split_heads(keys_all),
            preferred_element_type=jnp.float32,
        )
        * score_scale
    )
    probs = jnp.exp(scores - totals[..., None])
    grad_probs = jnp.einsum(
        "qhd,khd->hqk",
        split_heads(grad_attended),
        split_heads(values_all),
        preferred_element_type=jnp.float32,
    )
    grad_scores = (probs * (grad_probs - row_delta[..., None])).astype(jnp.bfloat16)
    grad_queries = (
        jnp.einsum(
            "hqk,khd->qhd", grad_scores, split_heads(keys_all), preferred_element_type=jnp.float32
        ).reshape(rows_here, D)
        * score_scale
    )
    grad_keys_all = (
        jnp.einsum(
            "hqk,qhd->khd", grad_scores, split_heads(queries), preferred_element_type=jnp.float32
        ).reshape(length_all, D)
        * score_scale
    )
    grad_values_all = jnp.einsum(
        "hqk,qhd->khd",
        probs.astype(jnp.bfloat16),
        split_heads(grad_attended),
        preferred_element_type=jnp.float32,
    ).reshape(length_all, D)
    partial_terms = jnp.concatenate([grad_keys_all, grad_values_all], axis=1)
    owned = lax.psum_scatter(
        partial_terms.astype(jnp.bfloat16), "ctx", scatter_dimension=0, tiled=True
    ).astype(jnp.float32)
    grad_keys = owned[:, :D]
    grad_values = owned[:, D:]
    return (grad_queries, grad_keys, grad_values)


def backward_layer(grad_output, stored, weights, cosine_table, sine_table):
    gain_one, qkv_weight, out_weight, gain_two, up_weight, down_weight = weights
    (
        source_wide,
        normed,
        queries,
        key_rows,
        values,
        attended,
        attended_low,
        totals,
        hidden,
        normed_two,
        gate_up,
        product,
        keys_kept,
        values_kept,
    ) = stored
    grad_mlp = grad_output.astype(jnp.bfloat16)
    grad_down = jnp.einsum("cf,cd->fd", product, grad_mlp, preferred_element_type=jnp.float32)
    grad_product = jnp.einsum(
        "cd,fd->cf", grad_mlp, down_weight, preferred_element_type=jnp.float32
    )
    gated_back = jax.vjp(gated_units, gate_up)[1]
    grad_gate_up = gated_back(grad_product)[0].astype(jnp.bfloat16)
    grad_up = jnp.einsum("cd,ce->de", normed_two, grad_gate_up, preferred_element_type=jnp.float32)
    grad_normed_two = jnp.einsum(
        "ce,de->cd", grad_gate_up, up_weight, preferred_element_type=jnp.float32
    )
    norm_two_back = jax.vjp(scaled_norm, hidden, gain_two.astype(jnp.float32))[1]
    hidden_part, grad_gain_two = norm_two_back(grad_normed_two)
    grad_hidden = grad_output + hidden_part
    grad_branch = grad_hidden.astype(jnp.bfloat16)
    grad_out_weight = jnp.einsum(
        "cd,ce->de", attended_low, grad_branch, preferred_element_type=jnp.float32
    )
    grad_attended = jnp.einsum(
        "ce,de->cd", grad_branch, out_weight, preferred_element_type=jnp.float32
    ).astype(jnp.bfloat16)
    row_delta = jnp.einsum(
        "qhd,qhd->hq", split_heads(grad_attended.astype(jnp.float32)), split_heads(attended)
    )
    grad_queries, grad_keys, grad_values = attention_back(
        queries, key_rows, values, grad_attended, totals, row_delta
    )
    grad_projected = jnp.concatenate(
        [
            rotate_back(grad_queries, cosine_table, sine_table),
            rotate_back(grad_keys, cosine_table, sine_table),
            grad_values,
        ],
        axis=1,
    ).astype(jnp.bfloat16)
    grad_qkv = jnp.einsum("cd,ce->de", normed, grad_projected, preferred_element_type=jnp.float32)
    grad_normed = jnp.einsum(
        "ce,de->cd", grad_projected, qkv_weight, preferred_element_type=jnp.float32
    )
    norm_one_back = jax.vjp(scaled_norm, source_wide, gain_one.astype(jnp.float32))[1]
    source_part, grad_gain_one = norm_one_back(grad_normed)
    grad_source = grad_hidden + source_part
    return (
        grad_source,
        (grad_gain_one, grad_qkv, grad_out_weight, grad_gain_two, grad_up, grad_down),
    )


def local(inputs, cotangent, attn_gain, qkv_weight, out_weight, mlp_gain, up_weight, down_weight):
    gathered = (
        lax.all_gather(attn_gain, "wshard", axis=1, tiled=True),
        lax.all_gather(qkv_weight, "wshard", axis=1, tiled=True),
        lax.all_gather(out_weight, "wshard", axis=1, tiled=True),
        lax.all_gather(mlp_gain, "wshard", axis=1, tiled=True),
        lax.all_gather(up_weight, "wshard", axis=1, tiled=True),
        lax.all_gather(down_weight, "wshard", axis=1, tiled=True),
    )
    weights = tuple((w[0] for w in gathered))
    first_section = lax.axis_index("section") == 0
    rows_here = inputs.shape[2]
    micro_count = inputs.shape[0]
    cosine_table, sine_table = rope_tables(lax.axis_index("ctx") * rows_here, rows_here)
    received = jnp.zeros((rows_here, D), jnp.bfloat16)
    outputs = []
    stored_all = []
    for tick_index in range(micro_count + 1):
        fresh = inputs[tick_index, 0] if tick_index < micro_count else jnp.zeros_like(received)
        source = jnp.where(first_section, fresh, received)
        output, stored = forward_layer(source, weights, cosine_table, sine_table)
        outputs.append(output)
        stored_all.append(stored)
        if tick_index < micro_count:
            received = passed_along(output, "section", 1)
    summed = tuple((jnp.zeros(w.shape, jnp.float32) for w in weights))
    returned = jnp.zeros((rows_here, D), jnp.bfloat16)
    sent_grads = []
    for tick_index in range(micro_count + 1):
        if tick_index < micro_count:
            fresh_grad = cotangent[micro_count - 1 - tick_index, 0].astype(jnp.float32)
        else:
            fresh_grad = jnp.zeros((rows_here, D), jnp.float32)
        incoming = jnp.where(first_section, returned.astype(jnp.float32), fresh_grad)
        grad_source, layer_grads = backward_layer(
            incoming, stored_all[micro_count - tick_index], weights, cosine_table, sine_table
        )
        summed = tuple((x + y for x, y in zip(summed, layer_grads)))
        sent_back = grad_source.astype(jnp.bfloat16)
        sent_grads.append(sent_back)
        if tick_index < micro_count:
            returned = passed_along(sent_back, "section", -1)
    activations = jnp.stack(
        [jnp.where(first_section, outputs[m], outputs[m + 1]) for m in range(micro_count)]
    )[None, :, None]
    input_grads = jnp.stack(
        [
            jnp.where(first_section, sent_grads[micro_count - m], sent_grads[micro_count - 1 - m])
            for m in range(micro_count)
        ]
    )[None, :, None]
    shards = jax.tree.map(
        lambda part: part.astype(jnp.float32),
        lax.psum_scatter(for_sending(summed), "wshard", scatter_dimension=0, tiled=True),
    )
    reduced = jax.tree.map(
        lambda part: part.astype(jnp.float32), lax.psum(for_sending(shards), "ctx")
    )
    return (
        activations,
        input_grads,
        reduced[0][None],
        reduced[1][None],
        reduced[2][None],
        reduced[3][None],
        reduced[4][None],
        reduced[5][None],
    )


def solution(mesh):
    placed = (
        P(None, "wshard", "ctx", None),
        P(None, "wshard", "ctx", None),
        P("section", "wshard"),
        P("section", "wshard", None),
        P("section", "wshard", None),
        P("section", "wshard"),
        P("section", "wshard", None),
        P("section", "wshard", None),
    )
    return jax.shard_map(
        local,
        mesh=mesh,
        in_specs=placed,
        out_specs=(
            P("section", None, "wshard", "ctx", None),
            P("section", None, "wshard", "ctx", None),
            P("section", "wshard"),
            P("section", "wshard", None),
            P("section", "wshard", None),
            P("section", "wshard"),
            P("section", "wshard", None),
            P("section", "wshard", None),
        ),
        check_vma=False,
    )
```

profile of v0, /device:TPU:25, one launch (start us, length us, event | category | flops | bytes accessed | tf_op | source)
XLA Modules:
  0.0 1254.8 jit_solution(6007797569199307270)
XLA Ops:
  11.8 9.7 all-reduce.13
  24.0 30.9 %all-gather.11.cloned.1.call-done = bf16[1,768,2304]{2,1,0:T(8,128)(2,1)} async-done(((bf16[1,192,2304]{2,1,0:T(8,128)(2,1)}), bf16[1,768,2304]{2,1,0:T(8,128)(2,1)}) %all-gather.11.cloned.1.call-update) | async-done | bytes 3538960 | tf_op jit(solution)/shard_map/all_gather | solution.py:258
  61.6 47.9 %all-gather.15.cloned.1.call-done = bf16[2048,768]{0,1:T(8,128)(2,1)} async-done(((bf16[128,768]{0,1:T(8,128)(2,1)}), bf16[2048,768]{0,1:T(8,128)(2,1)}) %all-gather.15.cloned.1.call-update) | async-done | bytes 3145744 | tf_op jit(solution)/shard_map/all_gather | solution.py:93
  117.9 44.7 %all-gather.13.cloned.1.call-done = bf16[2048,768]{1,0:T(8,128)(2,1)} async-done(((bf16[128,768]{1,0:T(8,128)(2,1)}), bf16[2048,768]{1,0:T(8,128)(2,1)}) %all-gather.13.cloned.1.call-update) | async-done | bytes 3145744 | tf_op jit(solution)/shard_map/all_gather | solution.py:94
  165.7 8.9 bitcast_convert_fusion.3
  174.7 11.8 all-gather.17.cloned.1.call-done
  188.6 43.9 %all-gather.19.cloned.1.call-done = bf16[1,768,2304]{2,1,0:T(8,128)(2,1)} async-done(((bf16[1,192,2304]{2,1,0:T(8,128)(2,1)}), bf16[1,768,2304]{2,1,0:T(8,128)(2,1)}) %all-gather.19.cloned.1.call-update) | async-done | bytes 3538960 | tf_op jit(solution)/shard_map/all_gather | solution.py:261
  238.4 24.1 %all-gather.21.cloned.1.call-done = bf16[1,1152,768]{2,1,0:T(8,128)(2,1)} async-done(((bf16[1,288,768]{2,1,0:T(8,128)(2,1)}), bf16[1,1152,768]{2,1,0:T(8,128)(2,1)}) %all-gather.21.cloned.1.call-update) | async-done | bytes 1769488 | tf_op jit(solution)/shard_map/all_gather | solution.py:262
  278.7 49.8 %all-gather.25.cloned.1.call-done = bf16[2048,768]{0,1:T(8,128)(2,1)} async-done(((bf16[128,768]{0,1:T(8,128)(2,1)}), bf16[2048,768]{0,1:T(8,128)(2,1)}) %all-gather.25.cloned.1.call-update) | async-done | bytes 3145744 | tf_op jit(solution)/shard_map/all_gather | solution.py:93
  337.5 44.0 %all-gather.23.cloned.1.call-done = bf16[2048,768]{1,0:T(8,128)(2,1)} async-done(((bf16[128,768]{1,0:T(8,128)(2,1)}), bf16[2048,768]{1,0:T(8,128)(2,1)}) %all-gather.23.cloned.1.call-update) | async-done | bytes 3145744 | tf_op jit(solution)/shard_map/all_gather | solution.py:94
  386.3 8.8 bitcast_convert_fusion.2
  417.2 50.0 %all-gather.29.cloned.1.call-done = bf16[2048,768]{0,1:T(8,128)(2,1)} async-done(((bf16[128,768]{0,1:T(8,128)(2,1)}), bf16[2048,768]{0,1:T(8,128)(2,1)}) %all-gather.29.cloned.1.call-update) | async-done | bytes 3145744 | tf_op jit(solution)/shard_map/all_gather | solution.py:93
  476.3 43.3 %all-gather.27.cloned.1.call-done = bf16[2048,768]{1,0:T(8,128)(2,1)} async-done(((bf16[128,768]{1,0:T(8,128)(2,1)}), bf16[2048,768]{1,0:T(8,128)(2,1)}) %all-gather.27.cloned.1.call-update) | async-done | bytes 3145744 | tf_op jit(solution)/shard_map/all_gather | solution.py:94
  524.3 8.7 bitcast_convert_fusion.1
  544.1 7.4 convolution_convert_fusion.2
  551.6 7.2 multiply_convert_fusion.2
  564.6 8.6 copy.90
  580.0 80.0 %reduce-scatter.22.cloned.1.call-done = bf16[128,1536]{1,0:T(8,128)(2,1)} async-done(((bf16[2048,1536]{1,0:T(8,128)(2,1)}), bf16[128,1536]{1,0:T(8,128)(2,1)}) %reduce-scatter.22.cloned.1.call-update) | async-done | bytes 393232
  686.3 7.4 convolution_convert_fusion.1
  706.5 8.6 copy.92
  722.0 82.3 %reduce-scatter.24.cloned.1.call-done = bf16[128,1536]{1,0:T(8,128)(2,1)} async-done(((bf16[2048,1536]{1,0:T(8,128)(2,1)}), bf16[128,1536]{1,0:T(8,128)(2,1)}) %reduce-scatter.24.cloned.1.call-update) | async-done | bytes 393232
  829.1 7.4 convolution_convert_fusion
  836.6 7.0 multiply_convert_fusion
  849.4 8.7 copy.94
  886.8 60.5 %reduce-scatter.26.cloned.1.call-done = bf16[128,1536]{1,0:T(8,128)(2,1)} async-done(((bf16[2048,1536]{1,0:T(8,128)(2,1)}), bf16[128,1536]{1,0:T(8,128)(2,1)}) %reduce-scatter.26.cloned.1.call-update) | async-done | bytes 393232
  948.9 8.1 add_convert_fusion.1
  957.2 16.9 %reduce-scatter.16.cloned.1.call-done = bf16[192,768]{1,0:T(8,128)(2,1)} async-done(((bf16[768,768]{1,0:T(8,128)(2,1)}), bf16[192,768]{1,0:T(8,128)(2,1)}) %reduce-scatter.16.cloned.1.call-update) | async-done | bytes 294928 | tf_op jit(solution)/shard_map/reduce_scatter | solution.py:308
  974.1 30.9 %reduce-scatter.20.cloned.1.call-done = bf16[288,768]{1,0:T(8,128)(2,1)} async-done(((bf16[1152,768]{1,0:T(8,128)(2,1)}), bf16[288,768]{1,0:T(8,128)(2,1)}) %reduce-scatter.20.cloned.1.call-update) | async-done | bytes 442384 | tf_op jit(solution)/shard_map/reduce_scatter | solution.py:308
  1005.0 43.6 %reduce-scatter.18.cloned.1.call-done = bf16[192,2304]{1,0:T(8,128)(2,1)} async-done(((bf16[768,2304]{1,0:T(8,128)(2,1)}), bf16[192,2304]{1,0:T(8,128)(2,1)}) %reduce-scatter.18.cloned.1.call-update) | async-done | bytes 884752 | tf_op jit(solution)/shard_map/reduce_scatter | solution.py:308
  1048.6 43.6 %reduce-scatter.14.cloned.1.call-done = bf16[192,2304]{1,0:T(8,128)(2,1)} async-done(((bf16[768,2304]{1,0:T(8,128)(2,1)}), bf16[192,2304]{1,0:T(8,128)(2,1)}) %reduce-scatter.14.cloned.1.call-update) | async-done | bytes 884752 | tf_op jit(solution)/shard_map/reduce_scatter | solution.py:308
  1106.3 32.6 %all-reduce.10 = (bf16[1,192]{1,0:T(2,128)(2,1)S(1)}, bf16[1,192]{1,0:T(2,128)(2,1)S(1)}) all-reduce(bf16[1,192]{1,0:T(2,128)(2,1)S(1)} %broadcast_in_dim.72, bf16[1,192]{1,0:T(2,128)(2,1)S(1)} %broadcast_in_dim.151), channel_id=1, replica_groups=mesh['section'=2,'ctx'=16,'wshard'=4] {'ctx'}, use_global_device_ids=true, to_apply=%region_37.38 | all-reduce | flops 384 | bytes 1536 | tf_op jit(solution)/shard_map/psum | solution.py:311
  1143.3 97.5 %all-reduce.16.cloned.1.call-done = (bf16[1,192,2304]{2,1,0:T(8,128)(2,1)}, bf16[1,192,768]{2,1,0:T(8,128)(2,1)}, bf16[1,192,2304]{2,1,0:T(8,128)(2,1)}, bf16[1,288,768]{2,1,0:T(8,128)(2,1)}) async-done(((bf16[1,192,2304]{2,1,0:T(8,128)(2,1)}, bf16[1,192,768]{2,1,0:T(8,128)(2,1)}, bf16[1,192,2304]{2,1,0:T(8,128)(2,1)}, bf16[1,288,768]{2,1,0:T(8,128)(2,1)}), (bf16[1,192,2304]{2,1,0:T(8,128)(2,1)}, ...) | async-done | bytes 2506768 | tf_op jit(solution)/shard_map/psum | solution.py:311
  (588 shorter events, 251.4 us)
Async XLA Ops:
  7.2 47.7 %all-gather.11.cloned.1.call-start = ((), (), s32[]{:S(2)}) async-start(), calls=%async_computation.7 | async-start | bytes 4423680 | tf_op jit(solution)/shard_map/all_gather | solution.py:258
  7.9 101.6 %all-gather.15.cloned.1.call-start = ((), (), s32[]{:S(2)}) async-start(), calls=%async_computation.9 | async-start | bytes 3342336 | tf_op jit(solution)/shard_map/all_gather | solution.py:93
  59.0 103.5 %all-gather.13.cloned.1.call-start = ((), (), s32[]{:S(2)}) async-start(), calls=%async_computation.8 | async-start | bytes 3342336 | tf_op jit(solution)/shard_map/all_gather | solution.py:94
  59.8 126.7 %all-gather.17.cloned.1.call-start = ((), (), s32[]{:S(2)}) async-start(), calls=%async_computation.10 | async-start | bytes 1474560 | tf_op jit(solution)/shard_map/all_gather | solution.py:259
  60.3 172.1 %all-gather.19.cloned.1.call-start = ((), (), s32[]{:S(2)}) async-start(), calls=%async_computation.11 | async-start | bytes 4423680 | tf_op jit(solution)/shard_map/all_gather | solution.py:261
  60.9 201.5 %all-gather.21.cloned.1.call-start = ((), (), s32[]{:S(2)}) async-start(), calls=%async_computation.12 | async-start | bytes 2211840 | tf_op jit(solution)/shard_map/all_gather | solution.py:262
  61.5 267.0 %all-gather.25.cloned.1.call-start = ((), (), s32[]{:S(2)}) async-start(), calls=%async_computation.14 | async-start | bytes 3342336 | tf_op jit(solution)/shard_map/all_gather | solution.py:93
  264.5 6.7 collective-permute-start
  276.0 56.3 %copy-start.93 = (bf16[128,12,32]{0,2,1:T(8,128)(2,1)}, bf16[128,12,32]{0,2,1:T(8,128)(2,1)S(1)}, u32[]{:S(2)}) copy-start(bf16[128,12,32]{0,2,1:T(8,128)(2,1)S(1)} %get-tuple-element.98) | copy-start | bytes 294916
  276.7 104.8 %all-gather.23.cloned.1.call-start = ((), (), s32[]{:S(2)}) async-start(), calls=%async_computation.13 | async-start | bytes 3342336 | tf_op jit(solution)/shard_map/all_gather | solution.py:94
  278.7 188.6 %all-gather.29.cloned.1.call-start = ((), (), s32[]{:S(2)}) async-start(), calls=%async_computation.16 | async-start | bytes 3342336 | tf_op jit(solution)/shard_map/all_gather | solution.py:93
  399.6 6.2 collective-permute-start.1
  415.4 104.2 %all-gather.27.cloned.1.call-start = ((), (), s32[]{:S(2)}) async-start(), calls=%async_computation.15 | async-start | bytes 3342336 | tf_op jit(solution)/shard_map/all_gather | solution.py:94
  417.2 242.9 %reduce-scatter.22.cloned.1.call-start = ((), (), s32[]{:S(2)}) async-start(), calls=%async_computation.21 | async-start | bytes 6684672
  573.2 231.1 %reduce-scatter.24.cloned.1.call-start = ((), (), s32[]{:S(2)}) async-start(), calls=%async_computation.22 | async-start | bytes 6684672
  673.0 6.4 collective-permute-start.2
  715.2 232.1 %reduce-scatter.26.cloned.1.call-start = ((), (), s32[]{:S(2)}) async-start(), calls=%async_computation.23 | async-start | bytes 6684672
  818.0 6.4 collective-permute-start.3
  858.1 115.9 %reduce-scatter.16.cloned.1.call-start = ((), (), s32[]{:S(2)}) async-start(), calls=%async_computation.18 | async-start | bytes 1474560 | tf_op jit(solution)/shard_map/reduce_scatter | solution.py:308
  861.6 143.4 %reduce-scatter.20.cloned.1.call-start = ((), (), s32[]{:S(2)}) async-start(), calls=%async_computation.20 | async-start | bytes 2211840 | tf_op jit(solution)/shard_map/reduce_scatter | solution.py:308
  865.6 183.0 %reduce-scatter.18.cloned.1.call-start = ((), (), s32[]{:S(2)}) async-start(), calls=%async_computation.19 | async-start | bytes 4423680 | tf_op jit(solution)/shard_map/reduce_scatter | solution.py:308
  871.6 220.5 %reduce-scatter.14.cloned.1.call-start = ((), (), s32[]{:S(2)}) async-start(), calls=%async_computation.17 | async-start | bytes 4423680 | tf_op jit(solution)/shard_map/reduce_scatter | solution.py:308
  881.1 67.6 %copy-start.99 = (f32[128,32]{0,1:T(8,128)S(1)}, f32[128,32]{0,1:T(8,128)}, u32[]{:S(2)}) copy-start(f32[128,32]{0,1:T(8,128)} %copy-done.98) | copy-start | bytes 49156
  881.1 67.6 %copy-start.101 = (f32[128,32]{0,1:T(8,128)S(1)}, f32[128,32]{0,1:T(8,128)}, u32[]{:S(2)}) copy-start(f32[128,32]{0,1:T(8,128)} %copy-done.100) | copy-start | bytes 49156
  886.7 62.2 %copy-start.40 = (bf16[2,1,128,768]{3,2,1,0:T(8,128)(2,1)S(1)}, bf16[2,1,128,768]{3,2,1,0:T(8,128)(2,1)}, u32[]{:S(2)}) copy-start(bf16[2,1,128,768]{3,2,1,0:T(8,128)(2,1)} %param.8) | copy-start | bytes 1179652
  886.8 62.1 %copy-start.146 = (f32[128]{0:T(128)S(1)}, f32[128]{0:T(128)}, u32[]{:S(2)}) copy-start(f32[128]{0:T(128)} %copy-done.145) | copy-start | bytes 1540
  886.8 62.1 %copy-start.163 = (f32[128]{0:T(128)S(1)}, f32[128]{0:T(128)}, u32[]{:S(2)}) copy-start(f32[128]{0:T(128)} %copy-done.162) | copy-start | bytes 1540
  957.1 139.8 %copy-start.140 = (f32[768]{0:T(1024)S(1)}, f32[768]{0:T(1024)}, u32[]{:S(2)}) copy-start(f32[768]{0:T(1024)} %get-tuple-element.36) | copy-start | bytes 9220
  957.1 139.7 %copy-start.142 = (f32[768]{0:T(1024)S(1)}, f32[768]{0:T(1024)}, u32[]{:S(2)}) copy-start(f32[768]{0:T(1024)} %get-tuple-element.34) | copy-start | bytes 9220
  957.1 139.7 %copy-start.144 = (f32[768]{0:T(1024)S(1)}, f32[768]{0:T(1024)}, u32[]{:S(2)}) copy-start(f32[768]{0:T(1024)} %get-tuple-element.38) | copy-start | bytes 9220
  957.1 140.3 %copy-start.13 = (bf16[1,768,2304]{2,1,0:T(8,128)(2,1)S(1)}, bf16[1,768,2304]{2,1,0:T(8,128)(2,1)}, u32[]{:S(2)}) copy-start(bf16[1,768,2304]{2,1,0:T(8,128)(2,1)} %all-gather.11.cloned.1.call-done) | copy-start | bytes 10616836
  957.1 283.7 %all-reduce.16.cloned.1.call-start = ((), (), s32[]{:S(2)}) async-start(), calls=%async_computation.24 | async-start | bytes 5013504 | tf_op jit(solution)/shard_map/psum | solution.py:311
  (172 other events, 1261.3 us)
Sparse Core Ops, SparseCore 0:
  9.7 45.1 all-gather.10
  59.1 50.2 all-gather.14
  112.5 49.9 all-gather.12
  164.0 22.4 all-gather.16
  188.0 44.4 all-gather.18
  234.0 28.4 all-gather.20
  276.8 51.6 all-gather.24
  331.5 49.9 all-gather.22
  415.5 51.6 all-gather.28
  469.6 49.9 all-gather.26
  573.3 86.6 reduce-scatter.21
  715.3 88.9 reduce-scatter.23
  858.2 88.9 reduce-scatter.25
  950.2 23.7 reduce-scatter.15
  977.0 27.9 reduce-scatter.19
  1007.3 41.2 reduce-scatter.17
  1050.8 41.2 reduce-scatter.13
  1094.7 146.0 all-reduce.15
where the time goes:
time: 1270 us; the launch traced here: 1250 us
  waiting for transfers between devices  866 us (68%)
  matrix products  169 us (13%)
  local copies, waits for them, and re-layouts  86.7 us (7%)
  other arithmetic  57 us (4%)
  blocking collectives  48.9 us (4%)
  between operations  18.6 us (1%)
    unnamed x21, waiting for transfers between devices  225 us
    all_gather x3, waiting for transfers between devices, forward_layer(): lax.all_gather(key_rows, 'ctx', axis=0, tiled=True)  148 us
    reduce_scatter x4, waiting for transfers between devices, local(): lax.psum_scatter(for_sending(summed), 'wshard', scatter_dimension=0, tile...  135 us
    all_gather x3, waiting for transfers between devices, forward_layer(): lax.all_gather(values, 'ctx', axis=0, tiled=True)  132 us
    psum x1, waiting for transfers between devices, local(): lax.psum(for_sending(shards), 'ctx')  97.5 us
    unnamed x380, local copies, waits for them, and re-layouts  56.1 us
    all_gather x1, waiting for transfers between devices, local(): lax.all_gather(up_weight, 'wshard', axis=1, tiled=True)  43.9 us
    psum x1, blocking collectives, local(): lax.psum(for_sending(shards), 'ctx')  32.6 us
  transfers between devices with their start and end apart: 22, of which 22 were waited for; matrix products, arithmetic and copies ran while one was open for 9% of the time, Pallas kernels for 0%

commit v1 on v0

v1 whole, which is shorter than its diff:
```python
import functools

import jax
import jax.numpy as jnp
from jax import lax
from jax.experimental import pallas as pl
from jax.experimental.pallas import tpu as pltpu
from jax.sharding import PartitionSpec as P

D = 768
HEADS = 12
HEAD_DIM = 64
FF = 1152
ROWS = 128
GROUPS = 4
GH = HEADS // GROUPS
GW = GH * HEAD_DIM
CTX = 16
SCALE = HEAD_DIM ** (-0.5)
F32 = jnp.float32
BF16 = jnp.bfloat16
MESH = pl.DeviceIdType.MESH
DMA = pltpu.SemaphoreType.DMA
ANY = pl.BlockSpec(memory_space=pl.ANY)
VM = pl.BlockSpec(memory_space=pltpu.VMEM)
VMEM_LIMIT = 56 * 1024 * 1024


def dot(a, b):
    return jnp.dot(a, b, preferred_element_type=F32)


def dot_nt(a, b):
    return lax.dot_general(a, b, (((1,), (1,)), ((), ())), preferred_element_type=F32)


def sds(shape, dtype):
    return jax.ShapeDtypeStruct(shape, dtype)


def compute_call(kernel, args, outs, scratch=(), name=None):
    return pl.pallas_call(
        kernel,
        out_shape=outs,
        in_specs=[VM] * len(args),
        out_specs=jax.tree.map(lambda _: VM, outs),
        scratch_shapes=list(scratch),
        compiler_params=pltpu.CompilerParams(vmem_limit_bytes=VMEM_LIMIT),
        name=name,
    )(*args)


def norm_parts(source):
    centered = source - jnp.mean(source, axis=-1, keepdims=True)
    variance = jnp.mean(centered * centered, axis=-1, keepdims=True)
    rstd = lax.rsqrt(variance + 1e-05)
    return centered * rstd, rstd


def norm_back(grad, normalized, rstd, gain):
    inner = grad * gain
    mean_one = jnp.mean(inner, axis=-1, keepdims=True)
    mean_two = jnp.mean(inner * normalized, axis=-1, keepdims=True)
    grad_gain = jnp.sum(grad * normalized, axis=0, keepdims=True)
    return rstd * (inner - mean_one - normalized * mean_two), grad_gain


def qkv_kernel(x_ref, gain_ref, w_ref, cos_ref, sin_ref, qkv_ref, normed_ref):
    normalized, _ = norm_parts(x_ref[...].astype(F32))
    normed = (normalized * gain_ref[...].astype(F32)).astype(BF16)
    normed_ref[...] = normed
    cos = cos_ref[...]
    sin = sin_ref[...]
    for part in range(3):
        for block in range(3):
            at = part * D + block * 256
            turned = dot(normed, w_ref[:, at : at + 256]).T
            for head_at in range(4):
                head = block * 4 + head_at
                one = turned[head_at * 64 : head_at * 64 + 32]
                two = turned[head_at * 64 + 32 : head_at * 64 + 64]
                if part < 2:
                    one, two = one * cos - two * sin, two * cos + one * sin
                if part == 0:
                    one, two = one * SCALE, two * SCALE
                row = part * GW + (head % GH) * HEAD_DIM
                qkv_ref[head // GH, row : row + 32, :] = one.astype(BF16)
                qkv_ref[head // GH, row + 32 : row + 64, :] = two.astype(BF16)


CHUNK = 256
CHUNKS = 2048 // CHUNK
PAIR = CHUNK // ROWS


def attend_kernel(q_ref, kv_ref, low_ref, wide_ref, totals_ref, s_ref):
    @pl.loop(0, GH)
    def _(h):
        at = pl.multiple_of(h * HEAD_DIM, HEAD_DIM)
        value_at = pl.multiple_of(h * HEAD_DIM + GW, HEAD_DIM)
        qt = jnp.concatenate([q_ref[i, pl.ds(at, HEAD_DIM), :] for i in range(4)], axis=1)
        top = jnp.full((8, 512), -jnp.inf, F32)
        for c in range(CHUNKS):
            keys = jnp.concatenate(
                [kv_ref[c * PAIR + i, pl.ds(at, HEAD_DIM), :].T for i in range(PAIR)], axis=0
            )
            scores = dot(keys, qt)
            s_ref[c * CHUNK : (c + 1) * CHUNK, :] = scores
            top = jnp.maximum(top, jnp.max(scores.reshape(CHUNK // 8, 8, 512), axis=0))
        top = jnp.max(top, axis=0, keepdims=True)
        total = jnp.zeros((8, 512), F32)
        acc = jnp.zeros((HEAD_DIM, 512), F32)
        for c in range(CHUNKS):
            p = jnp.exp(s_ref[c * CHUNK : (c + 1) * CHUNK, :] - top)
            total = total + jnp.sum(p.reshape(CHUNK // 8, 8, 512), axis=0)
            values = jnp.concatenate(
                [kv_ref[c * PAIR + i, pl.ds(value_at, HEAD_DIM), :] for i in range(PAIR)], axis=1
            )
            acc = acc + dot(values, p.astype(BF16))
        total = jnp.sum(total, axis=0, keepdims=True)
        out = acc / total
        totals_ref[h] = jnp.broadcast_to(top + jnp.log(total), (8, 512))
        for i in range(4):
            piece = out[:, i * ROWS : (i + 1) * ROWS]
            wide_ref[i, pl.ds(at, HEAD_DIM), :] = piece
            low_ref[i, pl.ds(at, HEAD_DIM), :] = piece.astype(BF16)


def attend_back_kernel(q_ref, kv_ref, wide_ref, totals_ref, do_ref, dq_ref, dkv_ref):
    @pl.loop(0, GH)
    def _(h):
        at = pl.multiple_of(h * HEAD_DIM, HEAD_DIM)
        value_at = pl.multiple_of(h * HEAD_DIM + GW, HEAD_DIM)
        out_at = pl.multiple_of(h * ROWS, ROWS)
        qt = jnp.concatenate([q_ref[i, pl.ds(at, HEAD_DIM), :] for i in range(4)], axis=1)
        dot_t = jnp.concatenate([do_ref[i, pl.ds(at, HEAD_DIM), :] for i in range(4)], axis=1)
        wide = jnp.concatenate([wide_ref[i, pl.ds(at, HEAD_DIM), :] for i in range(4)], axis=1)
        delta = jnp.sum(wide * dot_t.astype(F32), axis=0, keepdims=True)
        totals = totals_ref[h, 0:1, :]
        zero = jnp.zeros((512, HEAD_DIM), BF16)
        sides = jnp.concatenate(
            [
                jnp.concatenate([qt.T, zero], axis=1),
                jnp.concatenate([zero, dot_t.T], axis=1),
            ],
            axis=0,
        )

        def step(c, acc):
            keys_t = [kv_ref[c * PAIR + i, pl.ds(at, HEAD_DIM), :] for i in range(PAIR)]
            values_t = [kv_ref[c * PAIR + i, pl.ds(value_at, HEAD_DIM), :] for i in range(PAIR)]
            keys = jnp.concatenate([k.T for k in keys_t], axis=0)
            values = jnp.concatenate([v.T for v in values_t], axis=0)
            p = jnp.exp(dot(keys, qt) - totals)
            ds = (p * (dot(values, dot_t) - delta)).astype(BF16)
            both = jnp.concatenate([ds, p.astype(BF16)], axis=1)
            grads = dot(both, sides).astype(BF16)
            for i in range(PAIR):
                dkv_ref[c * PAIR + i, pl.ds(out_at, ROWS), :] = grads[i * ROWS : (i + 1) * ROWS]
            return acc + dot(jnp.concatenate(keys_t, axis=1), ds)

        acc = lax.fori_loop(0, CHUNKS, step, jnp.zeros((HEAD_DIM, 512), F32)) * SCALE
        for i in range(4):
            dq_ref[i, pl.ds(at, HEAD_DIM), :] = acc[:, i * ROWS : (i + 1) * ROWS].astype(BF16)


def mlp_kernel(
    ot_ref, x_ref, gain_ref, wo_ref, wu_ref, wd_ref,
    out_ref, hidden_ref, gate_up_ref, normed_ref, product_ref,
):
    attended = ot_ref[...].astype(F32).T.astype(BF16)
    hidden = x_ref[...].astype(F32) + dot(attended, wo_ref[...])
    hidden_ref[...] = hidden
    normalized, _ = norm_parts(hidden)
    normed = (normalized * gain_ref[...].astype(F32)).astype(BF16)
    normed_ref[...] = normed
    gate_up = dot(normed, wu_ref[...])
    gate_up_ref[...] = gate_up
    gate = gate_up[:, :FF]
    phi = 0.5 * (1.0 + lax.erf(gate * 0.5**0.5))
    product = (gate * phi * gate_up[:, FF:]).astype(BF16)
    product_ref[...] = product
    out_ref[...] = (hidden + dot(product, wd_ref[...])).astype(BF16)


def mlp_back_kernel(
    g_ref, ot_ref, hidden_ref, gate_up_ref, normed_ref, product_ref, gain_ref, wo_ref, wu_ref, wd_ref,
    dot_ref, grad_hidden_ref, d_out_ref, d_up_ref, d_down_ref, d_gain_ref,
):
    grad = g_ref[...]
    grad_product = dot_nt(grad, wd_ref[...])
    d_down_ref[...] = dot(product_ref[...].astype(F32).T.astype(BF16), grad).astype(BF16)
    gate = gate_up_ref[:, :FF]
    up = gate_up_ref[:, FF:]
    phi = 0.5 * (1.0 + lax.erf(gate * 0.5**0.5))
    density = jnp.exp(-0.5 * gate * gate) * 0.3989422804014327
    grad_gate = (grad_product * up * (phi + gate * density)).astype(BF16)
    grad_up = (grad_product * gate * phi).astype(BF16)
    normed_t = normed_ref[...].astype(F32).T.astype(BF16)
    d_up_ref[:, :FF] = dot(normed_t, grad_gate).astype(BF16)
    d_up_ref[:, FF:] = dot(normed_t, grad_up).astype(BF16)
    grad_normed = dot_nt(grad_gate, wu_ref[:, :FF]) + dot_nt(grad_up, wu_ref[:, FF:])
    normalized, rstd = norm_parts(hidden_ref[...])
    part, d_gain = norm_back(grad_normed, normalized, rstd, gain_ref[...].astype(F32))
    d_gain_ref[...] = d_gain
    grad_hidden = grad.astype(F32) + part
    grad_hidden_ref[...] = grad_hidden
    branch = grad_hidden.astype(BF16)
    d_out_ref[...] = dot(ot_ref[...], branch).astype(BF16)
    dot_ref[...] = dot_nt(branch, wo_ref[...]).T.astype(BF16)


def qkv_back_kernel(
    dq_ref, dkv_ref, x_ref, gain_ref, normed_ref, w_ref, cos_ref, sin_ref, grad_hidden_ref,
    grad_x_ref, d_qkv_ref, d_gain_ref, gp_ref,
):
    cos = cos_ref[...]
    sin = sin_ref[...]

    def back(one, two):
        return one * cos + two * sin, two * cos - one * sin

    for head in range(HEADS):
        group, inner = head // GH, head % GH
        at = inner * HEAD_DIM
        one = dq_ref[group, at : at + 32, :].astype(F32)
        two = dq_ref[group, at + 32 : at + 64, :].astype(F32)
        gq = back(one, two)
        rows = slice(inner * ROWS, (inner + 1) * ROWS)
        kv = (dkv_ref[2 * group, rows, :].astype(F32) + dkv_ref[2 * group + 1, rows, :].astype(F32)).T
        gk = back(kv[:32], kv[32:64])
        base = head * HEAD_DIM
        gp_ref[base : base + 32, :] = gq[0]
        gp_ref[base + 32 : base + 64, :] = gq[1]
        gp_ref[D + base : D + base + 32, :] = gk[0]
        gp_ref[D + base + 32 : D + base + 64, :] = gk[1]
        gp_ref[2 * D + base : 2 * D + base + 64, :] = kv[64:]
    normed_t = normed_ref[...].astype(F32).T.astype(BF16)
    grad_normed = jnp.zeros((ROWS, D), F32)
    for block in range(9):
        cols = slice(block * 256, (block + 1) * 256)
        gp = gp_ref[cols, :].T.astype(BF16)
        d_qkv_ref[:, cols] = dot(normed_t, gp).astype(BF16)
        grad_normed = grad_normed + dot_nt(gp, w_ref[:, cols])
    normalized, rstd = norm_parts(x_ref[...].astype(F32))
    part, d_gain = norm_back(grad_normed, normalized, rstd, gain_ref[...].astype(F32))
    d_gain_ref[...] = d_gain
    grad_x_ref[...] = (grad_hidden_ref[...] + part).astype(BF16)


def here():
    return lax.axis_index("section"), lax.axis_index("ctx"), lax.axis_index("wshard")


def flip(index, delta):
    for bit in (1, 2, 4, 8):
        if delta & bit:
            index = index + bit - 2 * bit * lax.rem(index // bit, 2)
    return index


def greet(peers):
    barrier = pltpu.get_barrier_semaphore()
    for peer in peers:
        pl.semaphore_signal(barrier, inc=1, device_id=peer, device_id_type=MESH)
    pl.semaphore_wait(barrier, len(peers))


def remote(src, dst, send, recv, peer):
    return pltpu.make_async_remote_copy(
        src_ref=src, dst_ref=dst, send_sem=send, recv_sem=recv, device_id=peer, device_id_type=MESH
    )


def exchange_call(kernel, args, outs, scratch, collective_id, name):
    return pl.pallas_call(
        kernel,
        out_shape=outs,
        in_specs=[ANY] * len(args),
        out_specs=jax.tree.map(lambda _: ANY, outs),
        scratch_shapes=list(scratch),
        compiler_params=pltpu.CompilerParams(
            collective_id=collective_id, has_side_effects=True, vmem_limit_bytes=VMEM_LIMIT
        ),
        name=name,
    )(*args)


def spread_kernel(qkv_ref, q_ref, kv_ref, kv_send, kv_recv, q_send, q_recv, sib_send, sib_recv, own):
    s, c, z = here()
    sibling = (s, flip(c, 1), z)
    peers = {delta: (s, flip(c, delta), z) for delta in range(2, CTX, 2)}
    greet([sibling, *peers.values()])
    kv_rows = pl.ds(GW, 2 * GW)
    q_rows = pl.ds(0, GW)
    order = [14, 10, 12, 8, 6, 4, 2]
    sends = []
    for delta in order:
        peer = peers[delta]
        copy = remote(
            qkv_ref.at[peer[1] // 4, kv_rows], kv_ref.at[c], kv_send.at[delta], kv_recv.at[delta], peer
        )
        copy.start()
        sends.append(copy)
        if delta % 4 == 0:
            copy = remote(
                qkv_ref.at[peer[1] // 4, q_rows], q_ref.at[c // 4], q_send.at[delta], q_recv.at[delta], peer
            )
            copy.start()
            sends.append(copy)
    own_kv = pltpu.make_async_copy(qkv_ref.at[c // 4, kv_rows], kv_ref.at[c], own.at[0])
    own_q = pltpu.make_async_copy(qkv_ref.at[c // 4, q_rows], q_ref.at[c // 4], own.at[1])
    own_kv.start()
    own_q.start()
    mine = remote(qkv_ref.at[c // 4, kv_rows], kv_ref.at[c], sib_send.at[0], sib_recv.at[0], sibling)
    mine.start()
    passed = [mine]
    for delta in reversed(order):
        source = flip(c, delta)
        remote(kv_ref.at[source], kv_ref.at[source], kv_send.at[delta], kv_recv.at[delta], sibling).wait_recv()
        copy = remote(kv_ref.at[source], kv_ref.at[source], sib_send.at[delta], sib_recv.at[delta], sibling)
        copy.start()
        passed.append(copy)
    own_kv.wait()
    own_q.wait()
    for delta in (4, 8, 12):
        slot = q_ref.at[flip(c, delta) // 4]
        remote(slot, slot, q_send.at[delta], q_recv.at[delta], sibling).wait_recv()
    for copy in sends:
        copy.wait_send()
    for copy in passed:
        copy.wait()


def spread(qkv, collective_id):
    return exchange_call(
        spread_kernel,
        (qkv,),
        (sds((4, GW, ROWS), BF16), sds((CTX, 2 * GW, ROWS), BF16)),
        [DMA((16,))] * 6 + [DMA((2,))],
        collective_id,
        "spread",
    )


def turn_kernel(x_ref, o_ref, send, recv, own):
    s, c, z = here()
    peers = [(s, flip(c, delta), z) for delta in (4, 8, 12)]
    greet(peers)
    copies = []
    for i, peer in enumerate(peers):
        copy = remote(x_ref.at[peer[1] // 4], o_ref.at[c // 4], send.at[i], recv.at[i], peer)
        copy.start()
        copies.append(copy)
    kept = pltpu.make_async_copy(x_ref.at[c // 4], o_ref.at[c // 4], own)
    kept.start()
    kept.wait()
    for copy in copies:
        copy.wait()


def turn(x, collective_id):
    return exchange_call(
        turn_kernel, (x,), sds((4, GW, ROWS), BF16), [DMA((3,)), DMA((3,)), DMA], collective_id, "turn"
    )


def return_kernel(
    dq_ref, dkv_ref, dqo_ref, sums_ref, mine, theirs, total, got,
    q_send, q_recv, sib_send, sib_recv, load, kv_send, kv_recv, own,
):
    s, c, z = here()
    core = lax.rem(c, 2)
    sibling = (s, flip(c, 1), z)
    peers = {delta: (s, flip(c, delta), z) for delta in range(2, CTX, 2)}
    greet([sibling, *peers.values()])
    passed = []
    for i in range(8):
        copy = remote(dkv_ref.at[2 * i + 1 - core], theirs.at[i], sib_send.at[i], sib_recv.at[i], sibling)
        copy.start()
        passed.append(copy)
    loads = []
    for i in range(8):
        copy = pltpu.make_async_copy(dkv_ref.at[2 * i + core], mine.at[i], load.at[i])
        copy.start()
        loads.append(copy)
    sends = []
    for delta in (4, 8, 12):
        peer = peers[delta]
        copy = remote(dq_ref.at[peer[1] // 4], dqo_ref.at[c // 4], q_send.at[delta], q_recv.at[delta], peer)
        copy.start()
        sends.append(copy)
    own_q = pltpu.make_async_copy(dq_ref.at[c // 4], dqo_ref.at[c // 4], own.at[0])
    own_q.start()
    for i in range(8):
        loads[i].wait()
        passed[i].wait()
        total[i] = (mine[i].astype(F32) + theirs[i].astype(F32)).astype(BF16)
    for delta in (14, 10, 12, 8, 6, 4, 2):
        peer = peers[delta]
        copy = remote(total.at[peer[1] // 2], sums_ref.at[c // 2], kv_send.at[delta], kv_recv.at[delta], peer)
        copy.start()
        sends.append(copy)
    own_kv = pltpu.make_async_copy(total.at[c // 2], sums_ref.at[c // 2], own.at[1])
    own_kv.start()
    own_kv.wait()
    own_q.wait()
    for copy in sends:
        copy.wait()


def give_back(dq, dkv, collective_id):
    block = pltpu.VMEM((8, 2 * GW, ROWS), BF16)
    return exchange_call(
        return_kernel,
        (dq, dkv),
        (sds((4, GW, ROWS), BF16), sds((8, 2 * GW, ROWS), BF16)),
        [block, block, block, pltpu.VMEM((8, ROWS), F32)]
        + [DMA((16,)), DMA((16,)), DMA((8,)), DMA((8,)), DMA((8,)), DMA((16,)), DMA((16,)), DMA((2,))],
        collective_id,
        "give_back",
    )


def rope_tables():
    positions = (lax.axis_index("ctx") * ROWS + lax.iota(jnp.int32, ROWS)).astype(F32)
    frequency = 1.0 / 160000.0 ** (jnp.arange(HEAD_DIM // 2, dtype=F32) * 2.0 / HEAD_DIM)
    angles = frequency[:, None] * positions[None, :]
    return jnp.cos(angles), jnp.sin(angles)


def forward_layer(x, weights, tables):
    gain_one, w_qkv, w_out, gain_two, w_up, w_down = weights
    qkv, normed = compute_call(
        qkv_kernel,
        (x, gain_one, w_qkv, *tables),
        (sds((4, 3 * GW, ROWS), BF16), sds((ROWS, D), BF16)),
        name="norm_qkv",
    )
    q, kv = spread(qkv, 1)
    low, wide, totals = compute_call(
        attend_kernel,
        (q, kv),
        (sds((4, GW, ROWS), BF16), sds((4, GW, ROWS), F32), sds((GH, 8, 512), F32)),
        [pltpu.VMEM((2048, 512), F32)],
        name="attend",
    )
    ot = turn(low, 2).reshape(D, ROWS)
    out, hidden, gate_up, normed_two, product = compute_call(
        mlp_kernel,
        (ot, x, gain_two, w_out, w_up, w_down),
        (sds((ROWS, D), BF16), sds((ROWS, D), F32), sds((ROWS, 2 * FF), F32),
         sds((ROWS, D), BF16), sds((ROWS, FF), BF16)),
        name="mlp",
    )
    return out, (x, normed, q, kv, wide, totals, ot, hidden, gate_up, normed_two, product)


def backward_layer(grad, stored, weights, tables):
    gain_one, w_qkv, w_out, gain_two, w_up, w_down = weights
    x, normed, q, kv, wide, totals, ot, hidden, gate_up, normed_two, product = stored
    d_ot, grad_hidden, d_out, d_up, d_down, d_gain_two = compute_call(
        mlp_back_kernel,
        (grad, ot, hidden, gate_up, normed_two, product, gain_two, w_out, w_up, w_down),
        (sds((D, ROWS), BF16), sds((ROWS, D), F32), sds((D, D), BF16),
         sds((D, 2 * FF), BF16), sds((FF, D), BF16), sds((1, D), F32)),
        name="mlp_back",
    )
    d_o = turn(d_ot.reshape(4, GW, ROWS), 2)
    dq, dkv = compute_call(
        attend_back_kernel,
        (q, kv, wide, totals, d_o),
        (sds((4, GW, ROWS), BF16), sds((CTX, 2 * GW, ROWS), BF16)),
        name="attend_back",
    )
    dq, dkv = give_back(dq, dkv, 3)
    grad_x, d_qkv, d_gain_one = compute_call(
        qkv_back_kernel,
        (dq, dkv, x, gain_one, normed, w_qkv, *tables, grad_hidden),
        (sds((ROWS, D), BF16), sds((D, 3 * D), BF16), sds((1, D), F32)),
        [pltpu.VMEM((3 * D, ROWS), F32)],
        name="qkv_back",
    )
    return grad_x, (d_gain_one, d_qkv, d_out, d_gain_two, d_up, d_down)


def gather_weights(arrays):
    gathered = []
    for a in arrays:
        whole = lax.all_gather(a[0], ("section", "wshard"), axis=0, tiled=True)
        gathered.append(whole.reshape(2, -1, whole.shape[-1]))
    return gathered


def reduce_grads(first, second):
    shards = []
    for a, b in zip(first, second):
        both = jnp.concatenate([a, b], axis=0).astype(BF16)
        part = lax.psum_scatter(both, ("section", "wshard"), scatter_dimension=0, tiled=True)
        shards.append(lax.psum(part, "ctx").astype(F32))
    return shards


def swap_layers(zero, one):
    first = lax.axis_index("section") == 0
    other = lax.ppermute(jnp.where(first, one, zero), "section", [(0, 1), (1, 0)])
    kept = jnp.where(first, zero, one)
    return jnp.stack([jnp.where(first, kept, other), jnp.where(first, other, kept)])[None, :, None]


def local(inputs, cotangent, attn_gain, qkv_weight, out_weight, mlp_gain, up_weight, down_weight):
    section = lax.axis_index("section")
    first = section == 0
    x = jnp.where(first, inputs[0, 0], inputs[1, 0])
    cot = jnp.where(first, cotangent[0, 0], cotangent[1, 0])
    w_qkv, w_out, w_up, w_down = gather_weights([qkv_weight, out_weight, up_weight, down_weight])
    gains = [
        lax.all_gather(g[0], ("section", "wshard"), axis=0, tiled=True).reshape(2, 1, D)
        for g in (attn_gain, mlp_gain)
    ]
    stacked = (gains[0], w_qkv, w_out, gains[1], w_up, w_down)
    weights = [tuple(w[layer] for w in stacked) for layer in range(2)]
    tables = rope_tables()
    mid, stored_zero = forward_layer(x, weights[0], tables)
    end, stored_one = forward_layer(mid, weights[1], tables)
    grad_mid, grads_one = backward_layer(cot, stored_one, weights[1], tables)
    grad_start, grads_zero = backward_layer(grad_mid, stored_zero, weights[0], tables)
    activations = swap_layers(mid, end)
    input_grads = swap_layers(grad_start, grad_mid)
    flat = lambda grads: [grads[0].reshape(D, 1), grads[1], grads[2], grads[3].reshape(D, 1), grads[4], grads[5]]
    reduced = reduce_grads(flat(grads_zero), flat(grads_one))
    return (
        activations,
        input_grads,
        reduced[0].reshape(1, -1),
        reduced[1][None],
        reduced[2][None],
        reduced[3].reshape(1, -1),
        reduced[4][None],
        reduced[5][None],
    )


def solution(mesh):
    placed = (
        P(None, "wshard", "ctx", None),
        P(None, "wshard", "ctx", None),
        P("section", "wshard"),
        P("section", "wshard", None),
        P("section", "wshard", None),
        P("section", "wshard"),
        P("section", "wshard", None),
        P("section", "wshard", None),
    )
    return jax.shard_map(
        local,
        mesh=mesh,
        in_specs=placed,
        out_specs=(
            P("section", None, "wshard", "ctx", None),
            P("section", None, "wshard", "ctx", None),
            P("section", "wshard"),
            P("section", "wshard", None),
            P("section", "wshard", None),
            P("section", "wshard"),
            P("section", "wshard", None),
            P("section", "wshard", None),
        ),
        check_vma=False,
    )
```

time: 1270 us -> 906 us (0.71); the launches traced: 1250 us -> 905 us
  waiting for transfers between devices: 866 us -> 547 us
  Pallas kernels: 0 us -> 227 us
  matrix products: 169 us -> 0 us
  local copies, waits for them, and re-layouts: 86.7 us -> 29.3 us
  other arithmetic: 57 us -> 31.3 us
    pallas_call x0 -> x20, Pallas kernels: none -> 227 us  [the longest x8 128 us: exchange_call(): pl.pallas_call(kernel, out_shape=outs, in_specs=[ANY] * len(args), out_sp...]
    all_gather x10 -> x4, waiting for transfers between devices: 390 us -> 170 us  [gather_weights(): whole = lax.all_gather(a[0], ('section', 'wshard'), axis=0, tiled=True)]
    dot_general x54 -> x0, matrix products: 169 us -> none  [the longest x3 26.5 us: forward_layer(): jnp.einsum('hqk,khd->qhd', probs, split_heads(values_all), preferred_elem...]
    unnamed x21 -> x13, waiting for transfers between devices: 225 us -> 73.6 us
    reduce_scatter x4, waiting for transfers between devices: 135 us -> 189 us  [reduce_grads(): lax.psum_scatter(both, ('section', 'wshard'), scatter_dimension=0, tiled=...]
    unnamed x380 -> x41, local copies, waits for them, and re-layouts: 56.1 us -> 7.98 us
    ppermute x4 -> x2, waiting for transfers between devices: 17.8 us -> 0.01 us  [swap_layers(): lax.ppermute(jnp.where(first, one, zero), 'section', [(0, 1), (1, 0)])]
    psum x1, waiting for transfers between devices: 97.5 us -> 114 us  [reduce_grads(): shards.append(lax.psum(part, 'ctx').astype(F32))]
  transfers between devices with their start and end apart: 22 -> 13, of which waited for: 22 -> 10; matrix products, arithmetic and copies ran while one was open for 9% -> 5% of each run, Pallas kernels for 0% -> 12%
where the time goes in v1:
time: 906 us; the launch traced here: 905 us
  waiting for transfers between devices  547 us (60%)
  Pallas kernels  227 us (25%)
  blocking collectives  53.5 us (6%)
  other arithmetic  31.3 us (3%)
  local copies, waits for them, and re-layouts  29.3 us (3%)
  between operations  14.8 us (2%)
    reduce_scatter x4, waiting for transfers between devices, reduce_grads(): lax.psum_scatter(both, ('section', 'wshard'), scatter_dimension=0, tiled=...  189 us
    all_gather x4, waiting for transfers between devices, gather_weights(): whole = lax.all_gather(a[0], ('section', 'wshard'), axis=0, tiled=True)  170 us
    pallas_call x8, Pallas kernels, exchange_call(): pl.pallas_call(kernel, out_shape=outs, in_specs=[ANY] * len(args), out_sp...  128 us
    psum x1, waiting for transfers between devices, reduce_grads(): shards.append(lax.psum(part, 'ctx').astype(F32))  114 us
    pallas_call x12, Pallas kernels, compute_call(): pl.pallas_call(kernel, out_shape=outs, in_specs=[VM] * len(args), out_spe...  98.7 us
    unnamed x13, waiting for transfers between devices  73.6 us
    psum x1, blocking collectives, reduce_grads(): shards.append(lax.psum(part, 'ctx').astype(F32))  35.3 us
    slice x6, local copies, waits for them, and re-layouts, local(): weights = [tuple((w[layer] for w in stacked)) for layer in range(2)]  21.3 us
  transfers between devices with their start and end apart: 13, of which 10 were waited for; matrix products, arithmetic and copies ran while one was open for 5% of the time, Pallas kernels for 12%

profile of v1, /device:TPU:25, one launch (start us, length us, event | category | flops | bytes accessed | tf_op | source)
XLA Modules:
  0.0 904.9 jit_solution(15921443704938013309)
XLA Ops:
  13.8 18.2 %all-reduce.4 = (bf16[1536]{0:T(1024)(128)(2,1)S(1)}, bf16[1536]{0:T(1024)(128)(2,1)S(1)}) all-reduce(bf16[1536]{0:T(1024)(128)(2,1)S(1)} %dynamic-update-slice, bf16[1536]{0:T(1024)(128)(2,1)S(1)} %dynamic-update-slice.1), channel_id=2, replica_groups=mesh['section'=2,'ctx'=16,'wshard'=4] {'section','wshard'}, use_global_device_ids=true, to_apply=%add | all-reduce | flops 3072 | bytes 12288
  37.5 12.8 %all-gather.13.cloned.1.call-done = bf16[1,1536,768]{2,1,0:T(8,128)(2,1)} async-done(((bf16[1,192,768]{2,1,0:T(8,128)(2,1)}), bf16[1,1536,768]{2,1,0:T(8,128)(2,1)}) %all-gather.13.cloned.1.call-update) | async-done | bytes 2359312 | tf_op jit(solution)/shard_map/all_gather | solution.py:490
  53.5 48.4 %all-gather.17.cloned.1.call-done = bf16[1,2304,768]{2,1,0:T(8,128)(2,1)} async-done(((bf16[1,288,768]{2,1,0:T(8,128)(2,1)}), bf16[1,2304,768]{2,1,0:T(8,128)(2,1)}) %all-gather.17.cloned.1.call-update) | async-done | bytes 3538960 | tf_op jit(solution)/shard_map/all_gather | solution.py:490
  106.0 76.8 %all-gather.11.cloned.1.call-done = bf16[1,1536,2304]{2,1,0:T(8,128)(2,1)} async-done(((bf16[1,192,2304]{2,1,0:T(8,128)(2,1)}), bf16[1,1536,2304]{2,1,0:T(8,128)(2,1)}) %all-gather.11.cloned.1.call-update) | async-done | bytes 7077904 | tf_op jit(solution)/shard_map/all_gather | solution.py:490
  182.7 6.4 slice_bitcast_fusion.1
  193.0 31.3 %spread.2 = (bf16[4,192,128]{2,1,0:T(8,128)(2,1)}, bf16[16,384,128]{2,1,0:T(8,128)(2,1)}) custom-call(bf16[4,576,128]{2,1,0:T(8,128)(2,1)} %get-tuple-element.58.qkv_ref), custom_call_target="tpu_custom_call" | custom-call | tf_op jit(solution)/shard_map/spread/pallas_call | solution.py:276
  224.3 7.9 attend.2
  232.2 10.9 %turn.4 = bf16[4,192,128]{2,1,0:T(8,128)(2,1)} custom-call(bf16[4,192,128]{2,1,0:T(8,128)(2,1)} %get-tuple-element.61.x_ref), custom_call_target="tpu_custom_call" | custom-call | tf_op jit(solution)/shard_map/turn/pallas_call | solution.py:276
  243.1 32.3 %all-gather.15.cloned.1.call-done = bf16[1,1536,2304]{2,1,0:T(8,128)(2,1)} async-done(((bf16[1,192,2304]{2,1,0:T(8,128)(2,1)}), bf16[1,1536,2304]{2,1,0:T(8,128)(2,1)}) %all-gather.15.cloned.1.call-update) | async-done | bytes 7077904 | tf_op jit(solution)/shard_map/all_gather | solution.py:490
  275.4 6.5 slice_bitcast_fusion
  291.1 20.1 %spread.3 = (bf16[4,192,128]{2,1,0:T(8,128)(2,1)}, bf16[16,384,128]{2,1,0:T(8,128)(2,1)}) custom-call(bf16[4,576,128]{2,1,0:T(8,128)(2,1)} %get-tuple-element.63.qkv_ref), custom_call_target="tpu_custom_call" | custom-call | tf_op jit(solution)/shard_map/spread/pallas_call | solution.py:276
  311.3 7.9 attend.3
  319.1 8.2 turn.5
  332.8 9.1 %mlp_back.2 = (bf16[768,128]{1,0:T(8,128)(2,1)}, f32[128,768]{1,0:T(8,128)}, bf16[768,768]{1,0:T(8,128)(2,1)}, bf16[768,2304]{1,0:T(8,128)(2,1)}, bf16[1152,768]{1,0:T(8,128)(2,1)}, /*index=5*/f32[1,768]{1,0:T(1,128)}) custom-call(bf16[128,768]{1,0:T(8,128)(2,1)} %select_bitcast_fusion.2.g_ref, bf16[768,128]{1,0:T(8,128)(2,1)} %bitcast.60, ...), custom_call_target="tpu_custom_call" | custom-call | tf_op jit(solution)/shard_map/mlp_back/pallas_call | solution.py:42
  341.9 7.9 turn.6.do_ref
  349.7 16.9 %attend_back.2 = (bf16[4,192,128]{2,1,0:T(8,128)(2,1)}, bf16[16,384,128]{2,1,0:T(8,128)(2,1)}) custom-call(bf16[4,192,128]{2,1,0:T(8,128)(2,1)} %get-tuple-element.64.q_ref, bf16[16,384,128]{2,1,0:T(8,128)(2,1)} %get-tuple-element.65.kv_ref, f32[4,192,128]{2,1,0:T(8,128)} %get-tuple-element.70.wide_ref, f32[3,8,512]{2,1,0:T(8,128)} %get-tuple-element.71.totals_ref, ...), custom_call_target="tpu_custom_call" | custom-call | tf_op jit(solution)/shard_map/attend_back/pallas_call | solution.py:42
  366.6 19.4 %give_back.2 = (bf16[4,192,128]{2,1,0:T(8,128)(2,1)}, bf16[8,384,128]{2,1,0:T(8,128)(2,1)}) custom-call(bf16[4,192,128]{2,1,0:T(8,128)(2,1)} %get-tuple-element.77.dq_ref, bf16[16,384,128]{2,1,0:T(8,128)(2,1)} %get-tuple-element.78.dkv_ref), custom_call_target="tpu_custom_call" | custom-call | tf_op jit(solution)/shard_map/give_back/pallas_call | solution.py:276
  386.0 6.3 qkv_back.2
  392.4 9.1 %mlp_back.3 = (bf16[768,128]{1,0:T(8,128)(2,1)}, f32[128,768]{1,0:T(8,128)}, bf16[768,768]{1,0:T(8,128)(2,1)}, bf16[768,2304]{1,0:T(8,128)(2,1)}, bf16[1152,768]{1,0:T(8,128)(2,1)}, /*index=5*/f32[1,768]{1,0:T(1,128)}) custom-call(bf16[128,768]{1,0:T(8,128)(2,1)} %get-tuple-element.83.g_ref, bf16[768,128]{1,0:T(8,128)(2,1)} %bitcast.58, ...), custom_call_target="tpu_custom_call" | custom-call | tf_op jit(solution)/shard_map/mlp_back/pallas_call | solution.py:42
  406.8 8.0 turn.7.do_ref
  414.7 16.7 %attend_back.3 = (bf16[4,192,128]{2,1,0:T(8,128)(2,1)}, bf16[16,384,128]{2,1,0:T(8,128)(2,1)}) custom-call(bf16[4,192,128]{2,1,0:T(8,128)(2,1)} %get-tuple-element.59.q_ref, bf16[16,384,128]{2,1,0:T(8,128)(2,1)} %get-tuple-element.60.kv_ref, f32[4,192,128]{2,1,0:T(8,128)} %get-tuple-element.68.wide_ref, f32[3,8,512]{2,1,0:T(8,128)} %get-tuple-element.69.totals_ref, ...), custom_call_target="tpu_custom_call" | custom-call | tf_op jit(solution)/shard_map/attend_back/pallas_call | solution.py:42
  431.5 22.6 %give_back.3 = (bf16[4,192,128]{2,1,0:T(8,128)(2,1)}, bf16[8,384,128]{2,1,0:T(8,128)(2,1)}) custom-call(bf16[4,192,128]{2,1,0:T(8,128)(2,1)} %get-tuple-element.89.dq_ref, bf16[16,384,128]{2,1,0:T(8,128)(2,1)} %get-tuple-element.90.dkv_ref), custom_call_target="tpu_custom_call" | custom-call | tf_op jit(solution)/shard_map/give_back/pallas_call | solution.py:276
  454.0 6.3 qkv_back.3
  460.4 5.6 pad_maximum_fusion
  468.0 5.4 pad_maximum_fusion.1
  476.3 21.6 %reduce-scatter.17.cloned.1.call-done = bf16[288,768]{1,0:T(8,128)(2,1)} async-done(((bf16[2304,768]{1,0:T(8,128)(2,1)}), bf16[288,768]{1,0:T(8,128)(2,1)}) %reduce-scatter.17.cloned.1.call-update) | async-done | bytes 442384 | tf_op jit(solution)/shard_map/reduce_scatter | solution.py:499
  498.0 85.1 %reduce-scatter.11.cloned.1.call-done = bf16[192,2304]{1,0:T(8,128)(2,1)} async-done(((bf16[1536,2304]{1,0:T(8,128)(2,1)}), bf16[192,2304]{1,0:T(8,128)(2,1)}) %reduce-scatter.11.cloned.1.call-update) | async-done | bytes 884752 | tf_op jit(solution)/shard_map/reduce_scatter | solution.py:499
  583.1 81.8 %reduce-scatter.15.cloned.1.call-done = bf16[192,2304]{1,0:T(8,128)(2,1)} async-done(((bf16[1536,2304]{1,0:T(8,128)(2,1)}), bf16[192,2304]{1,0:T(8,128)(2,1)}) %reduce-scatter.15.cloned.1.call-update) | async-done | bytes 884752 | tf_op jit(solution)/shard_map/reduce_scatter | solution.py:499
  666.6 32.6 %reduce-scatter.21.cloned.1.call-done = bf16[192,1]{1,0:T(8,128)(2,1)} async-done(((bf16[1536,1]{1,0:T(8,128)(2,1)}), bf16[192,1]{1,0:T(8,128)(2,1)}) %reduce-scatter.21.cloned.1.call-update) | async-done | bytes 400
  700.1 38.3 %reduce-scatter.19.cloned.1.call-done = bf16[192,1]{1,0:T(8,128)(2,1)} async-done(((bf16[1536,1]{1,0:T(8,128)(2,1)}), bf16[192,1]{1,0:T(8,128)(2,1)}) %reduce-scatter.19.cloned.1.call-update) | async-done | bytes 400
  739.3 35.3 %all-reduce.2 = (bf16[1,192]{1,0:T(2,128)(2,1)S(1)}, bf16[1,192]{1,0:T(2,128)(2,1)S(1)}) all-reduce(bf16[1,192]{1,0:T(2,128)(2,1)S(1)} %bitcast.68, bf16[1,192]{1,0:T(2,128)(2,1)S(1)} %bitcast.67), channel_id=1, replica_groups=mesh['section'=2,'ctx'=16,'wshard'=4] {'ctx'}, use_global_device_ids=true, to_apply=%region_1.2 | all-reduce | flops 384 | bytes 1536 | tf_op jit(solution)/shard_map/psum | solution.py:500
  777.3 114.3 %all-reduce.7.cloned.1.call-done = (bf16[1,192,2304]{2,1,0:T(8,128)(2,1)}, bf16[1,192,768]{2,1,0:T(8,128)(2,1)}, bf16[1,192,2304]{2,1,0:T(8,128)(2,1)}, bf16[1,288,768]{2,1,0:T(8,128)(2,1)}) async-done(((bf16[1,192,2304]{2,1,0:T(8,128)(2,1)}, bf16[1,192,768]{2,1,0:T(8,128)(2,1)}, bf16[1,192,2304]{2,1,0:T(8,128)(2,1)}, bf16[1,288,768]{2,1,0:T(8,128)(2,1)}), (bf16[1,192,2304]{2,1,0:T(8,128)(2,1)}, ...) | async-done | bytes 2506768 | tf_op jit(solution)/shard_map/psum | solution.py:500
  (101 shorter events, 60.0 us)
Async XLA Ops:
  7.2 43.1 %all-gather.13.cloned.1.call-start = ((), (), s32[]{:S(2)}) async-start(), calls=%async_computation.11 | async-start | bytes 2654208 | tf_op jit(solution)/shard_map/all_gather | solution.py:490
  7.9 94.0 %all-gather.17.cloned.1.call-start = ((), (), s32[]{:S(2)}) async-start(), calls=%async_computation.13 | async-start | bytes 3981312 | tf_op jit(solution)/shard_map/all_gather | solution.py:490
  8.7 174.1 %all-gather.11.cloned.1.call-start = ((), (), s32[]{:S(2)}) async-start(), calls=%async_computation.10 | async-start | bytes 7962624 | tf_op jit(solution)/shard_map/all_gather | solution.py:490
  9.4 266.0 %all-gather.15.cloned.1.call-start = ((), (), s32[]{:S(2)}) async-start(), calls=%async_computation.12 | async-start | bytes 7962624 | tf_op jit(solution)/shard_map/all_gather | solution.py:490
  10.0 466.4 %reduce-scatter.13.cloned.1.call-start = ((), (), s32[]{:S(2)}) async-start(), calls=%async_computation.7 | async-start | bytes 2654208 | tf_op jit(solution)/shard_map/reduce_scatter | solution.py:499
  392.4 9.1 %copy-start.6 = (bf16[768,768]{1,0:T(8,128)(2,1)S(1)}, bf16[768,768]{1,0:T(8,128)(2,1)}, u32[]{:S(2)}) copy-start(bf16[768,768]{1,0:T(8,128)(2,1)} %get-tuple-element.101) | copy-start | bytes 3538948
  401.5 3.2 copy-start.3
  401.5 3.2 copy-start.4
  404.6 93.4 %reduce-scatter.17.cloned.1.call-start = ((), (), s32[]{:S(2)}) async-start(), calls=%async_computation.9 | async-start | bytes 3981312 | tf_op jit(solution)/shard_map/reduce_scatter | solution.py:499
  406.7 176.4 %reduce-scatter.11.cloned.1.call-start = ((), (), s32[]{:S(2)}) async-start(), calls=%async_computation.6 | async-start | bytes 7962624 | tf_op jit(solution)/shard_map/reduce_scatter | solution.py:499
  431.5 28.9 %copy-start.2 = (bf16[768,2304]{1,0:T(8,128)(2,1)S(1)}, bf16[768,2304]{1,0:T(8,128)(2,1)}, u32[]{:S(2)}) copy-start(bf16[768,2304]{1,0:T(8,128)(2,1)} %get-tuple-element.99) | copy-start | bytes 10616836
  466.0 2.0 copy-start.1
  466.0 198.8 %reduce-scatter.15.cloned.1.call-start = ((), (), s32[]{:S(2)}) async-start(), calls=%async_computation.8 | async-start | bytes 7962624 | tf_op jit(solution)/shard_map/reduce_scatter | solution.py:499
  473.5 0.7 copy-start.11
  473.5 0.7 copy-start.13
  473.5 1.7 copy-start.12
  473.5 1.7 copy-start.14
  473.5 191.4 %copy-start = (bf16[128,768]{1,0:T(8,128)(2,1)S(1)}, bf16[128,768]{1,0:T(8,128)(2,1)}, u32[]{:S(2)}) copy-start(bf16[128,768]{1,0:T(8,128)(2,1)} %get-tuple-element.62.x_ref) | copy-start | bytes 589828
  473.5 191.4 %copy-start.8 = (bf16[128,768]{1,0:T(8,128)(2,1)S(1)}, bf16[128,768]{1,0:T(8,128)(2,1)}, u32[]{:S(2)}) copy-start(bf16[128,768]{1,0:T(8,128)(2,1)} %get-tuple-element.67) | copy-start | bytes 589828
  473.5 191.8 %copy-start.5 = (bf16[128,768]{1,0:T(8,128)(2,1)S(1)}, bf16[128,768]{1,0:T(8,128)(2,1)}, u32[]{:S(2)}) copy-start(bf16[128,768]{1,0:T(8,128)(2,1)} %get-tuple-element.83.g_ref) | copy-start | bytes 589828
  473.5 191.8 %copy-start.9 = (bf16[128,768]{1,0:T(8,128)(2,1)S(1)}, bf16[128,768]{1,0:T(8,128)(2,1)}, u32[]{:S(2)}) copy-start(bf16[128,768]{1,0:T(8,128)(2,1)} %get-tuple-element.95) | copy-start | bytes 589828
  473.5 225.6 %reduce-scatter.21.cloned.1.call-start = ((), (), s32[]{:S(2)}) async-start(), calls=%async_computation.15 | async-start | bytes 442368
  475.2 263.2 %reduce-scatter.19.cloned.1.call-start = ((), (), s32[]{:S(2)}) async-start(), calls=%async_computation.14 | async-start | bytes 442368
  476.2 415.4 %all-reduce.7.cloned.1.call-start = ((), (), s32[]{:S(2)}) async-start(), calls=%async_computation.16 | async-start | bytes 5013504 | tf_op jit(solution)/shard_map/psum | solution.py:500
  664.9 110.8 %collective-permute-start = (bf16[128,768]{1,0:T(8,128)(2,1)S(1)}, bf16[128,768]{1,0:T(8,128)(2,1)S(1)}, u32[]{:S(2)}, u32[]{:S(2)}) collective-permute-start(bf16[128,768]{1,0:T(8,128)(2,1)S(1)} %broadcast_select_fusion.2), channel_id=1, source_target_pairs={{0,64},{64,0},{1,65},{65,1},{2,66},{66,2},{3,67},{67,3},{4,68},{68... | collective-permute-start | bytes 589832 | tf_op jit(solution)/shard_map/ppermute | solution.py:506
  665.3 111.2 %collective-permute-start.1 = (bf16[128,768]{1,0:T(8,128)(2,1)S(1)}, bf16[128,768]{1,0:T(8,128)(2,1)S(1)}, u32[]{:S(2)}, u32[]{:S(2)}) collective-permute-start(bf16[128,768]{1,0:T(8,128)(2,1)S(1)} %broadcast_select_fusion), channel_id=1, source_target_pairs={{0,64},{64,0},{1,65},{65,1},{2,66},{66,2},{3,67},{67,3},{4,68},{68... | collective-permute-start | bytes 589832 | tf_op jit(solution)/shard_map/ppermute | solution.py:506
  891.6 4.4 copy-start.10
  891.6 5.4 copy-start.7
Sparse Core Ops, SparseCore 0:
  9.6 40.5 all-gather.12
  51.9 50.0 all-gather.16
  103.6 79.1 all-gather.10
  184.2 91.1 all-gather.14
  404.7 41.3 reduce-scatter.12
  448.4 49.5 reduce-scatter.16
  500.5 82.5 reduce-scatter.10
  585.6 79.1 reduce-scatter.14
  667.9 31.2 reduce-scatter.20
  702.0 36.3 reduce-scatter.18
  741.4 150.2 all-reduce.6

commit v2 on v1

v2 whole, which is shorter than its diff:
```python
import functools

import jax
import jax.numpy as jnp
from jax import lax
from jax.experimental import pallas as pl
from jax.experimental.pallas import tpu as pltpu
from jax.sharding import PartitionSpec as P

D = 768
HEADS = 12
HEAD_DIM = 64
FF = 1152
ROWS = 128
GROUPS = 4
GH = HEADS // GROUPS
GW = GH * HEAD_DIM
CTX = 16
SCALE = HEAD_DIM ** (-0.5)
F32 = jnp.float32
BF16 = jnp.bfloat16
MESH = pl.DeviceIdType.MESH
DMA = pltpu.SemaphoreType.DMA
ANY = pl.BlockSpec(memory_space=pl.ANY)
VM = pl.BlockSpec(memory_space=pltpu.VMEM)
VMEM_LIMIT = 56 * 1024 * 1024


def dot(a, b):
    return jnp.dot(a, b, preferred_element_type=F32)


def dot_nt(a, b):
    return lax.dot_general(a, b, (((1,), (1,)), ((), ())), preferred_element_type=F32)


def sds(shape, dtype):
    return jax.ShapeDtypeStruct(shape, dtype)


def compute_call(kernel, args, outs, scratch=(), name=None):
    return pl.pallas_call(
        kernel,
        out_shape=outs,
        in_specs=[VM] * len(args),
        out_specs=jax.tree.map(lambda _: VM, outs),
        scratch_shapes=list(scratch),
        compiler_params=pltpu.CompilerParams(vmem_limit_bytes=VMEM_LIMIT),
        name=name,
    )(*args)


def turned_low(x):
    return x.astype(F32).T.astype(BF16)


def norm_parts(source):
    centered = source - jnp.mean(source, axis=-1, keepdims=True)
    variance = jnp.mean(centered * centered, axis=-1, keepdims=True)
    rstd = lax.rsqrt(variance + 1e-05)
    return centered * rstd, rstd


def norm_back(grad, normalized, rstd, gain):
    inner = grad * gain
    mean_one = jnp.mean(inner, axis=-1, keepdims=True)
    mean_two = jnp.mean(inner * normalized, axis=-1, keepdims=True)
    grad_gain = jnp.sum(grad * normalized, axis=0, keepdims=True)
    return rstd * (inner - mean_one - normalized * mean_two), grad_gain


def qkv_kernel(x_ref, gain_ref, w_ref, cos_ref, sin_ref, qkv_ref, normed_ref):
    normalized, _ = norm_parts(x_ref[...].astype(F32))
    normed = (normalized * gain_ref[...].astype(F32)).astype(BF16)
    normed_ref[...] = turned_low(normed)
    cos = cos_ref[...]
    sin = sin_ref[...]
    for part in range(3):
        for block in range(3):
            at = part * D + block * 256
            turned = dot(normed, w_ref[:, at : at + 256]).T
            for head_at in range(4):
                head = block * 4 + head_at
                one = turned[head_at * 64 : head_at * 64 + 32]
                two = turned[head_at * 64 + 32 : head_at * 64 + 64]
                if part < 2:
                    one, two = one * cos - two * sin, two * cos + one * sin
                if part == 0:
                    one, two = one * SCALE, two * SCALE
                row = part * GW + (head % GH) * HEAD_DIM
                qkv_ref[head // GH, row : row + 32, :] = one.astype(BF16)
                qkv_ref[head // GH, row + 32 : row + 64, :] = two.astype(BF16)


CHUNK = 256
CHUNKS = 2048 // CHUNK
PAIR = CHUNK // ROWS


def attend_kernel(q_ref, kv_ref, low_ref, wide_ref, totals_ref, s_ref):
    @pl.loop(0, GH)
    def _(h):
        at = pl.multiple_of(h * HEAD_DIM, HEAD_DIM)
        value_at = pl.multiple_of(h * HEAD_DIM + GW, HEAD_DIM)
        qt = jnp.concatenate([q_ref[i, pl.ds(at, HEAD_DIM), :] for i in range(4)], axis=1)
        top = jnp.full((8, 512), -jnp.inf, F32)
        for c in range(CHUNKS):
            keys = jnp.concatenate(
                [kv_ref[c * PAIR + i, pl.ds(at, HEAD_DIM), :].T for i in range(PAIR)], axis=0
            )
            scores = dot(keys, qt)
            s_ref[c * CHUNK : (c + 1) * CHUNK, :] = scores
            top = jnp.maximum(top, jnp.max(scores.reshape(CHUNK // 8, 8, 512), axis=0))
        top = jnp.max(top, axis=0, keepdims=True)
        total = jnp.zeros((8, 512), F32)
        acc = jnp.zeros((HEAD_DIM, 512), F32)
        for c in range(CHUNKS):
            p = jnp.exp(s_ref[c * CHUNK : (c + 1) * CHUNK, :] - top)
            total = total + jnp.sum(p.reshape(CHUNK // 8, 8, 512), axis=0)
            values = jnp.concatenate(
                [kv_ref[c * PAIR + i, pl.ds(value_at, HEAD_DIM), :] for i in range(PAIR)], axis=1
            )
            acc = acc + dot(values, p.astype(BF16))
        total = jnp.sum(total, axis=0, keepdims=True)
        out = acc / total
        totals_ref[h] = jnp.broadcast_to(top + jnp.log(total), (8, 512))
        for i in range(4):
            piece = out[:, i * ROWS : (i + 1) * ROWS]
            wide_ref[i, pl.ds(at, HEAD_DIM), :] = piece
            low_ref[i, pl.ds(at, HEAD_DIM), :] = piece.astype(BF16)


def attend_back_kernel(q_ref, kv_ref, wide_ref, totals_ref, do_ref, dq_ref, dkv_ref):
    @pl.loop(0, GH)
    def _(h):
        at = pl.multiple_of(h * HEAD_DIM, HEAD_DIM)
        value_at = pl.multiple_of(h * HEAD_DIM + GW, HEAD_DIM)
        out_at = pl.multiple_of(h * ROWS, ROWS)
        qt = jnp.concatenate([q_ref[i, pl.ds(at, HEAD_DIM), :] for i in range(4)], axis=1)
        dot_t = jnp.concatenate([do_ref[i, pl.ds(at, HEAD_DIM), :] for i in range(4)], axis=1)
        wide = jnp.concatenate([wide_ref[i, pl.ds(at, HEAD_DIM), :] for i in range(4)], axis=1)
        delta = jnp.sum(wide * dot_t.astype(F32), axis=0, keepdims=True)
        totals = totals_ref[h, 0:1, :]
        zero = jnp.zeros((512, HEAD_DIM), BF16)
        sides = jnp.concatenate(
            [
                jnp.concatenate([qt.T, zero], axis=1),
                jnp.concatenate([zero, dot_t.T], axis=1),
            ],
            axis=0,
        )

        def step(c, acc):
            keys_t = [kv_ref[c * PAIR + i, pl.ds(at, HEAD_DIM), :] for i in range(PAIR)]
            values_t = [kv_ref[c * PAIR + i, pl.ds(value_at, HEAD_DIM), :] for i in range(PAIR)]
            keys = jnp.concatenate([k.T for k in keys_t], axis=0)
            values = jnp.concatenate([v.T for v in values_t], axis=0)
            p = jnp.exp(dot(keys, qt) - totals)
            ds = (p * (dot(values, dot_t) - delta)).astype(BF16)
            both = jnp.concatenate([ds, p.astype(BF16)], axis=1)
            grads = dot(both, sides).astype(BF16)
            for i in range(PAIR):
                dkv_ref[c * PAIR + i, pl.ds(out_at, ROWS), :] = grads[i * ROWS : (i + 1) * ROWS]
            return acc + dot(jnp.concatenate(keys_t, axis=1), ds)

        acc = lax.fori_loop(0, CHUNKS, step, jnp.zeros((HEAD_DIM, 512), F32)) * SCALE
        for i in range(4):
            dq_ref[i, pl.ds(at, HEAD_DIM), :] = acc[:, i * ROWS : (i + 1) * ROWS].astype(BF16)


def mlp_kernel(
    ot_ref, x_ref, gain_ref, wo_ref, wu_ref, wd_ref,
    out_ref, hidden_ref, gate_up_ref, normed_ref, product_ref,
):
    attended = turned_low(ot_ref[...])
    hidden = x_ref[...].astype(F32) + dot(attended, wo_ref[...])
    hidden_ref[...] = hidden
    normalized, _ = norm_parts(hidden)
    normed = (normalized * gain_ref[...].astype(F32)).astype(BF16)
    normed_ref[...] = turned_low(normed)
    gate_up = dot(normed, wu_ref[...])
    gate_up_ref[...] = gate_up
    gate = gate_up[:, :FF]
    phi = 0.5 * (1.0 + lax.erf(gate * 0.5**0.5))
    product = (gate * phi * gate_up[:, FF:]).astype(BF16)
    product_ref[...] = turned_low(product)
    out_ref[...] = (hidden + dot(product, wd_ref[...])).astype(BF16)


def mlp_back_kernel(
    g_ref, hidden_ref, gate_up_ref, gain_ref, wo_ref, wu_ref, wd_ref,
    dot_ref, grad_hidden_ref, gg_ref, branch_ref, d_gain_ref,
):
    grad = g_ref[...]
    grad_product = dot_nt(grad, wd_ref[...])
    gate = gate_up_ref[:, :FF]
    up = gate_up_ref[:, FF:]
    phi = 0.5 * (1.0 + lax.erf(gate * 0.5**0.5))
    density = jnp.exp(-0.5 * gate * gate) * 0.3989422804014327
    grad_gate = (grad_product * up * (phi + gate * density)).astype(BF16)
    grad_up = (grad_product * gate * phi).astype(BF16)
    gg_ref[:, :FF] = grad_gate
    gg_ref[:, FF:] = grad_up
    grad_normed = dot_nt(grad_gate, wu_ref[:, :FF]) + dot_nt(grad_up, wu_ref[:, FF:])
    normalized, rstd = norm_parts(hidden_ref[...])
    part, d_gain = norm_back(grad_normed, normalized, rstd, gain_ref[...].astype(F32))
    d_gain_ref[...] = d_gain
    grad_hidden = grad.astype(F32) + part
    grad_hidden_ref[...] = grad_hidden
    branch = grad_hidden.astype(BF16)
    branch_ref[...] = branch
    dot_ref[...] = dot_nt(branch, wo_ref[...]).T.astype(BF16)


def qkv_back_kernel(
    dq_ref, dkv_ref, x_ref, gain_ref, w_ref, cos_ref, sin_ref, grad_hidden_ref,
    grad_x_ref, gp_out_ref, d_gain_ref, gp_ref,
):
    cos = cos_ref[...]
    sin = sin_ref[...]

    def back(one, two):
        return one * cos + two * sin, two * cos - one * sin

    for head in range(HEADS):
        group, inner = head // GH, head % GH
        at = inner * HEAD_DIM
        one = dq_ref[group, at : at + 32, :].astype(F32)
        two = dq_ref[group, at + 32 : at + 64, :].astype(F32)
        gq = back(one, two)
        rows = slice(inner * ROWS, (inner + 1) * ROWS)
        kv = (dkv_ref[2 * group, rows, :].astype(F32) + dkv_ref[2 * group + 1, rows, :].astype(F32)).T
        gk = back(kv[:32], kv[32:64])
        base = head * HEAD_DIM
        gp_ref[base : base + 32, :] = gq[0]
        gp_ref[base + 32 : base + 64, :] = gq[1]
        gp_ref[D + base : D + base + 32, :] = gk[0]
        gp_ref[D + base + 32 : D + base + 64, :] = gk[1]
        gp_ref[2 * D + base : 2 * D + base + 64, :] = kv[64:]
    grad_normed = jnp.zeros((ROWS, D), F32)
    for block in range(9):
        cols = slice(block * 256, (block + 1) * 256)
        gp = gp_ref[cols, :].T.astype(BF16)
        gp_out_ref[:, cols] = gp
        grad_normed = grad_normed + dot_nt(gp, w_ref[:, cols])
    normalized, rstd = norm_parts(x_ref[...].astype(F32))
    part, d_gain = norm_back(grad_normed, normalized, rstd, gain_ref[...].astype(F32))
    d_gain_ref[...] = d_gain
    grad_x_ref[...] = (grad_hidden_ref[...] + part).astype(BF16)


MLP_ROWS = 576
QKV_ROWS = 320
SUM_ROWS = MLP_ROWS + QKV_ROWS


def weight_product(out_ref, shard, at, left_ref, left_sib_ref, right_ref, right_sib_ref):
    height = left_ref.shape[2]
    core = lax.rem(lax.axis_index("ctx"), 2)
    own = left_ref[shard, core]
    other = left_sib_ref[shard]
    for block in range(right_ref.shape[1] // D):
        cols = slice(block * D, (block + 1) * D)
        both = dot(own, right_ref[:, cols]) + dot(other, right_sib_ref[:, cols])
        row = at + block * height
        out_ref[shard, row : row + height, :] = both.astype(BF16)


def mlp_weights_kernel(
    normed_ref, normed_sib, product_ref, product_sib, ot_ref, ot_sib,
    gg_ref, gg_sib, grad_ref, grad_sib, branch_ref, branch_sib, out_ref,
):
    @pl.loop(0, 4)
    def _(shard):
        weight_product(out_ref, shard, 0, normed_ref, normed_sib, gg_ref, gg_sib)
        weight_product(out_ref, shard, 288, ot_ref, ot_sib, branch_ref, branch_sib)
        weight_product(out_ref, shard, 384, product_ref, product_sib, grad_ref, grad_sib)
        out_ref[shard, 528:, :] = jnp.zeros((48, D), BF16)


def qkv_weights_kernel(normed_ref, normed_sib, gp_ref, gp_sib, gain_one_ref, gain_two_ref, out_ref):
    gains = jnp.concatenate(
        [gain_one_ref[...], gain_two_ref[...], jnp.zeros((30, D), F32)], axis=0
    ).astype(BF16)

    @pl.loop(0, 4)
    def _(shard):
        weight_product(out_ref, shard, 0, normed_ref, normed_sib, gp_ref, gp_sib)
        out_ref[shard, 288:, :] = gains


def here():
    return lax.axis_index("section"), lax.axis_index("ctx"), lax.axis_index("wshard")


def flip(index, delta):
    for bit in (1, 2, 4, 8):
        if delta & bit:
            index = index + bit - 2 * bit * lax.rem(index // bit, 2)
    return index


def greet(peers):
    barrier = pltpu.get_barrier_semaphore()
    for peer in peers:
        pl.semaphore_signal(barrier, inc=1, device_id=peer, device_id_type=MESH)
    pl.semaphore_wait(barrier, len(peers))


def remote(src, dst, send, recv, peer):
    return pltpu.make_async_remote_copy(
        src_ref=src, dst_ref=dst, send_sem=send, recv_sem=recv, device_id=peer, device_id_type=MESH
    )


class Lines:
    count = 96

    def __init__(self, send, recv):
        self.send, self.recv, self.used, self.waits = send, recv, 0, []

    def make(self, src, dst, peer):
        at = self.used
        self.used += 1
        return remote(src, dst, self.send.at[at], self.recv.at[at], peer)

    def put(self, src, dst, peer):
        copy = self.make(src, dst, peer)
        copy.start()
        return copy

    def keep(self, src, dst):
        at = self.used
        self.used += 1
        copy = pltpu.make_async_copy(src, dst, self.send.at[at])
        copy.start()
        return copy


SEMS = [DMA((Lines.count,)), DMA((Lines.count,))]
ids = iter(range(1, 64))


def exchange_call(kernel, args, outs, scratch, collective_id, name):
    return pl.pallas_call(
        kernel,
        out_shape=outs,
        in_specs=[ANY] * len(args),
        out_specs=jax.tree.map(lambda _: ANY, outs),
        scratch_shapes=SEMS + list(scratch),
        compiler_params=pltpu.CompilerParams(
            collective_id=collective_id, has_side_effects=True, vmem_limit_bytes=VMEM_LIMIT
        ),
        name=name,
    )(*args)


def sibling_of(s, c, z):
    return (s, flip(c, 1), z)


def z_peers():
    s, c, z = here()
    return [(s, c, lax.rem(z + r, 4)) for r in (1, 3, 2)]


class Gather:
    def __init__(self, lines, layer, own, got, full):
        s, c, z = here()
        rows = full.shape[1] // 2
        self.half = half = pl.ds(pl.multiple_of(lax.rem(c, 2) * rows, 16), rows)
        self.lines, self.full = lines, full
        self.sibling = sibling_of(s, c, z)
        peers = z_peers()
        first = lines.used
        for source, holds in ((own, s == layer), (got, s != layer)):
            lines.used = first

            @pl.when(holds)
            def _():
                self.over = [lines.put(source.at[half], full.at[z, half], peer) for peer in peers]
                self.mine = lines.put(source.at[half], full.at[z, half], self.sibling)
                self.kept = lines.keep(source.at[half], full.at[z, half])

        lines.used = first
        block = full.at[z, half]
        self.over = [lines.make(block, block, peer) for peer in peers]
        self.mine = lines.make(block, block, self.sibling)
        at = lines.used
        self.kept = pltpu.make_async_copy(block, block, lines.send.at[at])
        lines.used += 1

    def forward(self):
        _, _, z = here()
        self.passed = [self.mine]
        for copy, r in zip(self.over, (1, 3, 2)):
            copy.wait_recv()
            block = self.full.at[lax.rem(z + 4 - r, 4), self.half]
            self.passed.append(self.lines.put(block, block, self.sibling))

    def finish(self):
        self.kept.wait()
        for copy in self.over:
            copy.wait_send()
        for copy in self.passed:
            copy.wait()


def full_shapes(pairs):
    return [sds((4, *own.shape), BF16) for own, _ in pairs]


def split_refs(refs, *counts):
    refs = list(refs)
    out = []
    for count in counts:
        out.append(refs[:count])
        refs = refs[count:]
    return out


class Scatter:
    def __init__(self, lines, comb, got):
        s, c, z = here()
        self.copies = [
            lines.put(comb.at[peer[2]], got.at[i], peer) for i, peer in enumerate(z_peers())
        ]

    def finish(self):
        for copy in self.copies:
            copy.wait()


def scatter_shapes(combs):
    return [sds((3, *comb.shape[1:]), BF16) for comb in combs]


def start_kernel(*refs):
    weights, (gain,), got, (full, gains), (send, recv) = split_refs(refs, 4, 1, 4, 2, 2)
    s, c, z = here()
    lines = Lines(send, recv)
    beside = [(1 - s, c, z), (1 - s, flip(c, 8), z)]
    across = [(1 - s, c, lax.rem(z + r, 4)) for r in range(4)]
    greet([sibling_of(s, c, z), *z_peers(), *across, beside[1]])
    copies = []

    def share(weight, target):
        rows, cols = weight.shape[0] // 2, weight.shape[1] // 2
        at = (
            pl.ds(pl.multiple_of(lax.rem(c, 2) * rows, 16), rows),
            pl.ds(pl.multiple_of(c // 8 * cols, 128), cols),
        )
        return [lines.put(weight.at[at], target.at[at], peer) for peer in beside]

    first = share(weights[0], got[0])
    copies += [lines.put(gain, gains.at[s, z], peer) for peer in (*z_peers(), *across)]
    kept = lines.keep(gain, gains.at[s, z])
    for i in range(1, 4):
        copies += share(weights[i], got[i])

    @pl.when(s == 1)
    def _():
        for copy in first:
            copy.wait_recv()

    gather = Gather(lines, 0, weights[0], got[0], full)
    gather.forward()
    gather.finish()

    @pl.when(s == 0)
    def _():
        for copy in first:
            copy.wait_recv()

    for copy in first:
        copy.wait_send()
    kept.wait()
    for copy in copies:
        copy.wait()


def start(weights, gain):
    outs = (
        *[sds(w.shape, BF16) for w in weights],
        sds((4, *weights[0].shape), BF16),
        sds((2, 4, *gain.shape), BF16),
    )
    res = exchange_call(start_kernel, (*weights, gain), outs, [], next(ids), "start")
    return res[:4], res[4], res[5]


def gather_kernel(layer, count, *refs):
    own, got, full, (send, recv) = split_refs(refs, count, count, count, 2)
    lines = Lines(send, recv)
    greet([sibling_of(*here()), *z_peers()])
    gathers = [Gather(lines, layer, *three) for three in zip(own, got, full)]
    for gather in gathers:
        gather.forward()
    for gather in gathers:
        gather.finish()


def gather(layer, pairs):
    args = [own for own, _ in pairs] + [got for _, got in pairs]
    kernel = functools.partial(gather_kernel, layer, len(pairs))
    return exchange_call(kernel, args, full_shapes(pairs), [], next(ids), "gather")


def spread_kernel(layer, count, *refs):
    (qkv_ref,), own_w, got_w, (q_ref, kv_ref), full, (send, recv) = split_refs(
        refs, 1, count, count, 2, count, 2
    )
    s, c, z = here()
    lines = Lines(send, recv)
    sibling = sibling_of(s, c, z)
    peers = {delta: (s, flip(c, delta), z) for delta in range(2, CTX, 2)}
    greet([sibling, *peers.values(), *(z_peers() if count else [])])
    kv_rows = pl.ds(GW, 2 * GW)
    q_rows = pl.ds(0, GW)
    order = [14, 10, 12, 8, 6, 4, 2]
    kv_sends, q_sends = {}, []
    for delta in order:
        peer = peers[delta]
        kv_sends[delta] = lines.put(qkv_ref.at[peer[1] // 4, kv_rows], kv_ref.at[c], peer)
        if delta % 4 == 0:
            q_sends.append(lines.put(qkv_ref.at[peer[1] // 4, q_rows], q_ref.at[c // 4], peer))
    gathers = [Gather(lines, layer, *three) for three in zip(own_w, got_w, full)]
    passed = [lines.put(qkv_ref.at[c // 4, kv_rows], kv_ref.at[c], sibling)]
    kept = [
        lines.keep(qkv_ref.at[c // 4, kv_rows], kv_ref.at[c]),
        lines.keep(qkv_ref.at[c // 4, q_rows], q_ref.at[c // 4]),
    ]
    for delta in reversed(order):
        kv_sends[delta].wait_recv()
        block = kv_ref.at[flip(c, delta)]
        passed.append(lines.put(block, block, sibling))
    for copy in kept:
        copy.wait()
    for copy in q_sends:
        copy.wait()
    for copy in kv_sends.values():
        copy.wait_send()
    for copy in passed:
        copy.wait()
    for gather in gathers:
        gather.forward()
    for gather in gathers:
        gather.finish()


def spread(qkv, layer, pairs):
    args = [qkv] + [own for own, _ in pairs] + [got for _, got in pairs]
    outs = [sds((4, GW, ROWS), BF16), sds((CTX, 2 * GW, ROWS), BF16)] + full_shapes(pairs)
    kernel = functools.partial(spread_kernel, layer, len(pairs))
    res = exchange_call(kernel, args, outs, [], next(ids), "spread")
    return res[0], res[1], res[2:]


class Pair:
    def __init__(self, lines, src, dst):
        s, c, z = here()
        if len(src.shape) == 4:
            src = src.at[:, 1 - lax.rem(c, 2)]
        self.copy = lines.put(src, dst, sibling_of(s, c, z))

    def finish(self):
        self.copy.wait()


def pair_shapes(arrays):
    return [sds((a.shape[0], *a.shape[2:]) if a.ndim == 4 else a.shape, BF16) for a in arrays]


def turn_kernel(layer, count, pairs, *refs):
    (x_ref,), own_w, got_w, sent, (o_ref,), full, taken, (send, recv) = split_refs(
        refs, 1, count, count, pairs, 1, count, pairs, 2
    )
    s, c, z = here()
    lines = Lines(send, recv)
    peers = [(s, flip(c, delta), z) for delta in (4, 8, 12)]
    greet(peers + ([sibling_of(s, c, z)] if count or pairs else []) + (z_peers() if count else []))
    copies = [lines.put(x_ref.at[peer[1] // 4], o_ref.at[c // 4], peer) for peer in peers]
    gathers = [Gather(lines, layer, *three) for three in zip(own_w, got_w, full)]
    moved = [Pair(lines, src, dst) for src, dst in zip(sent, taken)]
    lines.keep(x_ref.at[c // 4], o_ref.at[c // 4]).wait()
    for copy in copies:
        copy.wait()
    for gather in gathers:
        gather.forward()
    for work in gathers + moved:
        work.finish()


def turn(x, layer=0, pairs=(), acts=()):
    args = [x] + [own for own, _ in pairs] + [got for _, got in pairs] + list(acts)
    outs = [sds((4, GW, ROWS), BF16)] + full_shapes(pairs) + pair_shapes(acts)
    kernel = functools.partial(turn_kernel, layer, len(pairs), len(acts))
    res = exchange_call(kernel, args, outs, [], next(ids), "turn")
    return res[0], res[1 : 1 + len(pairs)], res[1 + len(pairs) :]


def pair_kernel(count, *refs):
    sent, taken, (send, recv) = split_refs(refs, count, count, 2)
    lines = Lines(send, recv)
    greet([sibling_of(*here())])
    for work in [Pair(lines, src, dst) for src, dst in zip(sent, taken)]:
        work.finish()


def pair(acts):
    kernel = functools.partial(pair_kernel, len(acts))
    return exchange_call(kernel, acts, pair_shapes(acts), [], next(ids), "pair")


def scatter_kernel(count, *refs):
    combs, got, (send, recv) = split_refs(refs, count, count, 2)
    lines = Lines(send, recv)
    greet(z_peers())
    for work in [Scatter(lines, *two) for two in zip(combs, got)]:
        work.finish()


def scatter(combs):
    kernel = functools.partial(scatter_kernel, len(combs))
    return exchange_call(kernel, combs, scatter_shapes(combs), [], next(ids), "scatter")


def return_kernel(count, *refs):
    (dq_ref, dkv_ref), combs, (dqo_ref, sums_ref), got, (send, recv, mine, theirs, total) = split_refs(
        refs, 2, count, 2, count, 5
    )
    s, c, z = here()
    lines = Lines(send, recv)
    core = lax.rem(c, 2)
    sibling = sibling_of(s, c, z)
    peers = {delta: (s, flip(c, delta), z) for delta in range(2, CTX, 2)}
    greet([sibling, *peers.values(), *(z_peers() if count else [])])
    passed = [lines.put(dkv_ref.at[2 * i + 1 - core], theirs.at[i], sibling) for i in range(8)]
    loads = [lines.keep(dkv_ref.at[2 * i + core], mine.at[i]) for i in range(8)]
    sends = [
        lines.put(dq_ref.at[peers[delta][1] // 4], dqo_ref.at[c // 4], peers[delta]) for delta in (4, 8, 12)
    ]
    scatters = [Scatter(lines, *two) for two in zip(combs, got)]
    kept = [lines.keep(dq_ref.at[c // 4], dqo_ref.at[c // 4])]
    for i in range(8):
        loads[i].wait()
        passed[i].wait()
        total[i] = (mine[i].astype(F32) + theirs[i].astype(F32)).astype(BF16)
    for delta in (14, 10, 12, 8, 6, 4, 2):
        sends.append(lines.put(total.at[peers[delta][1] // 2], sums_ref.at[c // 2], peers[delta]))
    kept.append(lines.keep(total.at[c // 2], sums_ref.at[c // 2]))
    for copy in kept + sends:
        copy.wait()
    for work in scatters:
        work.finish()


def give_back(dq, dkv, combs):
    block = pltpu.VMEM((8, 2 * GW, ROWS), BF16)
    outs = [sds((4, GW, ROWS), BF16), sds((8, 2 * GW, ROWS), BF16)] + scatter_shapes(combs)
    kernel = functools.partial(return_kernel, len(combs))
    res = exchange_call(kernel, [dq, dkv, *combs], outs, [block] * 3, next(ids), "give_back")
    return res[0], res[1], res[2:]


QUARTER = SUM_ROWS // 4


def finish_kernel(*refs):
    layers = split_refs(refs[:8], 4, 4)
    fin, send, recv, load, terms, own_sum, far_sum, parts, red = refs[8:]
    s, c, z = here()
    lines = Lines(send, recv)
    core = lax.rem(c, 2)
    sibling = sibling_of(s, c, z)
    near = {delta: (s, flip(c, delta), z) for delta in range(2, CTX, 2)}
    far = {delta: (1 - s, flip(c, delta), z) for delta in range(0, CTX, 2)}
    greet([sibling, *near.values(), *far.values()])

    def fill(target, layer):
        comb_m, got_m, comb_q, got_q = layer
        for comb, got, at, rows in ((comb_m, got_m, 0, MLP_ROWS), (comb_q, got_q, MLP_ROWS, QKV_ROWS)):
            copies = [pltpu.make_async_copy(comb.at[z], terms.at[0, pl.ds(at, rows)], load.at[0])]
            copies += [
                pltpu.make_async_copy(got.at[i], terms.at[i + 1, pl.ds(at, rows)], load.at[i + 1])
                for i in range(3)
            ]
            for copy in copies:
                copy.start()
            for copy in copies:
                copy.wait()
        for at in range(0, SUM_ROWS, 128):
            rows = slice(at, at + 128)
            both = terms[0, rows].astype(F32) + terms[1, rows].astype(F32)
            both += terms[2, rows].astype(F32) + terms[3, rows].astype(F32)
            target[rows] = both.astype(BF16)

    @pl.when(s == 0)
    def _():
        fill(far_sum, layers[1])

    @pl.when(s == 1)
    def _():
        fill(far_sum, layers[0])

    def block(at):
        rows = pl.ds(pl.multiple_of(lax.rem(at // 2, 4) * QUARTER, 16), QUARTER)
        return rows, pl.ds(pl.multiple_of(at // 8 * (D // 2), 128), D // 2)

    sends = [lines.put(far_sum.at[block(peer[1])], parts.at[8 + c // 2], peer) for peer in far.values()]

    @pl.when(s == 0)
    def _():
        fill(own_sum, layers[0])

    @pl.when(s == 1)
    def _():
        fill(own_sum, layers[1])

    sends += [lines.put(own_sum.at[block(peer[1])], parts.at[c // 2], peer) for peer in near.values()]
    lines.keep(own_sum.at[block(c)], parts.at[c // 2]).wait()
    for copy in sends:
        copy.wait()
    for at in range(0, QUARTER, 112):
        rows = slice(at, at + 112)
        total = parts[0, rows].astype(F32)
        for i in range(1, 16):
            total += parts[i, rows].astype(F32)
        red[rows] = total.astype(BF16)
    target = fin.at[core]
    kept = lines.keep(red, target.at[block(c)])
    passed = [lines.put(red, target.at[block(c)], sibling)]
    order = [14, 10, 12, 8, 6, 4, 2]
    shown = {delta: lines.put(red, target.at[block(c)], near[delta]) for delta in order}
    for delta in reversed(order):
        shown[delta].wait_recv()
        piece = target.at[block(flip(c, delta))]
        passed.append(lines.put(piece, piece, sibling))
    kept.wait()
    for copy in shown.values():
        copy.wait_send()
    for copy in passed:
        copy.wait()


def finish(zero, one):
    scratch = [
        DMA((4,)),
        pltpu.VMEM((4, SUM_ROWS, D), BF16),
        pltpu.VMEM((SUM_ROWS, D), BF16),
        pltpu.VMEM((SUM_ROWS, D), BF16),
        pltpu.VMEM((16, QUARTER, D // 2), BF16),
        pltpu.VMEM((QUARTER, D // 2), BF16),
    ]
    return exchange_call(
        finish_kernel, [*zero, *one], sds((2, SUM_ROWS, D), BF16), scratch, next(ids), "finish"
    )


def rope_tables():
    positions = (lax.axis_index("ctx") * ROWS + lax.iota(jnp.int32, ROWS)).astype(F32)
    frequency = 1.0 / 160000.0 ** (jnp.arange(HEAD_DIM // 2, dtype=F32) * 2.0 / HEAD_DIM)
    angles = frequency[:, None] * positions[None, :]
    return jnp.cos(angles), jnp.sin(angles)


def forward_layer(layer, x, gains, w_qkv, shards, tables):
    qkv, normed = compute_call(
        qkv_kernel,
        (x, gains[0], w_qkv, *tables),
        (sds((4, 3 * GW, ROWS), BF16), sds((D, ROWS), BF16)),
        name="norm_qkv",
    )
    q, kv, (w_up,) = spread(qkv, layer, [shards[2]])
    low, wide, totals = compute_call(
        attend_kernel,
        (q, kv),
        (sds((4, GW, ROWS), BF16), sds((4, GW, ROWS), F32), sds((GH, 8, 512), F32)),
        [pltpu.VMEM((2048, 512), F32)],
        name="attend",
    )
    ot, (w_out, w_down), _ = turn(low, layer, [shards[1], shards[3]])
    ot = ot.reshape(D, ROWS)
    w_out, w_up, w_down = w_out.reshape(D, D), w_up.reshape(D, 2 * FF), w_down.reshape(FF, D)
    out, hidden, gate_up, normed_two, product = compute_call(
        mlp_kernel,
        (ot, x, gains[1], w_out, w_up, w_down),
        (sds((ROWS, D), BF16), sds((ROWS, D), F32), sds((ROWS, 2 * FF), F32),
         sds((D, ROWS), BF16), sds((FF, ROWS), BF16)),
        name="mlp",
    )
    return out, (w_out, w_up, w_down), (x, normed, q, kv, wide, totals, ot, hidden, gate_up, normed_two, product)


def by_core(a):
    return a.reshape(4, 2, -1, ROWS)


def interleave(own, other):
    return [a for both in zip(own, other) for a in both]


def backward_layer(grad, stored, gains, w_qkv, weights, tables, before=()):
    w_out, w_up, w_down = weights
    x, normed, q, kv, wide, totals, ot, hidden, gate_up, normed_two, product = stored
    d_ot, grad_hidden, gg, branch, d_gain_two = compute_call(
        mlp_back_kernel,
        (grad, hidden, gate_up, gains[1], w_out, w_up, w_down),
        (sds((D, ROWS), BF16), sds((ROWS, D), F32), sds((ROWS, 2 * FF), BF16),
         sds((ROWS, D), BF16), sds((1, D), F32)),
        name="mlp_back",
    )
    acts = [by_core(normed_two), by_core(product), by_core(ot), gg, grad, branch]
    d_o, _, taken = turn(d_ot.reshape(4, GW, ROWS), acts=[*acts, *before[:2]])
    dq, dkv = compute_call(
        attend_back_kernel,
        (q, kv, wide, totals, d_o),
        (sds((4, GW, ROWS), BF16), sds((CTX, 2 * GW, ROWS), BF16)),
        name="attend_back",
    )
    combs = [
        compute_call(
            mlp_weights_kernel, interleave(acts, taken), sds((4, MLP_ROWS, D), BF16), name="mlp_weights"
        )
    ]
    if before:
        combs.append(qkv_weights(before, taken[len(acts) :]))
    dq, dkv, got = give_back(dq, dkv, combs)
    grad_x, gp, d_gain_one = compute_call(
        qkv_back_kernel,
        (dq, dkv, x, gains[0], w_qkv, *tables, grad_hidden),
        (sds((ROWS, D), BF16), sds((ROWS, 3 * D), BF16), sds((1, D), F32)),
        [pltpu.VMEM((3 * D, ROWS), F32)],
        name="qkv_back",
    )
    return grad_x, (by_core(normed), gp, d_gain_one, d_gain_two), combs, got


def qkv_weights(left, taken):
    return compute_call(
        qkv_weights_kernel,
        (*interleave(left[:2], taken), *left[2:]),
        sds((4, QKV_ROWS, D), BF16),
        name="qkv_weights",
    )


def swap_layers(zero, one):
    first = lax.axis_index("section") == 0
    other = lax.ppermute(jnp.where(first, one, zero), "section", [(0, 1), (1, 0)])
    kept = jnp.where(first, zero, one)
    return jnp.stack([jnp.where(first, kept, other), jnp.where(first, other, kept)])[None, :, None]


def local(inputs, cotangent, attn_gain, qkv_weight, out_weight, mlp_gain, up_weight, down_weight):
    first = lax.axis_index("section") == 0
    x = jnp.where(first, inputs[0, 0], inputs[1, 0])
    cot = jnp.where(first, cotangent[0, 0], cotangent[1, 0])
    own = [qkv_weight[0], out_weight[0], up_weight[0], down_weight[0]]
    gain = jnp.pad(jnp.concatenate([attn_gain, mlp_gain], axis=0), ((0, 14), (0, 64)))
    got, w_zero, gains = start(own, gain)
    shards = list(zip(own, got))
    gains = [
        [gains[layer, :, row, :192].reshape(1, D) for row in range(2)] for layer in range(2)
    ]
    tables = rope_tables()
    w_zero = w_zero.reshape(D, 3 * D)
    mid, weights_zero, stored_zero = forward_layer(0, x, gains[0], w_zero, shards, tables)
    (w_one,) = gather(1, [shards[0]])
    w_one = w_one.reshape(D, 3 * D)
    end, weights_one, stored_one = forward_layer(1, mid, gains[1], w_one, shards, tables)
    grad_mid, left_one, combs_one, got_one = backward_layer(
        cot, stored_one, gains[1], w_one, weights_one, tables
    )
    grad_start, left_zero, combs, got = backward_layer(
        grad_mid, stored_zero, gains[0], w_zero, weights_zero, tables, left_one
    )
    activations = swap_layers(mid, end)
    input_grads = swap_layers(grad_start, grad_mid)
    comb_last = qkv_weights(left_zero, pair(list(left_zero[:2])))
    (got_last,) = scatter([comb_last])
    fin = finish(
        [combs[0], got[0], comb_last, got_last], [combs_one[0], got_one[0], combs[1], got[1]]
    ).astype(F32)

    def columns(at):
        return fin[:, at : at + 288].reshape(2, 3, 96, D).transpose(0, 2, 1, 3).reshape(192, 3 * D)

    gain_at = MLP_ROWS + 288
    gain_sums = lax.dynamic_slice_in_dim(
        fin[0, gain_at : gain_at + 2] + fin[1, gain_at : gain_at + 2], lax.axis_index("wshard") * 192, 192, 1
    )
    return (
        activations,
        input_grads,
        gain_sums[0:1],
        columns(MLP_ROWS)[None],
        fin[:, 288:384].reshape(1, 192, D),
        gain_sums[1:2],
        columns(0)[None],
        fin[:, 384:528].reshape(1, 288, D),
    )


def solution(mesh):
    global ids
    ids = iter(range(1, 64))
    placed = (
        P(None, "wshard", "ctx", None),
        P(None, "wshard", "ctx", None),
        P("section", "wshard"),
        P("section", "wshard", None),
        P("section", "wshard", None),
        P("section", "wshard"),
        P("section", "wshard", None),
        P("section", "wshard", None),
    )
    return jax.shard_map(
        local,
        mesh=mesh,
        in_specs=placed,
        out_specs=(
            P("section", None, "wshard", "ctx", None),
            P("section", None, "wshard", "ctx", None),
            P("section", "wshard"),
            P("section", "wshard", None),
            P("section", "wshard", None),
            P("section", "wshard"),
            P("section", "wshard", None),
            P("section", "wshard", None),
        ),
        check_vma=False,
    )
```

time: 906 us -> 547 us (0.60)
  waiting for transfers between devices: 547 us -> 0.01 us
  Pallas kernels: 227 us -> 512 us
  blocking collectives: 53.5 us -> 0 us
  other arithmetic: 31.3 us -> 6.87 us
  between operations: 14.8 us -> 0.86 us
    pallas_call x8 -> x13, Pallas kernels: 128 us -> 400 us  [exchange_call(): pl.pallas_call(kernel, out_shape=outs, in_specs=[ANY] * len(args), out_sp...]
    reduce_scatter x4 -> x0, waiting for transfers between devices: 189 us -> none  [reduce_grads(): lax.psum_scatter(both, ('section', 'wshard'), scatter_dimension=0, tiled=...]
    all_gather x4 -> x0, waiting for transfers between devices: 170 us -> none  [gather_weights(): whole = lax.all_gather(a[0], ('section', 'wshard'), axis=0, tiled=True)]
    psum x1 -> x0, waiting for transfers between devices: 114 us -> none  [reduce_grads(): shards.append(lax.psum(part, 'ctx').astype(F32))]
    unnamed x13 -> x0, waiting for transfers between devices: 73.6 us -> none
    psum x1 -> x0, blocking collectives: 35.3 us -> none  [reduce_grads(): shards.append(lax.psum(part, 'ctx').astype(F32))]
    unnamed x1 -> x0, blocking collectives: 18.2 us -> none
    concatenate x8 -> x1, other arithmetic: 16.2 us -> 1.31 us  [local(): jnp.concatenate([attn_gain, mlp_gain], axis=0)]
  transfers between devices with their start and end apart: 13 -> 2, of which waited for: 10 -> 0; matrix products, arithmetic and copies ran while one was open for 5% -> 4% of each run, Pallas kernels for 12% -> 57%
where the time goes in v2:
time: 547 us; the launch traced here: 543 us
  Pallas kernels  512 us (94%)
  local copies, waits for them, and re-layouts  21.2 us (4%)
  other arithmetic  6.87 us (1%)
    pallas_call x13, Pallas kernels, exchange_call(): pl.pallas_call(kernel, out_shape=outs, in_specs=[ANY] * len(args), out_sp...  400 us
    pallas_call x16, Pallas kernels, compute_call(): pl.pallas_call(kernel, out_shape=outs, in_specs=[VM] * len(args), out_spe...  112 us
  transfers between devices with their start and end apart: 2, of which 0 were waited for; matrix products, arithmetic and copies ran while one was open for 4% of the time, Pallas kernels for 57%

profile of v2, /device:TPU:25, one launch (start us, length us, event | category | flops | bytes accessed | tf_op | source)
XLA Modules:
  0.0 543.4 jit_solution(17022532289520692253)
XLA Ops:
  2.0 31.2 %start.1 = (bf16[192,2304]{1,0:T(8,128)(2,1)}, bf16[192,768]{1,0:T(8,128)(2,1)}, bf16[192,2304]{1,0:T(8,128)(2,1)}, bf16[288,768]{1,0:T(8,128)(2,1)}, bf16[4,192...) custom-call(bf16[192,2304]{1,0:T(8,128)(2,1)} %bitcast.84, bf16[192,768]{1,0:T(8,128)(2,1)} %bitcast.86, ...), custom_call_target="tpu_custom_call" | custom-call | tf_op jit(solution)/shard_map/start/pallas_call | solution.py:345
  36.7 28.6 %gather.1 = bf16[4,192,2304]{2,1,0:T(8,128)(2,1)} custom-call(bf16[192,2304]{1,0:T(8,128)(2,1)} %bitcast.85, bf16[192,2304]{1,0:T(8,128)(2,1)} %get-tuple-element.105.refs_1_), custom_call_target="tpu_custom_call" | custom-call | tf_op jit(solution)/shard_map/gather/pallas_call | solution.py:345
  66.8 3.8 norm_qkv.2
  70.6 27.6 %spread.2 = (bf16[4,192,128]{2,1,0:T(8,128)(2,1)}, bf16[16,384,128]{2,1,0:T(8,128)(2,1)}, bf16[4,192,2304]{2,1,0:T(8,128)(2,1)}) custom-call(bf16[4,576,128]{2,1,0:T(8,128)(2,1)} %get-tuple-element.93.refs_0_, bf16[192,2304]{1,0:T(8,128)(2,1)} %bitcast.69, bf16[192,2304]{1,0:T(8,128)(2,1)} %get-tuple-element.94.refs_2_), custom_call_target="tpu_custom_call" | custom-call | tf_op jit(solution)/shard_map/spread/pallas_call | solution.py:345
  98.2 7.9 %attend.2 = (bf16[4,192,128]{2,1,0:T(8,128)(2,1)}, f32[4,192,128]{2,1,0:T(8,128)}, f32[3,8,512]{2,1,0:T(8,128)}) custom-call(bf16[4,192,128]{2,1,0:T(8,128)(2,1)} %get-tuple-element.95.q_ref, bf16[16,384,128]{2,1,0:T(8,128)(2,1)} %get-tuple-element.96.kv_ref), custom_call_target="tpu_custom_call" | custom-call | tf_op jit(solution)/shard_map/attend/pallas_call | solution.py:42
  106.1 26.8 %turn.4 = (bf16[4,192,128]{2,1,0:T(8,128)(2,1)}, bf16[4,192,768]{2,1,0:T(8,128)(2,1)}, bf16[4,288,768]{2,1,0:T(8,128)(2,1)}) custom-call(bf16[4,192,128]{2,1,0:T(8,128)(2,1)} %get-tuple-element.97.refs_0_, bf16[192,768]{1,0:T(8,128)(2,1)} %bitcast.87, bf16[288,768]{1,0:T(8,128)(2,1)} %bitcast.82, bf16[192,768]{1,0:T(8,128)(2,1)} %get-tuple-element.98.refs_3_, ...), custom_call_target="tpu_custom_call" | custom-call | tf_op jit(solution)/shard_map/turn/pallas_call | solution.py:345
  132.9 5.6 %mlp.2 = (bf16[128,768]{1,0:T(8,128)(2,1)}, f32[128,768]{1,0:T(8,128)}, f32[128,2304]{1,0:T(8,128)}, bf16[768,128]{1,0:T(8,128)(2,1)}, bf16[1152,128]{1,0:T(8,128)(2,1)}) custom-call(bf16[768,128]{1,0:T(8,128)(2,1)} %bitcast.92, bf16[128,768]{1,0:T(8,128)(2,1)} %select_bitcast_fusion.5.x_ref, bf16[1,768]{1,0:T(2,128)(2,1)} %reshape_squeeze.13.gain_ref, ...), custom_call_target="tpu_custom_call" | custom-call | tf_op jit(solution)/shard_map/mlp/pallas_call | solution.py:42
  138.5 3.8 norm_qkv.3
  142.4 27.2 %spread.3 = (bf16[4,192,128]{2,1,0:T(8,128)(2,1)}, bf16[16,384,128]{2,1,0:T(8,128)(2,1)}, bf16[4,192,2304]{2,1,0:T(8,128)(2,1)}) custom-call(bf16[4,576,128]{2,1,0:T(8,128)(2,1)} %get-tuple-element.106.refs_0_, bf16[192,2304]{1,0:T(8,128)(2,1)} %bitcast.70, bf16[192,2304]{1,0:T(8,128)(2,1)} %get-tuple-element.94.refs_2_), custom_call_target="tpu_custom_call" | custom-call | tf_op jit(solution)/shard_map/spread/pallas_call | solution.py:345
  169.6 7.9 %attend.3 = (bf16[4,192,128]{2,1,0:T(8,128)(2,1)}, f32[4,192,128]{2,1,0:T(8,128)}, f32[3,8,512]{2,1,0:T(8,128)}) custom-call(bf16[4,192,128]{2,1,0:T(8,128)(2,1)} %get-tuple-element.107.q_ref, bf16[16,384,128]{2,1,0:T(8,128)(2,1)} %get-tuple-element.108.kv_ref), custom_call_target="tpu_custom_call" | custom-call | tf_op jit(solution)/shard_map/attend/pallas_call | solution.py:42
  177.5 27.2 %turn.5 = (bf16[4,192,128]{2,1,0:T(8,128)(2,1)}, bf16[4,192,768]{2,1,0:T(8,128)(2,1)}, bf16[4,288,768]{2,1,0:T(8,128)(2,1)}) custom-call(bf16[4,192,128]{2,1,0:T(8,128)(2,1)} %get-tuple-element.109.refs_0_, bf16[192,768]{1,0:T(8,128)(2,1)} %bitcast.88, bf16[288,768]{1,0:T(8,128)(2,1)} %bitcast.83, bf16[192,768]{1,0:T(8,128)(2,1)} %get-tuple-element.98.refs_3_, ...), custom_call_target="tpu_custom_call" | custom-call | tf_op jit(solution)/shard_map/turn/pallas_call | solution.py:345
  204.7 5.7 %mlp.3 = (bf16[128,768]{1,0:T(8,128)(2,1)}, f32[128,768]{1,0:T(8,128)}, f32[128,2304]{1,0:T(8,128)}, bf16[768,128]{1,0:T(8,128)(2,1)}, bf16[1152,128]{1,0:T(8,128)(2,1)}) custom-call(bf16[768,128]{1,0:T(8,128)(2,1)} %bitcast.89, bf16[128,768]{1,0:T(8,128)(2,1)} %get-tuple-element.104.x_ref, bf16[1,768]{1,0:T(2,128)(2,1)} %reshape_squeeze.15.gain_ref, ...), custom_call_target="tpu_custom_call" | custom-call | tf_op jit(solution)/shard_map/mlp/pallas_call | solution.py:42
  214.4 7.0 %mlp_back.2 = (bf16[768,128]{1,0:T(8,128)(2,1)}, f32[128,768]{1,0:T(8,128)}, bf16[128,2304]{1,0:T(8,128)(2,1)}, bf16[128,768]{1,0:T(8,128)(2,1)}, f32[1,768]{1,0:T(1,128)}) custom-call(bf16[128,768]{1,0:T(8,128)(2,1)} %select_bitcast_fusion.2.g_ref.refs_5_.grad_ref, f32[128,768]{1,0:T(8,128)} %get-tuple-element.119.hidden_ref, ...), custom_call_target="tpu_custom_call" | custom-call | tf_op jit(solution)/shard_map/mlp_back/pallas_call | solution.py:42
  221.4 9.6 %turn.6 = (bf16[4,192,128]{2,1,0:T(8,128)(2,1)}, bf16[4,96,128]{2,1,0:T(8,128)(2,1)}, bf16[4,144,128]{2,1,0:T(8,128)(2,1)}, bf16[4,96,128]{2,1,0:T(8,128)(2,1)},...) custom-call(bf16[4,192,128]{2,1,0:T(8,128)(2,1)} %bitcast.109, ...), custom_call_target="tpu_custom_call" | custom-call | tf_op jit(solution)/shard_map/turn/pallas_call | solution.py:345
  231.0 16.6 %attend_back.2 = (bf16[4,192,128]{2,1,0:T(8,128)(2,1)}, bf16[16,384,128]{2,1,0:T(8,128)(2,1)}) custom-call(bf16[4,192,128]{2,1,0:T(8,128)(2,1)} %get-tuple-element.107.q_ref, bf16[16,384,128]{2,1,0:T(8,128)(2,1)} %get-tuple-element.108.kv_ref, f32[4,192,128]{2,1,0:T(8,128)} %get-tuple-element.117.wide_ref, f32[3,8,512]{2,1,0:T(8,128)} %get-tuple-element.118.totals_ref, ...), custom_call_target="tpu_custom_call" | custom-call | tf_op jit(solution)/shard_map/attend_back/pallas_call | solution.py:42
  247.7 6.0 %mlp_weights.2.refs_2_.refs_4_ = bf16[4,576,768]{2,1,0:T(8,128)(2,1)} custom-call(bf16[4,2,96,128]{3,2,1,0:T(8,128)(2,1)} %bitcast.101, bf16[4,96,128]{2,1,0:T(8,128)(2,1)} %get-tuple-element.129.normed_sib, bf16[4,2,144,128]{3,2,1,0:T(8,128)(2,1)} %bitcast.96, bf16[4,144,128]{2,1,0:T(8,128)(2,1)} %get-tuple-element.130.product_sib, ...), custom_call_target="tpu_custom_call" | custom-call | tf_op jit(solution)/shard_map/mlp_weights/pallas_call | solution.py:42
  253.6 43.4 %give_back.2 = (bf16[4,192,128]{2,1,0:T(8,128)(2,1)}, bf16[8,384,128]{2,1,0:T(8,128)(2,1)}, bf16[3,576,768]{2,1,0:T(8,128)(2,1)}) custom-call(bf16[4,192,128]{2,1,0:T(8,128)(2,1)} %get-tuple-element.127.refs_0_, bf16[16,384,128]{2,1,0:T(8,128)(2,1)} %get-tuple-element.128.refs_1_, bf16[4,576,768]{2,1,0:T(8,128)(2,1)} %mlp_weights.2.refs_2_.refs_4_), custom_call_target="tpu_custom_call" | custom-call | tf_op jit(solution)/shard_map/give_back/pallas_call | solution.py:345
  297.1 4.6 qkv_back.2
  301.7 7.0 %mlp_back.3 = (bf16[768,128]{1,0:T(8,128)(2,1)}, f32[128,768]{1,0:T(8,128)}, bf16[128,2304]{1,0:T(8,128)(2,1)}, bf16[128,768]{1,0:T(8,128)(2,1)}, f32[1,768]{1,0:T(1,128)}) custom-call(bf16[128,768]{1,0:T(8,128)(2,1)} %get-tuple-element.138.g_ref.refs_5_.grad_ref, f32[128,768]{1,0:T(8,128)} %get-tuple-element.139.hidden_ref, ...), custom_call_target="tpu_custom_call" | custom-call | tf_op jit(solution)/shard_map/mlp_back/pallas_call | solution.py:42
  308.7 11.5 %turn.7 = (bf16[4,192,128]{2,1,0:T(8,128)(2,1)}, bf16[4,96,128]{2,1,0:T(8,128)(2,1)}, bf16[4,144,128]{2,1,0:T(8,128)(2,1)}, bf16[4,96,128]{2,1,0:T(8,128)(2,1)},...) custom-call(bf16[4,192,128]{2,1,0:T(8,128)(2,1)} %bitcast.110, ...), custom_call_target="tpu_custom_call" | custom-call | tf_op jit(solution)/shard_map/turn/pallas_call | solution.py:345
  320.2 16.6 %attend_back.3 = (bf16[4,192,128]{2,1,0:T(8,128)(2,1)}, bf16[16,384,128]{2,1,0:T(8,128)(2,1)}) custom-call(bf16[4,192,128]{2,1,0:T(8,128)(2,1)} %get-tuple-element.95.q_ref, bf16[16,384,128]{2,1,0:T(8,128)(2,1)} %get-tuple-element.96.kv_ref, f32[4,192,128]{2,1,0:T(8,128)} %get-tuple-element.115.wide_ref, f32[3,8,512]{2,1,0:T(8,128)} %get-tuple-element.116.totals_ref, ...), custom_call_target="tpu_custom_call" | custom-call | tf_op jit(solution)/shard_map/attend_back/pallas_call | solution.py:42
  336.8 4.2 qkv_weights.2.refs_3_.refs_6_
  341.0 6.1 %mlp_weights.3.refs_2_.refs_0_ = bf16[4,576,768]{2,1,0:T(8,128)(2,1)} custom-call(bf16[4,2,96,128]{3,2,1,0:T(8,128)(2,1)} %bitcast.103, bf16[4,96,128]{2,1,0:T(8,128)(2,1)} %get-tuple-element.151.normed_sib, bf16[4,2,144,128]{3,2,1,0:T(8,128)(2,1)} %bitcast.98, bf16[4,144,128]{2,1,0:T(8,128)(2,1)} %get-tuple-element.152.product_sib, ...), custom_call_target="tpu_custom_call" | custom-call | tf_op jit(solution)/shard_map/mlp_weights/pallas_call | solution.py:42
  347.1 63.7 %give_back.3 = (bf16[4,192,128]{2,1,0:T(8,128)(2,1)}, bf16[8,384,128]{2,1,0:T(8,128)(2,1)}, bf16[3,576,768]{2,1,0:T(8,128)(2,1)}, bf16[3,320,768]{2,1,0:T(8,128)(2,1)}) custom-call(bf16[4,192,128]{2,1,0:T(8,128)(2,1)} %get-tuple-element.149.refs_0_, bf16[16,384,128]{2,1,0:T(8,128)(2,1)} %get-tuple-element.150.refs_1_, ...), custom_call_target="tpu_custom_call" | custom-call | tf_op jit(solution)/shard_map/give_back/pallas_call | solution.py:345
  410.8 4.7 qkv_back.3
  416.2 7.6 %pair.1 = (bf16[4,96,128]{2,1,0:T(8,128)(2,1)}, bf16[128,2304]{1,0:T(8,128)(2,1)}) custom-call(bf16[4,2,96,128]{3,2,1,0:T(8,128)(2,1)} %bitcast.104, bf16[128,2304]{1,0:T(8,128)(2,1)} %get-tuple-element.167.refs_1_.gp_ref), custom_call_target="tpu_custom_call" | custom-call | tf_op jit(solution)/shard_map/pair/pallas_call | solution.py:345
  423.8 4.2 qkv_weights.3.refs_0_.refs_2_
  428.0 26.5 %scatter.1.refs_3_ = bf16[3,320,768]{2,1,0:T(8,128)(2,1)} custom-call(bf16[4,320,768]{2,1,0:T(8,128)(2,1)} %qkv_weights.3.refs_0_.refs_2_), custom_call_target="tpu_custom_call" | custom-call | tf_op jit(solution)/shard_map/scatter/pallas_call | solution.py:345
  454.5 69.4 %finish.1 = bf16[2,896,768]{2,1,0:T(8,128)(2,1)} custom-call(bf16[4,576,768]{2,1,0:T(8,128)(2,1)} %mlp_weights.3.refs_2_.refs_0_, bf16[3,576,768]{2,1,0:T(8,128)(2,1)} %get-tuple-element.165.refs_1_, bf16[4,320,768]{2,1,0:T(8,128)(2,1)} %qkv_weights.3.refs_0_.refs_2_, bf16[3,320,768]{2,1,0:T(8,128)(2,1)} %scatter.1.refs_3_, ...), custom_call_target="tpu_custom_call" | custom-call | tf_op jit(solution)/shard_map/finish/pallas_call | solution.py:345
  530.8 2.7 copy.27
  533.5 2.5 broadcast_in_dim_reshape.6
  535.9 2.7 copy.26
  (44 shorter events, 22.6 us)
Async XLA Ops:
  36.7 29.4 %copy-start.6 = (bf16[2,1,128,768]{3,2,1,0:T(8,128)(2,1)S(1)}, bf16[2,1,128,768]{3,2,1,0:T(8,128)(2,1)}, u32[]{:S(2)}) copy-start(bf16[2,1,128,768]{3,2,1,0:T(8,128)(2,1)} %param.8) | copy-start | bytes 1179652
  204.6 5.7 %copy-start.1 = (bf16[128,768]{1,0:T(8,128)(2,1)S(1)}, bf16[128,768]{1,0:T(8,128)(2,1)}, u32[]{:S(2)}) copy-start(bf16[128,768]{1,0:T(8,128)(2,1)} %get-tuple-element.104.x_ref) | copy-start | bytes 589828
  204.7 9.1 %copy-start.7 = (bf16[2,1,128,768]{3,2,1,0:T(8,128)(2,1)S(1)}, bf16[2,1,128,768]{3,2,1,0:T(8,128)(2,1)}, u32[]{:S(2)}) copy-start(bf16[2,1,128,768]{3,2,1,0:T(8,128)(2,1)} %param.9) | copy-start | bytes 1179652
  211.3 330.4 %collective-permute-start = (bf16[128,768]{1,0:T(8,128)(2,1)S(1)}, bf16[128,768]{1,0:T(8,128)(2,1)S(1)}, u32[]{:S(2)}, u32[]{:S(2)}) collective-permute-start(bf16[128,768]{1,0:T(8,128)(2,1)S(1)} %broadcast_select_fusion.2), channel_id=1, source_target_pairs={{0,64},{64,0},{1,65},{65,1},{2,66},{66,2},{3,67},{67,3},{4,68},{68... | collective-permute-start | bytes 589832 | tf_op jit(solution)/shard_map/ppermute | solution.py:850
  410.8 4.7 copy-start.3
  416.2 126.4 %collective-permute-start.1 = (bf16[128,768]{1,0:T(8,128)(2,1)}, bf16[128,768]{1,0:T(8,128)(2,1)S(1)}, u32[]{:S(2)}, u32[]{:S(2)}) collective-permute-start(bf16[128,768]{1,0:T(8,128)(2,1)} %broadcast_select_fusion), channel_id=1, source_target_pairs={{0,64},{64,0},{1,65},{65,1},{2,66},{66,2},{3,67},{67,3},{4,68},{68... | collective-permute-start | bytes 589832 | tf_op jit(solution)/shard_map/ppermute | solution.py:850
  524.0 4.7 copy-start
  538.6 3.1 copy-start.2
  538.6 3.1 copy-start.4
  541.1 1.5 copy-start.5

commit v3 on v2

v3 whole, which is shorter than its diff:
```python
import functools

import jax
import jax.numpy as jnp
from jax import lax
from jax.experimental import pallas as pl
from jax.experimental.pallas import tpu as pltpu
from jax.sharding import PartitionSpec as P

D = 768
HEADS = 12
HEAD_DIM = 64
FF = 1152
ROWS = 128
GROUPS = 4
GH = HEADS // GROUPS
GW = GH * HEAD_DIM
CTX = 16
SCALE = HEAD_DIM ** (-0.5)
F32 = jnp.float32
BF16 = jnp.bfloat16
MESH = pl.DeviceIdType.MESH
DMA = pltpu.SemaphoreType.DMA
ANY = pl.BlockSpec(memory_space=pl.ANY)
VM = pl.BlockSpec(memory_space=pltpu.VMEM)
VMEM_LIMIT = 56 * 1024 * 1024


def dot(a, b):
    return jnp.dot(a, b, preferred_element_type=F32)


def dot_nt(a, b):
    return lax.dot_general(a, b, (((1,), (1,)), ((), ())), preferred_element_type=F32)


def sds(shape, dtype):
    return jax.ShapeDtypeStruct(shape, dtype)


def compute_call(kernel, args, outs, scratch=(), name=None, far=0):
    return pl.pallas_call(
        kernel,
        out_shape=outs,
        in_specs=[VM] * (len(args) - far) + [ANY] * far,
        out_specs=jax.tree.map(lambda _: VM, outs),
        scratch_shapes=list(scratch),
        compiler_params=pltpu.CompilerParams(vmem_limit_bytes=VMEM_LIMIT),
        name=name,
    )(*args)


def fetch(src, dst, sem):
    copy = pltpu.make_async_copy(src, dst, sem)
    copy.start()
    return copy


def turned_low(x):
    return x.astype(F32).T.astype(BF16)


def norm_parts(source):
    centered = source - jnp.mean(source, axis=-1, keepdims=True)
    variance = jnp.mean(centered * centered, axis=-1, keepdims=True)
    rstd = lax.rsqrt(variance + 1e-05)
    return centered * rstd, rstd


def norm_back(grad, normalized, rstd, gain):
    inner = grad * gain
    mean_one = jnp.mean(inner, axis=-1, keepdims=True)
    mean_two = jnp.mean(inner * normalized, axis=-1, keepdims=True)
    grad_gain = jnp.sum(grad * normalized, axis=0, keepdims=True)
    return rstd * (inner - mean_one - normalized * mean_two), grad_gain


def split_refs(refs, *counts):
    refs = list(refs)
    out = []
    for count in counts:
        out.append(refs[:count])
        refs = refs[count:]
    return out


def qkv_kernel(layer, x_ref, gain_ref, cos_ref, sin_ref, w_all, qkv_ref, normed_ref, w_ref, sem):
    load = fetch(w_all.at[layer], w_ref, sem)
    normalized, _ = norm_parts(x_ref[...].astype(F32))
    normed = (normalized * gain_ref[...].astype(F32)).astype(BF16)
    normed_ref[...] = turned_low(normed)
    load.wait()
    cos = cos_ref[...]
    sin = sin_ref[...]
    for part in range(3):
        for block in range(3):
            at = part * D + block * 256
            turned = dot(normed, w_ref[:, at : at + 256]).T
            for head_at in range(4):
                head = block * 4 + head_at
                one = turned[head_at * 64 : head_at * 64 + 32]
                two = turned[head_at * 64 + 32 : head_at * 64 + 64]
                if part < 2:
                    one, two = one * cos - two * sin, two * cos + one * sin
                if part == 0:
                    one, two = one * SCALE, two * SCALE
                row = part * GW + (head % GH) * HEAD_DIM
                qkv_ref[head // GH, row : row + 32, :] = one.astype(BF16)
                qkv_ref[head // GH, row + 32 : row + 64, :] = two.astype(BF16)


CHUNK = 256
CHUNKS = 2048 // CHUNK
PAIR = CHUNK // ROWS


def attend_kernel(q_ref, kv_ref, low_ref, wide_ref, totals_ref, s_ref):
    @pl.loop(0, GH)
    def _(h):
        at = pl.multiple_of(h * HEAD_DIM, HEAD_DIM)
        value_at = pl.multiple_of(h * HEAD_DIM + GW, HEAD_DIM)
        qt = jnp.concatenate([q_ref[i, pl.ds(at, HEAD_DIM), :] for i in range(4)], axis=1)
        top = jnp.full((8, 512), -jnp.inf, F32)
        for c in range(CHUNKS):
            keys = jnp.concatenate(
                [kv_ref[c * PAIR + i, pl.ds(at, HEAD_DIM), :].T for i in range(PAIR)], axis=0
            )
            scores = dot(keys, qt)
            s_ref[c * CHUNK : (c + 1) * CHUNK, :] = scores
            top = jnp.maximum(top, jnp.max(scores.reshape(CHUNK // 8, 8, 512), axis=0))
        top = jnp.max(top, axis=0, keepdims=True)
        total = jnp.zeros((8, 512), F32)
        acc = jnp.zeros((HEAD_DIM, 512), F32)
        for c in range(CHUNKS):
            p = jnp.exp(s_ref[c * CHUNK : (c + 1) * CHUNK, :] - top)
            total = total + jnp.sum(p.reshape(CHUNK // 8, 8, 512), axis=0)
            values = jnp.concatenate(
                [kv_ref[c * PAIR + i, pl.ds(value_at, HEAD_DIM), :] for i in range(PAIR)], axis=1
            )
            acc = acc + dot(values, p.astype(BF16))
        total = jnp.sum(total, axis=0, keepdims=True)
        out = acc / total
        totals_ref[h] = jnp.broadcast_to(top + jnp.log(total), (8, 512))
        for i in range(4):
            piece = out[:, i * ROWS : (i + 1) * ROWS]
            wide_ref[i, pl.ds(at, HEAD_DIM), :] = piece
            low_ref[i, pl.ds(at, HEAD_DIM), :] = piece.astype(BF16)


def attend_back_kernel(q_ref, kv_ref, wide_ref, totals_ref, do_ref, dq_ref, dkv_ref):
    @pl.loop(0, GH)
    def _(h):
        at = pl.multiple_of(h * HEAD_DIM, HEAD_DIM)
        value_at = pl.multiple_of(h * HEAD_DIM + GW, HEAD_DIM)
        out_at = pl.multiple_of(h * ROWS, ROWS)
        qt = jnp.concatenate([q_ref[i, pl.ds(at, HEAD_DIM), :] for i in range(4)], axis=1)
        dot_t = jnp.concatenate([do_ref[i, pl.ds(at, HEAD_DIM), :] for i in range(4)], axis=1)
        wide = jnp.concatenate([wide_ref[i, pl.ds(at, HEAD_DIM), :] for i in range(4)], axis=1)
        delta = jnp.sum(wide * dot_t.astype(F32), axis=0, keepdims=True)
        totals = totals_ref[h, 0:1, :]
        zero = jnp.zeros((512, HEAD_DIM), BF16)
        sides = jnp.concatenate(
            [
                jnp.concatenate([qt.T, zero], axis=1),
                jnp.concatenate([zero, dot_t.T], axis=1),
            ],
            axis=0,
        )

        def step(c, acc):
            keys_t = [kv_ref[c * PAIR + i, pl.ds(at, HEAD_DIM), :] for i in range(PAIR)]
            values_t = [kv_ref[c * PAIR + i, pl.ds(value_at, HEAD_DIM), :] for i in range(PAIR)]
            keys = jnp.concatenate([k.T for k in keys_t], axis=0)
            values = jnp.concatenate([v.T for v in values_t], axis=0)
            p = jnp.exp(dot(keys, qt) - totals)
            ds = (p * (dot(values, dot_t) - delta)).astype(BF16)
            both = jnp.concatenate([ds, p.astype(BF16)], axis=1)
            grads = dot(both, sides).astype(BF16)
            for i in range(PAIR):
                dkv_ref[c * PAIR + i, pl.ds(out_at, ROWS), :] = grads[i * ROWS : (i + 1) * ROWS]
            return acc + dot(jnp.concatenate(keys_t, axis=1), ds)

        acc = lax.fori_loop(0, CHUNKS, step, jnp.zeros((HEAD_DIM, 512), F32)) * SCALE
        for i in range(4):
            dq_ref[i, pl.ds(at, HEAD_DIM), :] = acc[:, i * ROWS : (i + 1) * ROWS].astype(BF16)


def mlp_kernel(
    layer, ot_ref, x_ref, gain_ref, wo_all, wu_all, wd_all,
    out_ref, hidden_ref, gate_up_ref, normed_ref, product_ref, wo_ref, wu_ref, wd_ref, sem,
):
    loads = [
        fetch(src.at[layer], dst, sem.at[i])
        for i, (src, dst) in enumerate([(wo_all, wo_ref), (wu_all, wu_ref), (wd_all, wd_ref)])
    ]
    attended = turned_low(ot_ref[...])
    loads[0].wait()
    hidden = x_ref[...].astype(F32) + dot(attended, wo_ref[...])
    hidden_ref[...] = hidden
    normalized, _ = norm_parts(hidden)
    normed = (normalized * gain_ref[...].astype(F32)).astype(BF16)
    normed_ref[...] = turned_low(normed)
    loads[1].wait()
    gate_up = dot(normed, wu_ref[...])
    gate_up_ref[...] = gate_up
    gate = gate_up[:, :FF]
    phi = 0.5 * (1.0 + lax.erf(gate * 0.5**0.5))
    product = (gate * phi * gate_up[:, FF:]).astype(BF16)
    product_ref[...] = turned_low(product)
    loads[2].wait()
    out_ref[...] = (hidden + dot(product, wd_ref[...])).astype(BF16)


def mlp_back_kernel(
    layer, g_ref, hidden_ref, gate_up_ref, gain_ref, wo_all, wu_all, wd_all,
    dot_ref, grad_hidden_ref, gg_ref, branch_ref, d_gain_ref, wo_ref, wu_ref, wd_ref, sem,
):
    loads = [
        fetch(src.at[layer], dst, sem.at[i])
        for i, (src, dst) in enumerate([(wd_all, wd_ref), (wu_all, wu_ref), (wo_all, wo_ref)])
    ]
    grad = g_ref[...]
    loads[0].wait()
    grad_product = dot_nt(grad, wd_ref[...])
    gate = gate_up_ref[:, :FF]
    up = gate_up_ref[:, FF:]
    phi = 0.5 * (1.0 + lax.erf(gate * 0.5**0.5))
    density = jnp.exp(-0.5 * gate * gate) * 0.3989422804014327
    grad_gate = (grad_product * up * (phi + gate * density)).astype(BF16)
    grad_up = (grad_product * gate * phi).astype(BF16)
    gg_ref[:, :FF] = grad_gate
    gg_ref[:, FF:] = grad_up
    loads[1].wait()
    grad_normed = dot_nt(grad_gate, wu_ref[:, :FF]) + dot_nt(grad_up, wu_ref[:, FF:])
    normalized, rstd = norm_parts(hidden_ref[...])
    part, d_gain = norm_back(grad_normed, normalized, rstd, gain_ref[...].astype(F32))
    d_gain_ref[...] = d_gain
    grad_hidden = grad.astype(F32) + part
    grad_hidden_ref[...] = grad_hidden
    branch = grad_hidden.astype(BF16)
    branch_ref[...] = branch
    loads[2].wait()
    dot_ref[...] = dot_nt(branch, wo_ref[...]).T.astype(BF16)


def qkv_back_kernel(
    layer, dq_ref, dkv_ref, x_ref, gain_ref, cos_ref, sin_ref, grad_hidden_ref, gain_two_ref, w_all,
    grad_x_ref, gp_out_ref, gains_ref, gp_ref, w_ref, sem,
):
    load = fetch(w_all.at[layer], w_ref, sem)
    cos = cos_ref[...]
    sin = sin_ref[...]

    def back(one, two):
        return one * cos + two * sin, two * cos - one * sin

    for head in range(HEADS):
        group, inner = head // GH, head % GH
        at = inner * HEAD_DIM
        one = dq_ref[group, at : at + 32, :].astype(F32)
        two = dq_ref[group, at + 32 : at + 64, :].astype(F32)
        gq = back(one, two)
        rows = slice(inner * ROWS, (inner + 1) * ROWS)
        kv = (dkv_ref[2 * group, rows, :].astype(F32) + dkv_ref[2 * group + 1, rows, :].astype(F32)).T
        gk = back(kv[:32], kv[32:64])
        base = head * HEAD_DIM
        gp_ref[base : base + 32, :] = gq[0]
        gp_ref[base + 32 : base + 64, :] = gq[1]
        gp_ref[D + base : D + base + 32, :] = gk[0]
        gp_ref[D + base + 32 : D + base + 64, :] = gk[1]
        gp_ref[2 * D + base : 2 * D + base + 64, :] = kv[64:]
    load.wait()
    grad_normed = jnp.zeros((ROWS, D), F32)
    for block in range(9):
        cols = slice(block * 256, (block + 1) * 256)
        gp = gp_ref[cols, :].T.astype(BF16)
        gp_out_ref[:, cols] = gp
        grad_normed = grad_normed + dot_nt(gp, w_ref[:, cols])
    normalized, rstd = norm_parts(x_ref[...].astype(F32))
    part, d_gain = norm_back(grad_normed, normalized, rstd, gain_ref[...].astype(F32))
    gains_ref[...] = jnp.concatenate(
        [d_gain, gain_two_ref[...], jnp.zeros((14, D), F32)], axis=0
    ).astype(BF16)
    grad_x_ref[...] = (grad_hidden_ref[...] + part).astype(BF16)


MLP_ROWS = 576
QKV_ROWS = 320
SUM_ROWS = MLP_ROWS + QKV_ROWS


def load_rows(sems, own, rest, left, right):
    section = lax.axis_index("section")
    core = lax.rem(lax.axis_index("ctx"), 2)

    def lanes(i):
        return left.at[:, :, pl.ds(i * ROWS, ROWS)]

    def rows(i):
        return right.at[pl.ds(i * ROWS, ROWS)]

    for layer, (a, g) in enumerate(own):

        @pl.when(section == layer)
        def _():
            fetch(a.at[:, core], lanes(0), sems.at[0])
            fetch(g, rows(0), sems.at[1])

    (a_sib, a_far, a_both), (g_sib, g_far, g_both) = rest
    copies = [
        fetch(a_sib, lanes(1), sems.at[2]),
        fetch(a_far.at[:, core], lanes(2), sems.at[3]),
        fetch(a_both, lanes(3), sems.at[4]),
        fetch(g_sib, rows(1), sems.at[5]),
        fetch(g_far, rows(2), sems.at[6]),
        fetch(g_both, rows(3), sems.at[7]),
    ]
    copies.append(pltpu.make_async_copy(a_sib, lanes(0), sems.at[0]))
    copies.append(pltpu.make_async_copy(g_sib, rows(0), sems.at[1]))
    return copies


def weight_product(out_ref, at, left, right):
    height = left.shape[1]

    @pl.loop(0, 4)
    def _(shard):
        for block in range(right.shape[1] // D):
            row = at + block * height
            both = dot(left[shard], right[:, block * D : (block + 1) * D])
            out_ref[shard, row : row + height, :] = both.astype(BF16)


def mlp_weights_kernel(*refs):
    zero, one, lefts, rights, (out_ref,), scratch, (sems,) = split_refs(refs, 6, 6, 9, 9, 1, 6, 1)
    copies = []
    for i in range(3):
        own = [(layer[i], layer[i + 3]) for layer in (zero, one)]
        rest = lefts[i::3], rights[i::3]
        copies.append(load_rows(sems.at[i], own, rest, scratch[2 * i], scratch[2 * i + 1]))
    for i, at in ((0, 0), (2, 288), (1, 384)):
        for copy in copies[i]:
            copy.wait()
        weight_product(out_ref, at, scratch[2 * i], scratch[2 * i + 1])
    out_ref[:, 528:, :] = jnp.zeros((4, 48, D), BF16)


def qkv_weights_kernel(*refs):
    gain_far, zero, one, lefts, rights, (out_ref,), (left, right, gain, sems) = split_refs(
        refs, 1, 3, 3, 3, 3, 1, 4
    )
    copies = load_rows(sems, [(a, g) for a, g, _ in (zero, one)], (lefts, rights), left, right)
    section = lax.axis_index("section")
    for layer, (_, _, own) in enumerate((zero, one)):

        @pl.when(section == layer)
        def _():
            fetch(own, gain, sems.at[8]).wait()

    gains = (gain[...].astype(F32) + gain_far[0][...].astype(F32)).astype(BF16)
    for shard in range(4):
        out_ref[shard, 288:304, :] = gains
        out_ref[shard, 304:, :] = jnp.zeros((16, D), BF16)
    for copy in copies:
        copy.wait()
    weight_product(out_ref, 0, left, right)


def assemble_kernel(fin_ref, up_ref, out_ref, down_ref, qkv_ref, gains_ref):
    for half in range(2):
        rows = slice(half * 96, half * 96 + 96)
        for block in range(3):
            cols = slice(block * D, (block + 1) * D)
            up_ref[rows, cols] = fin_ref[half, block * 96 : block * 96 + 96, :].astype(F32)
            at = MLP_ROWS + block * 96
            qkv_ref[rows, cols] = fin_ref[half, at : at + 96, :].astype(F32)
        out_ref[rows, :] = fin_ref[half, 288:384, :].astype(F32)
        down_ref[half * 144 : half * 144 + 144, :] = fin_ref[half, 384:528, :].astype(F32)
    gain_rows = slice(MLP_ROWS + 288, MLP_ROWS + 304)
    gains_ref[...] = fin_ref[0, gain_rows, :].astype(F32) + fin_ref[1, gain_rows, :].astype(F32)


def here():
    return lax.axis_index("section"), lax.axis_index("ctx"), lax.axis_index("wshard")


def flip(index, delta):
    for bit in (1, 2, 4, 8):
        if delta & bit:
            index = index + bit - 2 * bit * lax.rem(index // bit, 2)
    return index


def greet(peers):
    barrier = pltpu.get_barrier_semaphore()
    for peer in peers:
        pl.semaphore_signal(barrier, inc=1, device_id=peer, device_id_type=MESH)
    pl.semaphore_wait(barrier, len(peers))


def remote(src, dst, send, recv, peer):
    return pltpu.make_async_remote_copy(
        src_ref=src, dst_ref=dst, send_sem=send, recv_sem=recv, device_id=peer, device_id_type=MESH
    )


class Lines:
    count = 112

    def __init__(self, send, recv):
        self.send, self.recv, self.used, self.waits = send, recv, 0, []

    def make(self, src, dst, peer):
        at = self.used
        self.used += 1
        return remote(src, dst, self.send.at[at], self.recv.at[at], peer)

    def put(self, src, dst, peer):
        copy = self.make(src, dst, peer)
        copy.start()
        return copy

    def keep(self, src, dst):
        at = self.used
        self.used += 1
        copy = pltpu.make_async_copy(src, dst, self.send.at[at])
        copy.start()
        return copy


SEMS = [DMA((Lines.count,)), DMA((Lines.count,))]
ids = iter(range(1, 64))


def exchange_call(kernel, args, outs, scratch, collective_id, name):
    return pl.pallas_call(
        kernel,
        out_shape=outs,
        in_specs=[ANY] * len(args),
        out_specs=jax.tree.map(lambda _: ANY, outs),
        scratch_shapes=SEMS + list(scratch),
        compiler_params=pltpu.CompilerParams(
            collective_id=collective_id, has_side_effects=True, vmem_limit_bytes=VMEM_LIMIT
        ),
        name=name,
    )(*args)


def sibling_of(s, c, z):
    return (s, flip(c, 1), z)


def z_peers():
    s, c, z = here()
    return [(s, c, lax.rem(z + r, 4)) for r in (1, 3, 2)]


def beside_peers():
    s, c, z = here()
    return [(1 - s, c, z), (1 - s, flip(c, 8), z)]


class Gather:
    def __init__(self, lines, own, full):
        s, c, z = here()
        rows, cols = full.shape[2] // 2, full.shape[3] // 2
        self.rows = pl.ds(pl.multiple_of(lax.rem(c, 2) * rows, 16), rows)
        self.cols = [
            pl.ds(pl.multiple_of(side * cols, 128), cols) for side in (c // 8, 1 - c // 8)
        ]
        self.halves = [pl.ds(0, cols), pl.ds(cols, cols)]
        self.lines, self.full = lines, full
        self.sibling = sibling_of(s, c, z)
        after, before, _ = z_peers()
        self.step = []
        for cut, order in ((0, (after, before)), (1, (after, before))):
            where = full.at[s, z, self.rows, self.halves[cut]]
            piece = own.at[self.rows, self.halves[cut]]
            self.step.append([lines.put(piece, where, peer) for peer in order])
        self.peers = (after, before)
        self.aside = [self.beside(own.at[self.rows, self.cols[0]], z)]
        whole = full.at[s, z, self.rows]
        self.passed = [lines.put(own.at[self.rows], whole, self.sibling)]
        self.kept = lines.keep(own.at[self.rows], whole)
        self.sent = []

    def beside(self, src, z):
        s, _, _ = here()
        where = self.full.at[s, z, self.rows, self.cols[0]]
        return [self.lines.put(src, where, peer) for peer in beside_peers()]

    def from_neighbours(self):
        s, _, z = here()
        self.sources = [lax.rem(z + 3, 4), lax.rem(z + 1, 4)]
        self.second = []
        for side in (0, 1):
            self.step[side][side].wait_recv()
            block = self.full.at[s, self.sources[side], self.rows, self.halves[side]]
            self.second.append(self.lines.put(block, block, self.peers[side]))
        for side in (0, 1):
            self.step[1 - side][side].wait_recv()
            self.onward(self.sources[side])

    def onward(self, z):
        s, _, _ = here()
        block = self.full.at[s, z, self.rows]
        self.passed.append(self.lines.put(block, block, self.sibling))
        self.aside.append(self.beside(block.at[:, self.cols[0]], z))

    def from_opposite(self):
        _, _, z = here()
        for copy in self.second:
            copy.wait_recv()
        self.onward(lax.rem(z + 2, 4))

    def from_beside(self):
        s, _, z = here()
        for copies, source in zip(self.aside, (z, *self.sources, lax.rem(z + 2, 4))):
            for i, copy in enumerate(copies):
                copy.wait_recv()
                block = self.full.at[1 - s, source, self.rows, self.cols[i]]
                self.passed.append(self.lines.put(block, block, self.sibling))

    def finish(self):
        self.kept.wait()
        for copies in (*self.step, *self.aside, self.second):
            for copy in copies:
                copy.wait_send()
        for copy in self.passed:
            copy.wait()


def run_gathers(gathers):
    for gather in gathers:
        gather.from_neighbours()
    for gather in gathers:
        gather.from_opposite()
    for gather in gathers:
        gather.from_beside()
    for gather in gathers:
        gather.finish()


def full_shapes(weights):
    return [sds((2, 4, *w.shape), BF16) for w in weights]


def gather_peers():
    return [sibling_of(*here()), *z_peers()[:2], *beside_peers()]


class Scatter:
    def __init__(self, lines, comb, got):
        s, c, z = here()
        self.copies = [
            lines.put(comb.at[peer[2]], got.at[i], peer) for i, peer in enumerate(z_peers())
        ]

    def finish(self):
        for copy in self.copies:
            copy.wait()


def scatter_shapes(combs):
    return [sds((3, *comb.shape[1:]), BF16) for comb in combs]


def start_kernel(*refs):
    own, gain, full, gains, send, recv = refs
    s, c, z = here()
    lines = Lines(send, recv)
    across = [(1 - s, c, lax.rem(z + r, 4)) for r in (1, 3, 2)]
    greet([*gather_peers(), z_peers()[2], *across])
    gather = Gather(lines, own, full)
    copies = [
        lines.put(gain, gains.at[s, z], peer) for peer in (*z_peers(), beside_peers()[0], *across)
    ]
    kept = lines.keep(gain, gains.at[s, z])
    run_gathers([gather])
    kept.wait()
    for copy in copies:
        copy.wait()


def start(weight, gain):
    outs = (*full_shapes([weight]), sds((2, 4, *gain.shape), BF16))
    return exchange_call(start_kernel, (weight, gain), outs, [], next(ids), "start")


def spread_kernel(count, *refs):
    (qkv_ref,), own_w, (q_ref, kv_ref), full, (send, recv) = split_refs(refs, 1, count, 2, count, 2)
    s, c, z = here()
    lines = Lines(send, recv)
    sibling = sibling_of(s, c, z)
    peers = {delta: (s, flip(c, delta), z) for delta in range(2, CTX, 2)}
    greet([sibling, *peers.values(), *(gather_peers()[1:] if count else [])])
    kv_rows = pl.ds(GW, 2 * GW)
    q_rows = pl.ds(0, GW)
    order = [14, 10, 12, 8, 6, 4, 2]
    kv_sends, q_sends = {}, []
    for delta in order:
        peer = peers[delta]
        kv_sends[delta] = lines.put(qkv_ref.at[peer[1] // 4, kv_rows], kv_ref.at[c], peer)
        if delta % 4 == 0:
            q_sends.append(lines.put(qkv_ref.at[peer[1] // 4, q_rows], q_ref.at[c // 4], peer))
    gathers = [Gather(lines, *two) for two in zip(own_w, full)]
    passed = [lines.put(qkv_ref.at[c // 4, kv_rows], kv_ref.at[c], sibling)]
    kept = [
        lines.keep(qkv_ref.at[c // 4, kv_rows], kv_ref.at[c]),
        lines.keep(qkv_ref.at[c // 4, q_rows], q_ref.at[c // 4]),
    ]
    for delta in reversed(order):
        kv_sends[delta].wait_recv()
        block = kv_ref.at[flip(c, delta)]
        passed.append(lines.put(block, block, sibling))
    for copy in kept:
        copy.wait()
    for copy in q_sends:
        copy.wait()
    for copy in kv_sends.values():
        copy.wait_send()
    for copy in passed:
        copy.wait()
    run_gathers(gathers)


def spread(qkv, weights):
    outs = [sds((4, GW, ROWS), BF16), sds((CTX, 2 * GW, ROWS), BF16)] + full_shapes(weights)
    kernel = functools.partial(spread_kernel, len(weights))
    res = exchange_call(kernel, [qkv, *weights], outs, [], next(ids), "spread")
    return res[0], res[1], res[2:]


class Meet:
    def __init__(self, lines, zero, one, sib, far, both):
        s, c, z = here()
        self.core = core = lax.rem(c, 2)
        self.lines, self.far, self.both = lines, far, both
        self.sibling = sibling_of(s, c, z)
        peer = (1 - s, flip(c, 8) * core + c * (1 - core), z)
        first = lines.used
        for layer, (near, other) in enumerate(((zero, one), (one, zero))):
            lines.used = first

            @pl.when(s == layer)
            def _():
                self.apart = lines.put(other, far, peer)
                if sib is not None:
                    self.close = lines.put(self.half(near), sib, self.sibling)

        lines.used = first
        self.apart = lines.make(zero, far, peer)
        if sib is not None:
            self.close = lines.make(sib, sib, self.sibling)

    def half(self, ref):
        return ref.at[:, 1 - self.core] if len(ref.shape) == 4 else ref

    def forward(self):
        self.apart.wait_recv()
        if self.both is not None:
            self.passed = self.lines.put(self.half(self.far), self.both, self.sibling)

    def finish(self):
        self.apart.wait_send()
        if self.both is not None:
            self.close.wait()
            self.passed.wait()


def meet_peers():
    return [sibling_of(*here()), *beside_peers()]


def half_shape(a):
    return sds((a.shape[0], *a.shape[2:]) if a.ndim == 4 else a.shape, BF16)


def meet_shapes(zero):
    return [shape(a) for shape in (half_shape, lambda a: sds(a.shape, BF16), half_shape) for a in zero]


class Show:
    def __init__(self, lines, zero, one, out):
        s, c, z = here()
        first = lines.used
        for layer, (near, other) in enumerate(((zero, one), (one, zero))):
            lines.used = first

            @pl.when(s == layer)
            def _():
                lines.put(other, out.at[s], (1 - s, c, z))
                lines.keep(near, out.at[s])

        lines.used = first
        self.copy = lines.make(zero, out.at[s], (1 - s, c, z))
        self.kept = pltpu.make_async_copy(zero, out.at[s], lines.send.at[lines.used])
        lines.used += 1

    def finish(self):
        self.copy.wait()
        self.kept.wait()


def turn_kernel(count, acts, shows, *refs):
    (x_ref,), own_w, zero, one, shown, (o_ref,), full, taken, outs, (send, recv) = split_refs(
        refs, 1, count, acts, acts, 2 * shows, 1, count, 3 * acts, shows, 2
    )
    s, c, z = here()
    lines = Lines(send, recv)
    peers = [(s, flip(c, delta), z) for delta in (4, 8, 12)]
    greet(peers + (gather_peers() if count else meet_peers() if acts else []))
    copies = [lines.put(x_ref.at[peer[1] // 4], o_ref.at[c // 4], peer) for peer in peers]
    gathers = [Gather(lines, *two) for two in zip(own_w, full)]
    meets = [Meet(lines, *five) for five in zip(zero, one, *split_refs(taken, acts, acts, acts))]
    shown = [Show(lines, *shown, out) for out in outs]
    lines.keep(x_ref.at[c // 4], o_ref.at[c // 4]).wait()
    for copy in copies:
        copy.wait()
    for meet in meets:
        meet.forward()
    run_gathers(gathers)
    for work in meets + shown:
        work.finish()


def turn(x, weights=(), zero=(), one=(), show=()):
    args = [x, *weights, *zero, *one, *show]
    counts = len(weights), len(zero), len(show) // 2
    outs = [sds((4, GW, ROWS), BF16)] + full_shapes(weights) + meet_shapes(zero)
    outs += [sds((2, *a.shape), BF16) for a in show[::2]]
    res = exchange_call(functools.partial(turn_kernel, *counts), args, outs, [], next(ids), "turn")
    return res[0], *split_refs(res[1:], counts[0], 3 * counts[1], counts[2])


def meet_kernel(*refs):
    zero, one, taken, (out,), (send, recv) = split_refs(refs, 3, 3, 4, 1, 2)
    lines = Lines(send, recv)
    greet(meet_peers())
    work = [
        Meet(lines, zero[0], one[0], *taken[:3]),
        Meet(lines, zero[1], one[1], None, taken[3], None),
    ]
    shown = Show(lines, zero[2], one[2], out)
    for meet in work:
        meet.forward()
    for meet in (*work, shown):
        meet.finish()


def meet(zero, one):
    outs = meet_shapes(zero[:1]) + [sds(zero[1].shape, BF16), sds((2, *zero[2].shape), BF16)]
    return exchange_call(meet_kernel, (*zero, *one), outs, [], next(ids), "meet")


def scatter_kernel(count, *refs):
    combs, got, (send, recv) = split_refs(refs, count, count, 2)
    lines = Lines(send, recv)
    greet(z_peers())
    for work in [Scatter(lines, *two) for two in zip(combs, got)]:
        work.finish()


def scatter(combs):
    kernel = functools.partial(scatter_kernel, len(combs))
    return exchange_call(kernel, combs, scatter_shapes(combs), [], next(ids), "scatter")


def return_kernel(count, *refs):
    (dq_ref, dkv_ref), combs, (dqo_ref, sums_ref), got, (send, recv, mine, theirs, total) = split_refs(
        refs, 2, count, 2, count, 5
    )
    s, c, z = here()
    lines = Lines(send, recv)
    core = lax.rem(c, 2)
    sibling = sibling_of(s, c, z)
    peers = {delta: (s, flip(c, delta), z) for delta in range(2, CTX, 2)}
    greet([sibling, *peers.values(), *(z_peers() if count else [])])
    passed = [lines.put(dkv_ref.at[2 * i + 1 - core], theirs.at[i], sibling) for i in range(8)]
    loads = [lines.keep(dkv_ref.at[2 * i + core], mine.at[i]) for i in range(8)]
    sends = [
        lines.put(dq_ref.at[peers[delta][1] // 4], dqo_ref.at[c // 4], peers[delta]) for delta in (4, 8, 12)
    ]
    scatters = [Scatter(lines, *two) for two in zip(combs, got)]
    kept = [lines.keep(dq_ref.at[c // 4], dqo_ref.at[c // 4])]
    for i in range(8):
        loads[i].wait()
        passed[i].wait()
        total[i] = (mine[i].astype(F32) + theirs[i].astype(F32)).astype(BF16)
    for delta in (14, 10, 12, 8, 6, 4, 2):
        sends.append(lines.put(total.at[peers[delta][1] // 2], sums_ref.at[c // 2], peers[delta]))
    kept.append(lines.keep(total.at[c // 2], sums_ref.at[c // 2]))
    for copy in kept + sends:
        copy.wait()
    for work in scatters:
        work.finish()


def give_back(dq, dkv, combs):
    block = pltpu.VMEM((8, 2 * GW, ROWS), BF16)
    outs = [sds((4, GW, ROWS), BF16), sds((8, 2 * GW, ROWS), BF16)] + scatter_shapes(combs)
    kernel = functools.partial(return_kernel, len(combs))
    res = exchange_call(kernel, [dq, dkv, *combs], outs, [block] * 3, next(ids), "give_back")
    return res[0], res[1], res[2:]


QUARTER = SUM_ROWS // 4


def finish_kernel(comb_m, got_m, comb_q, got_q, fin, send, recv, load, terms, own_sum, parts, red):
    s, c, z = here()
    lines = Lines(send, recv)
    core = lax.rem(c, 2)
    sibling = sibling_of(s, c, z)
    near = {delta: (s, flip(c, delta), z) for delta in range(2, CTX, 2)}
    loads = []
    for part, (comb, got, at, rows) in enumerate(
        ((comb_m, got_m, 0, MLP_ROWS), (comb_q, got_q, MLP_ROWS, QKV_ROWS))
    ):
        rows = pl.ds(at, rows)
        loads.append(fetch(comb.at[z], terms.at[0, rows], load.at[4 * part]))
        loads += [fetch(got.at[i], terms.at[i + 1, rows], load.at[4 * part + i + 1]) for i in range(3)]
    greet([sibling, *near.values()])
    for copy in loads:
        copy.wait()
    for at in range(0, SUM_ROWS, 128):
        rows = slice(at, at + 128)
        both = terms[0, rows].astype(F32) + terms[1, rows].astype(F32)
        both += terms[2, rows].astype(F32) + terms[3, rows].astype(F32)
        own_sum[rows] = both.astype(BF16)

    def block(at):
        rows = pl.ds(pl.multiple_of(lax.rem(at // 2, 4) * QUARTER, 16), QUARTER)
        return rows, pl.ds(pl.multiple_of(at // 8 * (D // 2), 128), D // 2)

    order = [14, 10, 12, 8, 6, 4, 2]
    sends = [lines.put(own_sum.at[block(near[delta][1])], parts.at[c // 2], near[delta]) for delta in order]
    lines.keep(own_sum.at[block(c)], parts.at[c // 2]).wait()
    for copy in sends:
        copy.wait()
    for at in range(0, QUARTER, 112):
        rows = slice(at, at + 112)
        total = parts[0, rows].astype(F32)
        for i in range(1, 8):
            total += parts[i, rows].astype(F32)
        red[rows] = total.astype(BF16)
    target = fin.at[core]
    kept = lines.keep(red, target.at[block(c)])
    passed = [lines.put(red, target.at[block(c)], sibling)]
    shown = {delta: lines.put(red, target.at[block(c)], near[delta]) for delta in order}
    for delta in reversed(order):
        shown[delta].wait_recv()
        piece = target.at[block(flip(c, delta))]
        passed.append(lines.put(piece, piece, sibling))
    kept.wait()
    for copy in shown.values():
        copy.wait_send()
    for copy in passed:
        copy.wait()


def finish(*args):
    scratch = [
        DMA((8,)),
        pltpu.VMEM((4, SUM_ROWS, D), BF16),
        pltpu.VMEM((SUM_ROWS, D), BF16),
        pltpu.VMEM((8, QUARTER, D // 2), BF16),
        pltpu.VMEM((QUARTER, D // 2), BF16),
    ]
    return exchange_call(
        finish_kernel, args, sds((2, SUM_ROWS, D), BF16), scratch, next(ids), "finish"
    )


def rope_tables():
    positions = (lax.axis_index("ctx") * ROWS + lax.iota(jnp.int32, ROWS)).astype(F32)
    frequency = 1.0 / 160000.0 ** (jnp.arange(HEAD_DIM // 2, dtype=F32) * 2.0 / HEAD_DIM)
    angles = frequency[:, None] * positions[None, :]
    return jnp.cos(angles), jnp.sin(angles)


def weight_scratch(*shapes):
    return [pltpu.VMEM(shape, BF16) for shape in shapes]


def forward_layer(layer, x, gains, w_qkv, late, tables):
    qkv, normed = compute_call(
        functools.partial(qkv_kernel, layer),
        (x, gains[0], *tables, w_qkv),
        (sds((4, 3 * GW, ROWS), BF16), sds((D, ROWS), BF16)),
        [*weight_scratch((D, 3 * D)), DMA],
        name="norm_qkv",
        far=1,
    )
    q, kv, w_up = spread(qkv, late[1:2] if layer == 0 else [])
    low, wide, totals = compute_call(
        attend_kernel,
        (q, kv),
        (sds((4, GW, ROWS), BF16), sds((4, GW, ROWS), F32), sds((GH, 8, 512), F32)),
        [pltpu.VMEM((2048, 512), F32)],
        name="attend",
    )
    ot, w_rest, _, _ = turn(low, late[::2] if layer == 0 else [])
    if layer == 0:
        late = [w.reshape(2, -1, w.shape[-1]) for w in (w_rest[0], w_up[0], w_rest[1])]
    ot = ot.reshape(D, ROWS)
    out, hidden, gate_up, normed_two, product = compute_call(
        functools.partial(mlp_kernel, layer),
        (ot, x, gains[1], *late),
        (sds((ROWS, D), BF16), sds((ROWS, D), F32), sds((ROWS, 2 * FF), F32),
         sds((D, ROWS), BF16), sds((FF, ROWS), BF16)),
        [*weight_scratch((D, D), (D, 2 * FF), (FF, D)), DMA((3,))],
        name="mlp",
        far=3,
    )
    lefts = [by_core(a) for a in (normed_two, product, ot, normed)]
    return out, late, lefts, (x, q, kv, wide, totals, hidden, gate_up)


def by_core(a):
    return a.reshape(4, 2, -1, ROWS)


def mlp_back(layer, grad, stored, gains, late):
    hidden, gate_up = stored[5:]
    return compute_call(
        functools.partial(mlp_back_kernel, layer),
        (grad, hidden, gate_up, gains[1], *late),
        (sds((D, ROWS), BF16), sds((ROWS, D), F32), sds((ROWS, 2 * FF), BF16),
         sds((ROWS, D), BF16), sds((1, D), F32)),
        [*weight_scratch((D, D), (D, 2 * FF), (FF, D)), DMA((3,))],
        name="mlp_back",
        far=3,
    )


def attend_back(d_o, stored):
    _, q, kv, wide, totals = stored[:5]
    return compute_call(
        attend_back_kernel,
        (q, kv, wide, totals, d_o),
        (sds((4, GW, ROWS), BF16), sds((CTX, 2 * GW, ROWS), BF16)),
        name="attend_back",
    )


def qkv_back(layer, dq, dkv, stored, gains, tables, grad_hidden, d_gain_two, w_qkv):
    return compute_call(
        functools.partial(qkv_back_kernel, layer),
        (dq, dkv, stored[0], gains[0], *tables, grad_hidden, d_gain_two, w_qkv),
        (sds((ROWS, D), BF16), sds((ROWS, 3 * D), BF16), sds((16, D), BF16)),
        [pltpu.VMEM((3 * D, ROWS), F32), *weight_scratch((D, 3 * D)), DMA],
        name="qkv_back",
        far=1,
    )


def local(inputs, cotangent, attn_gain, qkv_weight, out_weight, mlp_gain, up_weight, down_weight):
    first = lax.axis_index("section") == 0
    x = jnp.where(first, inputs[0, 0], inputs[1, 0])
    cot = jnp.where(first, cotangent[0, 0], cotangent[1, 0])
    gain = jnp.pad(jnp.concatenate([attn_gain, mlp_gain], axis=0), ((0, 14), (0, 64)))
    w_qkv, gains = start(qkv_weight[0], gain)
    w_qkv = w_qkv.reshape(2, D, 3 * D)
    gains = [
        [gains[layer, :, row, :192].reshape(1, D) for row in range(2)] for layer in range(2)
    ]
    tables = rope_tables()
    late = [out_weight[0], up_weight[0], down_weight[0]]
    mid, late, left_zero, kept_zero = forward_layer(0, x, gains[0], w_qkv, late, tables)
    end, _, left_one, kept_one = forward_layer(1, mid, gains[1], w_qkv, late, tables)

    d_ot, grad_hidden, gg_one, branch_one, d_gain = mlp_back(1, cot, kept_one, gains[1], late)
    d_o, _, lefts, (activations,) = turn(
        d_ot.reshape(4, GW, ROWS), zero=left_zero, one=left_one, show=(mid, end)
    )
    dq, dkv = attend_back(d_o, kept_one)
    dq, dkv, _ = give_back(dq, dkv, [])
    grad_mid, gp_one, gains_one = qkv_back(
        1, dq, dkv, kept_one, gains[1], tables, grad_hidden, d_gain, w_qkv
    )

    d_ot, grad_hidden, gg_zero, branch_zero, d_gain = mlp_back(0, grad_mid, kept_zero, gains[0], late)
    rights_zero, rights_one = [gg_zero, grad_mid, branch_zero], [gg_one, cot, branch_one]
    d_o, _, rights, _ = turn(d_ot.reshape(4, GW, ROWS), zero=rights_zero, one=rights_one)
    mlp_lefts = [lefts[4 * i + j] for i in range(3) for j in range(3)]
    heights = (96, 144, 96)
    comb_mlp = compute_call(
        mlp_weights_kernel,
        (*left_zero[:3], *rights_zero, *left_one[:3], *rights_one, *mlp_lefts, *rights),
        sds((4, MLP_ROWS, D), BF16),
        [
            pltpu.VMEM(shape, BF16)
            for height, right in zip(heights, rights_zero)
            for shape in ((4, height, 4 * ROWS), (4 * ROWS, right.shape[1]))
        ]
        + [DMA((3, 8))],
        name="mlp_weights",
        far=30,
    )
    dq, dkv = attend_back(d_o, kept_zero)
    dq, dkv, (got_mlp,) = give_back(dq, dkv, [comb_mlp])
    grad_start, gp_zero, gains_zero = qkv_back(
        0, dq, dkv, kept_zero, gains[0], tables, grad_hidden, d_gain, w_qkv
    )
    *gp_rest, gains_far, input_grads = meet(
        (gp_zero, gains_zero, grad_start), (gp_one, gains_one, grad_mid)
    )
    comb_qkv = compute_call(
        qkv_weights_kernel,
        (gains_far, left_zero[3], gp_zero, gains_zero, left_one[3], gp_one, gains_one,
         *lefts[3::4], *gp_rest),
        sds((4, QKV_ROWS, D), BF16),
        [*weight_scratch((4, 96, 4 * ROWS), (4 * ROWS, 3 * D), (16, D)), DMA((9,))],
        name="qkv_weights",
        far=12,
    )
    (got_qkv,) = scatter([comb_qkv])
    fin = finish(comb_mlp, got_mlp, comb_qkv, got_qkv)
    grad_up, grad_out, grad_down, grad_qkv, gain_sums = compute_call(
        assemble_kernel,
        (fin,),
        [sds(shape, F32) for shape in ((192, 3 * D), (192, D), (288, D), (192, 3 * D), (16, D))],
        name="assemble",
    )
    gain_sums = lax.dynamic_slice_in_dim(gain_sums[:2], lax.axis_index("wshard") * 192, 192, 1)
    return (
        activations[None, :, None],
        input_grads[None, :, None],
        gain_sums[0:1],
        grad_qkv[None],
        grad_out[None],
        gain_sums[1:2],
        grad_up[None],
        grad_down[None],
    )


def solution(mesh):
    global ids
    ids = iter(range(1, 64))
    placed = (
        P(None, "wshard", "ctx", None),
        P(None, "wshard", "ctx", None),
        P("section", "wshard"),
        P("section", "wshard", None),
        P("section", "wshard", None),
        P("section", "wshard"),
        P("section", "wshard", None),
        P("section", "wshard", None),
    )
    return jax.shard_map(
        local,
        mesh=mesh,
        in_specs=placed,
        out_specs=(
            P("section", None, "wshard", "ctx", None),
            P("section", None, "wshard", "ctx", None),
            P("section", "wshard"),
            P("section", "wshard", None),
            P("section", "wshard", None),
            P("section", "wshard"),
            P("section", "wshard", None),
            P("section", "wshard", None),
        ),
        check_vma=False,
    )
```

time: 547 us -> 470 us (0.86)
  Pallas kernels: 512 us -> 455 us
  local copies, waits for them, and re-layouts: 21.2 us -> 6.42 us
    pallas_call x13 -> x12, Pallas kernels: 400 us -> 341 us  [exchange_call(): pl.pallas_call(kernel, out_shape=outs, in_specs=[ANY] * len(args), out_sp...]
    slice x4 -> x1, local copies, waits for them, and re-layouts: 6.77 us -> 0.74 us  [local(): gain_sums[:2]]
    pallas_call x16 -> x15, Pallas kernels: 112 us -> 113 us  [compute_call(): pl.pallas_call(kernel, out_shape=outs, in_specs=[VM] * (len(args) - far)...]
  transfers between devices with their start and end apart: 2 -> 0, of which waited for: 0 -> 0; matrix products, arithmetic and copies ran while one was open for 4% -> 0% of each run, Pallas kernels for 57% -> 0%
where the time goes in v3:
time: 470 us; the launch traced here: 466 us
  Pallas kernels  455 us (97%)
  local copies, waits for them, and re-layouts  6.42 us (1%)
    pallas_call x12, Pallas kernels, exchange_call(): pl.pallas_call(kernel, out_shape=outs, in_specs=[ANY] * len(args), out_sp...  341 us
    pallas_call x15, Pallas kernels, compute_call(): pl.pallas_call(kernel, out_shape=outs, in_specs=[VM] * (len(args) - far)...  113 us

profile of v3, /device:TPU:25, one launch (start us, length us, event | category | flops | bytes accessed | tf_op | source)
XLA Modules:
  0.0 466.2 jit_solution(13300072660425729484)
XLA Ops:
  0.6 2.0 select_bitcast_fusion
  2.7 1.3 fusion.5.refs_1_
  4.0 36.9 %start.1 = (bf16[2,4,192,2304]{3,2,1,0:T(8,128)(2,1)}, bf16[2,4,16,256]{3,2,1,0:T(8,128)(2,1)}) custom-call(bf16[192,2304]{1,0:T(8,128)(2,1)} %bitcast.60, bf16[16,256]{1,0:T(8,128)(2,1)} %fusion.5.refs_1_), custom_call_target="tpu_custom_call" | custom-call | tf_op jit(solution)/shard_map/start/pallas_call | solution.py:436
  40.9 0.8 slice_reduce_fusion
  42.4 0.8 multiply_sine_fusion
  43.2 4.5 norm_qkv.2
  47.7 42.7 %spread.2 = (bf16[4,192,128]{2,1,0:T(8,128)(2,1)}, bf16[16,384,128]{2,1,0:T(8,128)(2,1)}, bf16[2,4,192,2304]{3,2,1,0:T(8,128)(2,1)}) custom-call(bf16[4,576,128]{2,1,0:T(8,128)(2,1)} %get-tuple-element.99.refs_0_, bf16[192,2304]{1,0:T(8,128)(2,1)} %bitcast.61), custom_call_target="tpu_custom_call" | custom-call | tf_op jit(solution)/shard_map/spread/pallas_call | solution.py:436
  90.4 7.9 %attend.2 = (bf16[4,192,128]{2,1,0:T(8,128)(2,1)}, f32[4,192,128]{2,1,0:T(8,128)}, f32[3,8,512]{2,1,0:T(8,128)}) custom-call(bf16[4,192,128]{2,1,0:T(8,128)(2,1)} %get-tuple-element.100.q_ref, bf16[16,384,128]{2,1,0:T(8,128)(2,1)} %get-tuple-element.101.kv_ref), custom_call_target="tpu_custom_call" | custom-call | tf_op jit(solution)/shard_map/attend/pallas_call | solution.py:42
  98.2 34.9 %turn.4 = (bf16[4,192,128]{2,1,0:T(8,128)(2,1)}, bf16[2,4,192,768]{3,2,1,0:T(8,128)(2,1)}, bf16[2,4,288,768]{3,2,1,0:T(8,128)(2,1)}) custom-call(bf16[4,192,128]{2,1,0:T(8,128)(2,1)} %get-tuple-element.102.refs_0_, bf16[192,768]{1,0:T(8,128)(2,1)} %bitcast.73, bf16[288,768]{1,0:T(8,128)(2,1)} %bitcast.70), custom_call_target="tpu_custom_call" | custom-call | tf_op jit(solution)/shard_map/turn/pallas_call | solution.py:436
  133.8 5.5 %mlp.2 = (bf16[128,768]{1,0:T(8,128)(2,1)}, f32[128,768]{1,0:T(8,128)}, f32[128,2304]{1,0:T(8,128)}, bf16[768,128]{1,0:T(8,128)(2,1)}, bf16[1152,128]{1,0:T(8,128)(2,1)}) custom-call(bf16[768,128]{1,0:T(8,128)(2,1)} %bitcast.53, bf16[128,768]{1,0:T(8,128)(2,1)} %get-tuple-element.210.x_ref, bf16[1,768]{1,0:T(2,128)(2,1)} %reshape_squeeze.13.gain_ref, ...), custom_call_target="tpu_custom_call" | custom-call | tf_op jit(solution)/shard_map/mlp/pallas_call | solution.py:42
  140.0 4.5 norm_qkv.3
  144.5 20.2 %spread.3 = (bf16[4,192,128]{2,1,0:T(8,128)(2,1)}, bf16[16,384,128]{2,1,0:T(8,128)(2,1)}) custom-call(bf16[4,576,128]{2,1,0:T(8,128)(2,1)} %get-tuple-element.108.refs_0_), custom_call_target="tpu_custom_call" | custom-call | tf_op jit(solution)/shard_map/spread/pallas_call | solution.py:436
  164.8 8.0 %attend.3 = (bf16[4,192,128]{2,1,0:T(8,128)(2,1)}, f32[4,192,128]{2,1,0:T(8,128)}, f32[3,8,512]{2,1,0:T(8,128)}) custom-call(bf16[4,192,128]{2,1,0:T(8,128)(2,1)} %get-tuple-element.109.q_ref, bf16[16,384,128]{2,1,0:T(8,128)(2,1)} %get-tuple-element.110.kv_ref), custom_call_target="tpu_custom_call" | custom-call | tf_op jit(solution)/shard_map/attend/pallas_call | solution.py:42
  172.8 10.2 %turn.5 = bf16[4,192,128]{2,1,0:T(8,128)(2,1)} custom-call(bf16[4,192,128]{2,1,0:T(8,128)(2,1)} %get-tuple-element.111.refs_0_), custom_call_target="tpu_custom_call" | custom-call | tf_op jit(solution)/shard_map/turn/pallas_call | solution.py:436
  183.7 5.5 %mlp.3 = (bf16[128,768]{1,0:T(8,128)(2,1)}, f32[128,768]{1,0:T(8,128)}, f32[128,2304]{1,0:T(8,128)}, bf16[768,128]{1,0:T(8,128)(2,1)}, bf16[1152,128]{1,0:T(8,128)(2,1)}) custom-call(bf16[768,128]{1,0:T(8,128)(2,1)} %bitcast.50, bf16[128,768]{1,0:T(8,128)(2,1)} %get-tuple-element.107.x_ref.refs_9_, bf16[1,768]{1,0:T(2,128)(2,1)} %reshape_squeeze.15.gain_ref, ...), custom_call_target="tpu_custom_call" | custom-call | tf_op jit(solution)/shard_map/mlp/pallas_call | solution.py:42
  189.2 7.2 %mlp_back.2 = (bf16[768,128]{1,0:T(8,128)(2,1)}, f32[128,768]{1,0:T(8,128)}, bf16[128,2304]{1,0:T(8,128)(2,1)}, bf16[128,768]{1,0:T(8,128)(2,1)}, f32[1,768]{1,0:T(1,128)}) custom-call(bf16[128,768]{1,0:T(8,128)(2,1)} %get-tuple-element.211.g_ref.refs_5_.refs_10_, f32[128,768]{1,0:T(8,128)} %get-tuple-element.112.hidden_ref, ...), custom_call_target="tpu_custom_call" | custom-call | tf_op jit(solution)/shard_map/mlp_back/pallas_call | solution.py:42
  196.5 23.4 %turn.6 = (bf16[4,192,128]{2,1,0:T(8,128)(2,1)}, bf16[4,96,128]{2,1,0:T(8,128)(2,1)}, bf16[4,144,128]{2,1,0:T(8,128)(2,1)}, bf16[4,96,128]{2,1,0:T(8,128)(2,1)},...) custom-call(bf16[4,192,128]{2,1,0:T(8,128)(2,1)} %bitcast.74, ...), custom_call_target="tpu_custom_call" | custom-call | tf_op jit(solution)/shard_map/turn/pallas_call | solution.py:436
  219.9 16.6 %attend_back.2 = (bf16[4,192,128]{2,1,0:T(8,128)(2,1)}, bf16[16,384,128]{2,1,0:T(8,128)(2,1)}) custom-call(bf16[4,192,128]{2,1,0:T(8,128)(2,1)} %get-tuple-element.109.q_ref, bf16[16,384,128]{2,1,0:T(8,128)(2,1)} %get-tuple-element.110.kv_ref, f32[4,192,128]{2,1,0:T(8,128)} %get-tuple-element.125.wide_ref, f32[3,8,512]{2,1,0:T(8,128)} %get-tuple-element.126.totals_ref, ...), custom_call_target="tpu_custom_call" | custom-call | tf_op jit(solution)/shard_map/attend_back/pallas_call | solution.py:42
  236.5 20.0 %give_back.2 = (bf16[4,192,128]{2,1,0:T(8,128)(2,1)}, bf16[8,384,128]{2,1,0:T(8,128)(2,1)}) custom-call(bf16[4,192,128]{2,1,0:T(8,128)(2,1)} %get-tuple-element.128.refs_0_, bf16[16,384,128]{2,1,0:T(8,128)(2,1)} %get-tuple-element.129.refs_1_), custom_call_target="tpu_custom_call" | custom-call | tf_op jit(solution)/shard_map/give_back/pallas_call | solution.py:436
  256.5 5.6 %qkv_back.2 = (bf16[128,768]{1,0:T(8,128)(2,1)}, bf16[128,2304]{1,0:T(8,128)(2,1)}, bf16[16,768]{1,0:T(8,128)(2,1)}) custom-call(bf16[4,192,128]{2,1,0:T(8,128)(2,1)} %get-tuple-element.130.dq_ref, bf16[8,384,128]{2,1,0:T(8,128)(2,1)} %get-tuple-element.131.dkv_ref, bf16[128,768]{1,0:T(8,128)(2,1)} %get-tuple-element.107.x_ref.refs_9_, ...), custom_call_target="tpu_custom_call" | custom-call | tf_op jit(solution)/shard_map/qkv_back/pallas_call | solution.py:42
  262.1 7.2 %mlp_back.3 = (bf16[768,128]{1,0:T(8,128)(2,1)}, f32[128,768]{1,0:T(8,128)}, bf16[128,2304]{1,0:T(8,128)(2,1)}, bf16[128,768]{1,0:T(8,128)(2,1)}, f32[1,768]{1,0:T(1,128)}) custom-call(bf16[128,768]{1,0:T(8,128)(2,1)} %get-tuple-element.134.g_ref.refs_2_.refs_4_.refs_5_, f32[128,768]{1,0:T(8,128)} %get-tuple-element.135.hidden_ref, ...), custom_call_target="tpu_custom_call" | custom-call | tf_op jit(solution)/shard_map/mlp_back/pallas_call | solution.py:42
  269.4 21.7 %turn.7 = (bf16[4,192,128]{2,1,0:T(8,128)(2,1)}, bf16[128,2304]{1,0:T(8,128)(2,1)}, bf16[128,768]{1,0:T(8,128)(2,1)}, bf16[128,768]{1,0:T(8,128)(2,1)}, bf16[128...) custom-call(bf16[4,192,128]{2,1,0:T(8,128)(2,1)} %bitcast.75, ...), custom_call_target="tpu_custom_call" | custom-call | tf_op jit(solution)/shard_map/turn/pallas_call | solution.py:436
  291.0 16.6 %attend_back.3 = (bf16[4,192,128]{2,1,0:T(8,128)(2,1)}, bf16[16,384,128]{2,1,0:T(8,128)(2,1)}) custom-call(bf16[4,192,128]{2,1,0:T(8,128)(2,1)} %get-tuple-element.100.q_ref, bf16[16,384,128]{2,1,0:T(8,128)(2,1)} %get-tuple-element.101.kv_ref, f32[4,192,128]{2,1,0:T(8,128)} %get-tuple-element.123.wide_ref, f32[3,8,512]{2,1,0:T(8,128)} %get-tuple-element.124.totals_ref, ...), custom_call_target="tpu_custom_call" | custom-call | tf_op jit(solution)/shard_map/attend_back/pallas_call | solution.py:42
  307.7 8.4 %mlp_weights.1.refs_2_.comb_m = bf16[4,576,768]{2,1,0:T(8,128)(2,1)} custom-call(bf16[4,2,96,128]{3,2,1,0:T(8,128)(2,1)} %bitcast.67, bf16[4,2,144,128]{3,2,1,0:T(8,128)(2,1)} %bitcast.57, bf16[4,2,96,128]{3,2,1,0:T(8,128)(2,1)} %bitcast.55, bf16[128,2304]{1,0:T(8,128)(2,1)} %get-tuple-element.138.refs_1_.refs_3_, ...), custom_call_target="tpu_custom_call" | custom-call | tf_op jit(solution)/shard_map/mlp_weights/pallas_call | solution.py:42
  316.1 45.6 %give_back.3 = (bf16[4,192,128]{2,1,0:T(8,128)(2,1)}, bf16[8,384,128]{2,1,0:T(8,128)(2,1)}, bf16[3,576,768]{2,1,0:T(8,128)(2,1)}) custom-call(bf16[4,192,128]{2,1,0:T(8,128)(2,1)} %get-tuple-element.143.refs_0_, bf16[16,384,128]{2,1,0:T(8,128)(2,1)} %get-tuple-element.144.refs_1_, bf16[4,576,768]{2,1,0:T(8,128)(2,1)} %mlp_weights.1.refs_2_.comb_m), custom_call_target="tpu_custom_call" | custom-call | tf_op jit(solution)/shard_map/give_back/pallas_call | solution.py:436
  361.7 5.6 %qkv_back.3 = (bf16[128,768]{1,0:T(8,128)(2,1)}, bf16[128,2304]{1,0:T(8,128)(2,1)}, bf16[16,768]{1,0:T(8,128)(2,1)}) custom-call(bf16[4,192,128]{2,1,0:T(8,128)(2,1)} %get-tuple-element.163.dq_ref, bf16[8,384,128]{2,1,0:T(8,128)(2,1)} %get-tuple-element.164.dkv_ref, bf16[128,768]{1,0:T(8,128)(2,1)} %get-tuple-element.210.x_ref, ...), custom_call_target="tpu_custom_call" | custom-call | tf_op jit(solution)/shard_map/qkv_back/pallas_call | solution.py:42
  367.2 15.8 %meet.1 = (bf16[128,2304]{1,0:T(8,128)(2,1)}, bf16[128,2304]{1,0:T(8,128)(2,1)}, bf16[128,2304]{1,0:T(8,128)(2,1)}, bf16[16,768]{1,0:T(8,128)(2,1)}, bf16[2,128,768]{2,1,0:T(8,128)(2,1)}) custom-call(bf16[128,2304]{1,0:T(8,128)(2,1)} %get-tuple-element.167.refs_0_.refs_2_, bf16[16,768]{1,0:T(8,128)(2,1)} %get-tuple-element.168.refs_1_.refs_3_, ...), custom_call_target="tpu_custom_call" | custom-call | tf_op jit(solution)/shard_map/meet/pallas_call | solution.py:436
  383.0 5.9 %qkv_weights.1.refs_0_.comb_q = bf16[4,320,768]{2,1,0:T(8,128)(2,1)} custom-call(bf16[16,768]{1,0:T(8,128)(2,1)} %get-tuple-element.174.refs_0_, bf16[4,2,96,128]{3,2,1,0:T(8,128)(2,1)} %bitcast.63, bf16[128,2304]{1,0:T(8,128)(2,1)} %get-tuple-element.167.refs_0_.refs_2_, bf16[16,768]{1,0:T(8,128)(2,1)} %get-tuple-element.168.refs_1_.refs_3_, ...), custom_call_target="tpu_custom_call" | custom-call | tf_op jit(solution)/shard_map/qkv_weights/pallas_call | solution.py:42
  389.0 26.8 %scatter.1.got_q = bf16[3,320,768]{2,1,0:T(8,128)(2,1)} custom-call(bf16[4,320,768]{2,1,0:T(8,128)(2,1)} %qkv_weights.1.refs_0_.comb_q), custom_call_target="tpu_custom_call" | custom-call | tf_op jit(solution)/shard_map/scatter/pallas_call | solution.py:436
  415.7 43.3 %finish.1.fin_ref = bf16[2,896,768]{2,1,0:T(8,128)(2,1)} custom-call(bf16[4,576,768]{2,1,0:T(8,128)(2,1)} %mlp_weights.1.refs_2_.comb_m, bf16[3,576,768]{2,1,0:T(8,128)(2,1)} %get-tuple-element.173.got_m, bf16[4,320,768]{2,1,0:T(8,128)(2,1)} %qkv_weights.1.refs_0_.comb_q, bf16[3,320,768]{2,1,0:T(8,128)(2,1)} %scatter.1.got_q), custom_call_target="tpu_custom_call" | custom-call | tf_op jit(solution)/shard_map/finish/pallas_call | solution.py:436
  459.1 4.3 assemble.1
  464.7 0.7 copy.22
  (13 shorter events, 4.8 us)
Async XLA Ops:
  459.0 5.7 %copy-start = (bf16[2,128,768]{2,1,0:T(8,128)(2,1)S(1)}, bf16[2,128,768]{2,1,0:T(8,128)(2,1)}, u32[]{:S(2)}) copy-start(bf16[2,128,768]{2,1,0:T(8,128)(2,1)} %get-tuple-element.122) | copy-start | bytes 1179652
  459.0 6.4 %copy-start.1 = (bf16[2,128,768]{2,1,0:T(8,128)(2,1)S(1)}, bf16[2,128,768]{2,1,0:T(8,128)(2,1)}, u32[]{:S(2)}) copy-start(bf16[2,128,768]{2,1,0:T(8,128)(2,1)} %get-tuple-element.172) | copy-start | bytes 1179652

commit v4 on v3

--- a/solution.py
+++ b/solution.py
@@ -84,12 +84,11 @@
     return out
 
 
-def qkv_kernel(layer, x_ref, gain_ref, cos_ref, sin_ref, w_all, qkv_ref, normed_ref, w_ref, sem):
-    load = fetch(w_all.at[layer], w_ref, sem)
+def project(x_ref, gain, cos_ref, sin_ref, w_ref, loaded, qkv_ref, normed_ref):
     normalized, _ = norm_parts(x_ref[...].astype(F32))
-    normed = (normalized * gain_ref[...].astype(F32)).astype(BF16)
+    normed = (normalized * gain).astype(BF16)
     normed_ref[...] = turned_low(normed)
-    load.wait()
+    loaded()
     cos = cos_ref[...]
     sin = sin_ref[...]
     for part in range(3):
@@ -114,7 +113,7 @@
 PAIR = CHUNK // ROWS
 
 
-def attend_kernel(q_ref, kv_ref, low_ref, wide_ref, totals_ref, s_ref):
+def attend(q_ref, kv_ref, low_ref, wide_ref, totals_ref, s_ref):
     @pl.loop(0, GH)
     def _(h):
         at = pl.multiple_of(h * HEAD_DIM, HEAD_DIM)
@@ -185,29 +184,25 @@
             dq_ref[i, pl.ds(at, HEAD_DIM), :] = acc[:, i * ROWS : (i + 1) * ROWS].astype(BF16)
 
 
-def mlp_kernel(
-    layer, ot_ref, x_ref, gain_ref, wo_all, wu_all, wd_all,
-    out_ref, hidden_ref, gate_up_ref, normed_ref, product_ref, wo_ref, wu_ref, wd_ref, sem,
+def mlp(
+    ot_ref, x_ref, gain, wo_ref, wu_ref, wd_ref, loaded,
+    out_ref, hidden_ref, gate_up_ref, normed_ref, product_ref,
 ):
-    loads = [
-        fetch(src.at[layer], dst, sem.at[i])
-        for i, (src, dst) in enumerate([(wo_all, wo_ref), (wu_all, wu_ref), (wd_all, wd_ref)])
-    ]
-    attended = turned_low(ot_ref[...])
-    loads[0].wait()
+    attended = turned_low(ot_ref[...].reshape(D, ROWS))
+    loaded(0)
     hidden = x_ref[...].astype(F32) + dot(attended, wo_ref[...])
     hidden_ref[...] = hidden
     normalized, _ = norm_parts(hidden)
-    normed = (normalized * gain_ref[...].astype(F32)).astype(BF16)
+    normed = (normalized * gain).astype(BF16)
     normed_ref[...] = turned_low(normed)
-    loads[1].wait()
+    loaded(1)
     gate_up = dot(normed, wu_ref[...])
     gate_up_ref[...] = gate_up
     gate = gate_up[:, :FF]
     phi = 0.5 * (1.0 + lax.erf(gate * 0.5**0.5))
     product = (gate * phi * gate_up[:, FF:]).astype(BF16)
     product_ref[...] = turned_low(product)
-    loads[2].wait()
+    loaded(2)
     out_ref[...] = (hidden + dot(product, wd_ref[...])).astype(BF16)
 
 
@@ -565,70 +560,178 @@
     return [sds((3, *comb.shape[1:]), BF16) for comb in combs]
 
 
-def start_kernel(*refs):
-    own, gain, full, gains, send, recv = refs
+def shard_loads(full, layer, dst, sems):
+    rows = full.shape[2]
+    return [
+        pltpu.make_async_copy(full.at[layer, i], dst.at[pl.ds(i * rows, rows)], sems.at[i])
+        for i in range(4)
+    ]
+
+
+class Spread:
+    order = [14, 10, 12, 8, 6, 4, 2]
+
+    def __init__(self, lines, qkv_ref, q_ref, kv_ref):
+        s, c, z = here()
+        self.lines, self.kv_ref = lines, kv_ref
+        self.sibling = sibling_of(s, c, z)
+        kv_rows = pl.ds(GW, 2 * GW)
+        q_rows = pl.ds(0, GW)
+        self.kv_sends, self.q_sends = {}, []
+        for delta in self.order:
+            peer = (s, flip(c, delta), z)
+            self.kv_sends[delta] = lines.put(qkv_ref.at[peer[1] // 4, kv_rows], kv_ref.at[c], peer)
+            if delta % 4 == 0:
+                self.q_sends.append(lines.put(qkv_ref.at[peer[1] // 4, q_rows], q_ref.at[c // 4], peer))
+        self.passed = [lines.put(qkv_ref.at[c // 4, kv_rows], kv_ref.at[c], self.sibling)]
+        self.kept = [
+            lines.keep(qkv_ref.at[c // 4, kv_rows], kv_ref.at[c]),
+            lines.keep(qkv_ref.at[c // 4, q_rows], q_ref.at[c // 4]),
+        ]
+
+    def finish(self):
+        _, c, _ = here()
+        for delta in reversed(self.order):
+            self.kv_sends[delta].wait_recv()
+            block = self.kv_ref.at[flip(c, delta)]
+            self.passed.append(self.lines.put(block, block, self.sibling))
+        for copy in self.kept + self.q_sends + self.passed:
+            copy.wait()
+        for copy in self.kv_sends.values():
+            copy.wait_send()
+
+
+class Turn:
+    def __init__(self, lines, x_ref, o_ref):
+        s, c, z = here()
+        peers = [(s, flip(c, delta), z) for delta in (4, 8, 12)]
+        self.copies = [lines.put(x_ref.at[peer[1] // 4], o_ref.at[c // 4], peer) for peer in peers]
+        self.copies.append(lines.keep(x_ref.at[c // 4], o_ref.at[c // 4]))
+
+    def finish(self):
+        for copy in self.copies:
+            copy.wait()
+
+
+def forward_kernel(*refs):
+    (cos, sin, inputs, gain), own, per_layer, full, (gains,), scratch = split_refs(refs, 4, 4, 22, 4, 1, 14)
+    x_s, w_q, w_o, w_u, w_d, qkv_s, low_s, s_ref, got_gain, load_sem, in_sem, send, recv, gain_s = scratch
     s, c, z = here()
     lines = Lines(send, recv)
+    x_load = fetch(inputs.at[s, 0], x_s, in_sem.at[0])
     across = [(1 - s, c, lax.rem(z + r, 4)) for r in (1, 3, 2)]
-    greet([*gather_peers(), z_peers()[2], *across])
-    gather = Gather(lines, own, full)
-    copies = [
-        lines.put(gain, gains.at[s, z], peer) for peer in (*z_peers(), beside_peers()[0], *across)
+    ctx_peers = [(s, flip(c, delta), z) for delta in range(2, CTX, 2)]
+    greet([*gather_peers(), z_peers()[2], *across, *ctx_peers])
+
+    first = Gather(lines, own[0], full[0])
+    gain_copies = [
+        lines.put(gain, got_gain.at[s, z], peer) for peer in (*z_peers(), beside_peers()[0], *across)
     ]
-    kept = lines.keep(gain, gains.at[s, z])
-    run_gathers([gather])
-    kept.wait()
-    for copy in copies:
+    gain_copies.append(lines.keep(gain, got_gain.at[s, z]))
+    run_gathers([first])
+    rest = [Gather(lines, own[i], full[i]) for i in (2, 1, 3)]
+
+    targets = (w_q, w_o, w_u, w_d)
+    loads = [
+        [shard_loads(full[i], layer, targets[i], load_sem.at[layer, i]) for i in range(4)]
+        for layer in range(2)
+    ]
+
+    def begin(layer, which):
+        for i in which:
+            for copy in loads[layer][i]:
+                copy.start()
+
+    def loaded(layer, i):
+        for copy in loads[layer][i]:
+            copy.wait()
+
+    begin(0, [0])
+    for copy in gain_copies:
         copy.wait()
-
-
-def start(weight, gain):
-    outs = (*full_shapes([weight]), sds((2, 4, *gain.shape), BF16))
-    return exchange_call(start_kernel, (weight, gain), outs, [], next(ids), "start")
-
-
-def spread_kernel(count, *refs):
-    (qkv_ref,), own_w, (q_ref, kv_ref), full, (send, recv) = split_refs(refs, 1, count, 2, count, 2)
-    s, c, z = here()
-    lines = Lines(send, recv)
-    sibling = sibling_of(s, c, z)
-    peers = {delta: (s, flip(c, delta), z) for delta in range(2, CTX, 2)}
-    greet([sibling, *peers.values(), *(gather_peers()[1:] if count else [])])
-    kv_rows = pl.ds(GW, 2 * GW)
-    q_rows = pl.ds(0, GW)
-    order = [14, 10, 12, 8, 6, 4, 2]
-    kv_sends, q_sends = {}, []
-    for delta in order:
-        peer = peers[delta]
-        kv_sends[delta] = lines.put(qkv_ref.at[peer[1] // 4, kv_rows], kv_ref.at[c], peer)
-        if delta % 4 == 0:
-            q_sends.append(lines.put(qkv_ref.at[peer[1] // 4, q_rows], q_ref.at[c // 4], peer))
-    gathers = [Gather(lines, *two) for two in zip(own_w, full)]
-    passed = [lines.put(qkv_ref.at[c // 4, kv_rows], kv_ref.at[c], sibling)]
-    kept = [
-        lines.keep(qkv_ref.at[c // 4, kv_rows], kv_ref.at[c]),
-        lines.keep(qkv_ref.at[c // 4, q_rows], q_ref.at[c // 4]),
+    for layer in range(2):
+        total = got_gain[layer, 0].astype(F32) + got_gain[layer, 1].astype(F32)
+        gain_s[layer] = total + got_gain[layer, 2].astype(F32) + got_gain[layer, 3].astype(F32)
+    gains[...] = gain_s[...]
+    x_load.wait()
+    source = x_s
+    for layer in range(2):
+        q, kv, wide, totals, ot, out, hidden, gate_up, normed_two, product, normed = per_layer[layer::2]
+        project(
+            source, gain_s[layer, 0:1, :], cos, sin, w_q, lambda: loaded(layer, 0), qkv_s.at[layer], normed
+        )
+        if layer == 0:
+            begin(1, [0])
+        spread = Spread(lines, qkv_s.at[layer], q, kv)
+        spread.finish()
+        if layer == 0:
+            for gather in rest:
+                gather.from_neighbours()
+        attend(q, kv, low_s.at[layer], wide, totals, s_ref)
+        if layer == 0:
+            for gather in rest:
+                gather.from_opposite()
+        turn = Turn(lines, low_s.at[layer], ot)
+        turn.finish()
+        if layer == 0:
+            for gather in rest:
+                gather.from_beside()
+            for gather in rest:
+                gather.finish()
+            begin(0, [1, 2, 3])
+        mlp(
+            ot, source, gain_s[layer, 1:2, :], w_o, w_u, w_d, lambda i: loaded(layer, i + 1),
+            out, hidden, gate_up, normed_two, product,
+        )
+        if layer == 0:
+            begin(1, [1, 2, 3])
+        source = out
+
+
+LAYER_SHAPES = (
+    sds((4, GW, ROWS), BF16),
+    sds((CTX, 2 * GW, ROWS), BF16),
+    sds((4, GW, ROWS), F32),
+    sds((GH, 8, 512), F32),
+    sds((4, GW, ROWS), BF16),
+    sds((ROWS, D), BF16),
+    sds((ROWS, D), F32),
+    sds((ROWS, 2 * FF), F32),
+    sds((D, ROWS), BF16),
+    sds((FF, ROWS), BF16),
+    sds((D, ROWS), BF16),
+)
+
+
+def forward(inputs, gain, weights, tables):
+    per_layer = [shape for shape in LAYER_SHAPES for _ in range(2)]
+    full = full_shapes(weights)
+    scratch = [
+        pltpu.VMEM((ROWS, D), BF16),
+        *[pltpu.VMEM((4 * w.shape[0], w.shape[1]), BF16) for w in weights],
+        pltpu.VMEM((2, 4, 3 * GW, ROWS), BF16),
+        pltpu.VMEM((2, 4, GW, ROWS), BF16),
+        pltpu.VMEM((2048, 512), F32),
+        pltpu.VMEM((2, 4, 16, D), BF16),
+        DMA((2, 4, 4)),
+        DMA((1,)),
+        DMA((192,)),
+        DMA((192,)),
+        pltpu.VMEM((2, 16, D), F32),
     ]
-    for delta in reversed(order):
-        kv_sends[delta].wait_recv()
-        block = kv_ref.at[flip(c, delta)]
-        passed.append(lines.put(block, block, sibling))
-    for copy in kept:
-        copy.wait()
-    for copy in q_sends:
-        copy.wait()
-    for copy in kv_sends.values():
-        copy.wait_send()
-    for copy in passed:
-        copy.wait()
-    run_gathers(gathers)
-
-
-def spread(qkv, weights):
-    outs = [sds((4, GW, ROWS), BF16), sds((CTX, 2 * GW, ROWS), BF16)] + full_shapes(weights)
-    kernel = functools.partial(spread_kernel, len(weights))
-    res = exchange_call(kernel, [qkv, *weights], outs, [], next(ids), "spread")
-    return res[0], res[1], res[2:]
+    res = pl.pallas_call(
+        forward_kernel,
+        out_shape=[*per_layer, *full, sds((2, 16, D), F32)],
+        in_specs=[VM, VM, ANY, ANY] + [ANY] * 4,
+        out_specs=[VM] * 22 + [ANY] * 4 + [VM],
+        scratch_shapes=scratch,
+        compiler_params=pltpu.CompilerParams(
+            collective_id=next(ids), has_side_effects=True, vmem_limit_bytes=VMEM_LIMIT
+        ),
+        name="forward",
+    )(*tables, inputs, gain, *weights)
+    layers = [res[layer:22:2] for layer in range(2)]
+    return layers, res[22:26], res[26]
 
 
 class Meet:
@@ -702,35 +805,30 @@
         self.kept.wait()
 
 
-def turn_kernel(count, acts, shows, *refs):
-    (x_ref,), own_w, zero, one, shown, (o_ref,), full, taken, outs, (send, recv) = split_refs(
-        refs, 1, count, acts, acts, 2 * shows, 1, count, 3 * acts, shows, 2
+def turn_kernel(acts, shows, *refs):
+    (x_ref,), zero, one, shown, (o_ref,), taken, outs, (send, recv) = split_refs(
+        refs, 1, acts, acts, 2 * shows, 1, 3 * acts, shows, 2
     )
     s, c, z = here()
     lines = Lines(send, recv)
-    peers = [(s, flip(c, delta), z) for delta in (4, 8, 12)]
-    greet(peers + (gather_peers() if count else meet_peers() if acts else []))
-    copies = [lines.put(x_ref.at[peer[1] // 4], o_ref.at[c // 4], peer) for peer in peers]
-    gathers = [Gather(lines, *two) for two in zip(own_w, full)]
+    greet([(s, flip(c, delta), z) for delta in (4, 8, 12)] + meet_peers())
+    turn = Turn(lines, x_ref, o_ref)
     meets = [Meet(lines, *five) for five in zip(zero, one, *split_refs(taken, acts, acts, acts))]
     shown = [Show(lines, *shown, out) for out in outs]
-    lines.keep(x_ref.at[c // 4], o_ref.at[c // 4]).wait()
-    for copy in copies:
-        copy.wait()
+    turn.finish()
     for meet in meets:
         meet.forward()
-    run_gathers(gathers)
     for work in meets + shown:
         work.finish()
 
 
-def turn(x, weights=(), zero=(), one=(), show=()):
-    args = [x, *weights, *zero, *one, *show]
-    counts = len(weights), len(zero), len(show) // 2
-    outs = [sds((4, GW, ROWS), BF16)] + full_shapes(weights) + meet_shapes(zero)
+def turn(x, zero=(), one=(), show=()):
+    args = [x, *zero, *one, *show]
+    counts = len(zero), len(show) // 2
+    outs = [sds((4, GW, ROWS), BF16)] + meet_shapes(zero)
     outs += [sds((2, *a.shape), BF16) for a in show[::2]]
     res = exchange_call(functools.partial(turn_kernel, *counts), args, outs, [], next(ids), "turn")
-    return res[0], *split_refs(res[1:], counts[0], 3 * counts[1], counts[2])
+    return res[0], *split_refs(res[1:], 3 * counts[0], counts[1])
 
 
 def meet_kernel(*refs):
@@ -883,40 +981,6 @@
     return [pltpu.VMEM(shape, BF16) for shape in shapes]
 
 
-def forward_layer(layer, x, gains, w_qkv, late, tables):
-    qkv, normed = compute_call(
-        functools.partial(qkv_kernel, layer),
-        (x, gains[0], *tables, w_qkv),
-        (sds((4, 3 * GW, ROWS), BF16), sds((D, ROWS), BF16)),
-        [*weight_scratch((D, 3 * D)), DMA],
-        name="norm_qkv",
-        far=1,
-    )
-    q, kv, w_up = spread(qkv, late[1:2] if layer == 0 else [])
-    low, wide, totals = compute_call(
-        attend_kernel,
-        (q, kv),
-        (sds((4, GW, ROWS), BF16), sds((4, GW, ROWS), F32), sds((GH, 8, 512), F32)),
-        [pltpu.VMEM((2048, 512), F32)],
-        name="attend",
-    )
-    ot, w_rest, _, _ = turn(low, late[::2] if layer == 0 else [])
-    if layer == 0:
-        late = [w.reshape(2, -1, w.shape[-1]) for w in (w_rest[0], w_up[0], w_rest[1])]
-    ot = ot.reshape(D, ROWS)
-    out, hidden, gate_up, normed_two, product = compute_call(
-        functools.partial(mlp_kernel, layer),
-        (ot, x, gains[1], *late),
-        (sds((ROWS, D), BF16), sds((ROWS, D), F32), sds((ROWS, 2 * FF), F32),
-         sds((D, ROWS), BF16), sds((FF, ROWS), BF16)),
-        [*weight_scratch((D, D), (D, 2 * FF), (FF, D)), DMA((3,))],
-        name="mlp",
-        far=3,
-    )
-    lefts = [by_core(a) for a in (normed_two, product, ot, normed)]
-    return out, late, lefts, (x, q, kv, wide, totals, hidden, gate_up)
-
-
 def by_core(a):
     return a.reshape(4, 2, -1, ROWS)
 
@@ -957,21 +1021,30 @@
 
 def local(inputs, cotangent, attn_gain, qkv_weight, out_weight, mlp_gain, up_weight, down_weight):
     first = lax.axis_index("section") == 0
+    z = lax.axis_index("wshard")
+    cot = jnp.where(first, cotangent[0, 0], cotangent[1, 0])
+    gain = jnp.concatenate([attn_gain, mlp_gain], axis=0)
+    lanes = lax.broadcasted_iota(jnp.int32, (2, 4, 192), 1) == z
+    gain = jnp.where(lanes, gain[:, None, :], jnp.zeros((), BF16)).reshape(2, D)
+    gain = jnp.pad(gain, ((0, 14), (0, 0)))
     x = jnp.where(first, inputs[0, 0], inputs[1, 0])
-    cot = jnp.where(first, cotangent[0, 0], cotangent[1, 0])
-    gain = jnp.pad(jnp.concatenate([attn_gain, mlp_gain], axis=0), ((0, 14), (0, 64)))
-    w_qkv, gains = start(qkv_weight[0], gain)
-    w_qkv = w_qkv.reshape(2, D, 3 * D)
-    gains = [
-        [gains[layer, :, row, :192].reshape(1, D) for row in range(2)] for layer in range(2)
-    ]
     tables = rope_tables()
-    late = [out_weight[0], up_weight[0], down_weight[0]]
-    mid, late, left_zero, kept_zero = forward_layer(0, x, gains[0], w_qkv, late, tables)
-    end, _, left_one, kept_one = forward_layer(1, mid, gains[1], w_qkv, late, tables)
+    layers, full, gains = forward(
+        inputs, gain, [w[0] for w in (qkv_weight, out_weight, up_weight, down_weight)], tables
+    )
+    full = [w.reshape(2, -1, w.shape[-1]) for w in full]
+    w_qkv, late = full[0], full[1:]
+    gains = [[gains[layer, row : row + 1] for row in range(2)] for layer in range(2)]
+    kept, lefts_all = [], []
+    for source, layer in zip((x, layers[0][5]), layers):
+        q, kv, wide, totals, ot, out, hidden, gate_up, normed_two, product, normed = layer
+        kept.append((source, q, kv, wide, totals, hidden, gate_up))
+        lefts_all.append([by_core(a) for a in (normed_two, product, ot, normed)])
+    (kept_zero, kept_one), (left_zero, left_one) = kept, lefts_all
+    mid, end = layers[0][5], layers[1][5]
 
     d_ot, grad_hidden, gg_one, branch_one, d_gain = mlp_back(1, cot, kept_one, gains[1], late)
-    d_o, _, lefts, (activations,) = turn(
+    d_o, lefts, (activations,) = turn(
         d_ot.reshape(4, GW, ROWS), zero=left_zero, one=left_one, show=(mid, end)
     )
     dq, dkv = attend_back(d_o, kept_one)
@@ -982,7 +1055,7 @@
 
     d_ot, grad_hidden, gg_zero, branch_zero, d_gain = mlp_back(0, grad_mid, kept_zero, gains[0], late)
     rights_zero, rights_one = [gg_zero, grad_mid, branch_zero], [gg_one, cot, branch_one]
-    d_o, _, rights, _ = turn(d_ot.reshape(4, GW, ROWS), zero=rights_zero, one=rights_one)
+    d_o, rights, _ = turn(d_ot.reshape(4, GW, ROWS), zero=rights_zero, one=rights_one)
     mlp_lefts = [lefts[4 * i + j] for i in range(3) for j in range(3)]
     heights = (96, 144, 96)
     comb_mlp = compute_call(

time: 470 us -> 424 us (0.902)
  Pallas kernels: 455 us -> 412 us
    pallas_call x12 -> x7, Pallas kernels: 341 us -> 195 us  [exchange_call(): pl.pallas_call(kernel, out_shape=outs, in_specs=[ANY] * len(args), out_sp...]
    pallas_call x0 -> x1, Pallas kernels: none -> 139 us  [forward(): pl.pallas_call(forward_kernel, out_shape=[*per_layer, *full, sds((2, 16,...]
    pallas_call x15 -> x9, Pallas kernels: 113 us -> 77.6 us  [compute_call(): pl.pallas_call(kernel, out_shape=outs, in_specs=[VM] * (len(args) - far)...]
where the time goes in v4:
time: 424 us; the launch traced here: 420 us
  Pallas kernels  412 us (97%)
  local copies, waits for them, and re-layouts  5.19 us (1%)
    pallas_call x7, Pallas kernels, exchange_call(): pl.pallas_call(kernel, out_shape=outs, in_specs=[ANY] * len(args), out_sp...  195 us
    pallas_call x1, Pallas kernels, forward(): pl.pallas_call(forward_kernel, out_shape=[*per_layer, *full, sds((2, 16,...  139 us
    pallas_call x9, Pallas kernels, compute_call(): pl.pallas_call(kernel, out_shape=outs, in_specs=[VM] * (len(args) - far)...  77.6 us

profile of v4, /device:TPU:25, one launch (start us, length us, event | category | flops | bytes accessed | tf_op | source)
XLA Modules:
  0.0 420.1 jit_solution(10355221810257401341)
XLA Ops:
  0.6 0.0 copy-start
  0.7 0.8 multiply_sine_fusion
  1.5 0.1 iota.23
  1.5 0.1 iota.24
  1.6 0.7 pad_maximum_fusion
  2.3 0.1 broadcast_in_dim.36
  2.4 0.6 pad.4.refs_3_
  3.1 139.2 %forward.1 = (bf16[4,192,128]{2,1,0:T(8,128)(2,1)}, bf16[4,192,128]{2,1,0:T(8,128)(2,1)}, bf16[16,384,128]{2,1,0:T(8,128)(2,1)}, bf16[16,384,128]{2,1,0:T(8,128)...) custom-call(f32[32,128]{1,0:T(8,128)} %get-tuple-element.195.refs_0_, ...), custom_call_target="tpu_custom_call" | custom-call | tf_op jit(solution)/shard_map/forward/pallas_call | solution.py:722
  142.3 1.4 slice_bitcast_fusion
  143.7 0.8 select_bitcast_fusion
  144.5 7.2 %mlp_back.2 = (bf16[768,128]{1,0:T(8,128)(2,1)}, f32[128,768]{1,0:T(8,128)}, bf16[128,2304]{1,0:T(8,128)(2,1)}, bf16[128,768]{1,0:T(8,128)(2,1)}, f32[1,768]{1,0:T(1,128)}) custom-call(bf16[128,768]{1,0:T(8,128)(2,1)} %get-tuple-element.197.g_ref.refs_5_.refs_10_, f32[128,768]{1,0:T(8,128)} %get-tuple-element.94.hidden_ref, ...), custom_call_target="tpu_custom_call" | custom-call | tf_op jit(solution)/shard_map/mlp_back/pallas_call | solution.py:42
  151.8 21.9 %turn.2 = (bf16[4,192,128]{2,1,0:T(8,128)(2,1)}, bf16[4,96,128]{2,1,0:T(8,128)(2,1)}, bf16[4,144,128]{2,1,0:T(8,128)(2,1)}, bf16[4,96,128]{2,1,0:T(8,128)(2,1)},...) custom-call(bf16[4,192,128]{2,1,0:T(8,128)(2,1)} %bitcast.70, ...), custom_call_target="tpu_custom_call" | custom-call | tf_op jit(solution)/shard_map/turn/pallas_call | solution.py:431
  173.7 16.9 %attend_back.2 = (bf16[4,192,128]{2,1,0:T(8,128)(2,1)}, bf16[16,384,128]{2,1,0:T(8,128)(2,1)}) custom-call(bf16[4,192,128]{2,1,0:T(8,128)(2,1)} %get-tuple-element.116.q_ref, bf16[16,384,128]{2,1,0:T(8,128)(2,1)} %get-tuple-element.117.kv_ref, f32[4,192,128]{2,1,0:T(8,128)} %get-tuple-element.118.wide_ref, f32[3,8,512]{2,1,0:T(8,128)} %get-tuple-element.119.totals_ref, ...), custom_call_target="tpu_custom_call" | custom-call | tf_op jit(solution)/shard_map/attend_back/pallas_call | solution.py:42
  190.6 20.0 %give_back.2 = (bf16[4,192,128]{2,1,0:T(8,128)(2,1)}, bf16[8,384,128]{2,1,0:T(8,128)(2,1)}) custom-call(bf16[4,192,128]{2,1,0:T(8,128)(2,1)} %get-tuple-element.121.refs_0_, bf16[16,384,128]{2,1,0:T(8,128)(2,1)} %get-tuple-element.122.refs_1_), custom_call_target="tpu_custom_call" | custom-call | tf_op jit(solution)/shard_map/give_back/pallas_call | solution.py:431
  210.6 5.6 %qkv_back.2 = (bf16[128,768]{1,0:T(8,128)(2,1)}, bf16[128,2304]{1,0:T(8,128)(2,1)}, bf16[16,768]{1,0:T(8,128)(2,1)}) custom-call(bf16[4,192,128]{2,1,0:T(8,128)(2,1)} %get-tuple-element.123.dq_ref, bf16[8,384,128]{2,1,0:T(8,128)(2,1)} %get-tuple-element.124.dkv_ref, bf16[128,768]{1,0:T(8,128)(2,1)} %get-tuple-element.109.refs_9_.x_ref, ...), custom_call_target="tpu_custom_call" | custom-call | tf_op jit(solution)/shard_map/qkv_back/pallas_call | solution.py:42
  216.2 7.2 %mlp_back.3 = (bf16[768,128]{1,0:T(8,128)(2,1)}, f32[128,768]{1,0:T(8,128)}, bf16[128,2304]{1,0:T(8,128)(2,1)}, bf16[128,768]{1,0:T(8,128)(2,1)}, f32[1,768]{1,0:T(1,128)}) custom-call(bf16[128,768]{1,0:T(8,128)(2,1)} %get-tuple-element.128.g_ref.refs_2_.refs_4_.refs_5_, f32[128,768]{1,0:T(8,128)} %get-tuple-element.129.hidden_ref, ...), custom_call_target="tpu_custom_call" | custom-call | tf_op jit(solution)/shard_map/mlp_back/pallas_call | solution.py:42
  223.4 22.4 %turn.3 = (bf16[4,192,128]{2,1,0:T(8,128)(2,1)}, bf16[128,2304]{1,0:T(8,128)(2,1)}, bf16[128,768]{1,0:T(8,128)(2,1)}, bf16[128,768]{1,0:T(8,128)(2,1)}, bf16[128...) custom-call(bf16[4,192,128]{2,1,0:T(8,128)(2,1)} %bitcast.71, ...), custom_call_target="tpu_custom_call" | custom-call | tf_op jit(solution)/shard_map/turn/pallas_call | solution.py:431
  245.9 8.2 %mlp_weights.1.refs_2_.comb_m = bf16[4,576,768]{2,1,0:T(8,128)(2,1)} custom-call(bf16[4,2,96,128]{3,2,1,0:T(8,128)(2,1)} %bitcast.63, bf16[4,2,144,128]{3,2,1,0:T(8,128)(2,1)} %bitcast.49, bf16[4,2,96,128]{3,2,1,0:T(8,128)(2,1)} %bitcast.59, bf16[128,2304]{1,0:T(8,128)(2,1)} %get-tuple-element.132.refs_1_.refs_3_, ...), custom_call_target="tpu_custom_call" | custom-call | tf_op jit(solution)/shard_map/mlp_weights/pallas_call | solution.py:42
  254.1 16.7 %attend_back.3 = (bf16[4,192,128]{2,1,0:T(8,128)(2,1)}, bf16[16,384,128]{2,1,0:T(8,128)(2,1)}) custom-call(bf16[4,192,128]{2,1,0:T(8,128)(2,1)} %get-tuple-element.112.q_ref, bf16[16,384,128]{2,1,0:T(8,128)(2,1)} %get-tuple-element.113.kv_ref, f32[4,192,128]{2,1,0:T(8,128)} %get-tuple-element.114.wide_ref, f32[3,8,512]{2,1,0:T(8,128)} %get-tuple-element.115.totals_ref, ...), custom_call_target="tpu_custom_call" | custom-call | tf_op jit(solution)/shard_map/attend_back/pallas_call | solution.py:42
  270.8 44.3 %give_back.3 = (bf16[4,192,128]{2,1,0:T(8,128)(2,1)}, bf16[8,384,128]{2,1,0:T(8,128)(2,1)}, bf16[3,576,768]{2,1,0:T(8,128)(2,1)}) custom-call(bf16[4,192,128]{2,1,0:T(8,128)(2,1)} %get-tuple-element.137.refs_0_, bf16[16,384,128]{2,1,0:T(8,128)(2,1)} %get-tuple-element.138.refs_1_, bf16[4,576,768]{2,1,0:T(8,128)(2,1)} %mlp_weights.1.refs_2_.comb_m), custom_call_target="tpu_custom_call" | custom-call | tf_op jit(solution)/shard_map/give_back/pallas_call | solution.py:431
  315.1 5.6 %qkv_back.3 = (bf16[128,768]{1,0:T(8,128)(2,1)}, bf16[128,2304]{1,0:T(8,128)(2,1)}, bf16[16,768]{1,0:T(8,128)(2,1)}) custom-call(bf16[4,192,128]{2,1,0:T(8,128)(2,1)} %get-tuple-element.157.dq_ref, bf16[8,384,128]{2,1,0:T(8,128)(2,1)} %get-tuple-element.158.dkv_ref, bf16[128,768]{1,0:T(8,128)(2,1)} %get-tuple-element.196.x_ref, ...), custom_call_target="tpu_custom_call" | custom-call | tf_op jit(solution)/shard_map/qkv_back/pallas_call | solution.py:42
  320.7 16.1 %meet.1 = (bf16[128,2304]{1,0:T(8,128)(2,1)}, bf16[128,2304]{1,0:T(8,128)(2,1)}, bf16[128,2304]{1,0:T(8,128)(2,1)}, bf16[16,768]{1,0:T(8,128)(2,1)}, bf16[2,128,768]{2,1,0:T(8,128)(2,1)}) custom-call(bf16[128,2304]{1,0:T(8,128)(2,1)} %get-tuple-element.161.refs_0_.refs_2_, bf16[16,768]{1,0:T(8,128)(2,1)} %get-tuple-element.162.refs_1_.refs_3_, ...), custom_call_target="tpu_custom_call" | custom-call | tf_op jit(solution)/shard_map/meet/pallas_call | solution.py:431
  336.8 5.9 %qkv_weights.1.refs_0_.comb_q = bf16[4,320,768]{2,1,0:T(8,128)(2,1)} custom-call(bf16[16,768]{1,0:T(8,128)(2,1)} %get-tuple-element.168.refs_0_, bf16[4,2,96,128]{3,2,1,0:T(8,128)(2,1)} %bitcast.55, bf16[128,2304]{1,0:T(8,128)(2,1)} %get-tuple-element.161.refs_0_.refs_2_, bf16[16,768]{1,0:T(8,128)(2,1)} %get-tuple-element.162.refs_1_.refs_3_, ...), custom_call_target="tpu_custom_call" | custom-call | tf_op jit(solution)/shard_map/qkv_weights/pallas_call | solution.py:42
  342.7 26.7 %scatter.1.got_q = bf16[3,320,768]{2,1,0:T(8,128)(2,1)} custom-call(bf16[4,320,768]{2,1,0:T(8,128)(2,1)} %qkv_weights.1.refs_0_.comb_q), custom_call_target="tpu_custom_call" | custom-call | tf_op jit(solution)/shard_map/scatter/pallas_call | solution.py:431
  369.4 43.5 %finish.1.fin_ref = bf16[2,896,768]{2,1,0:T(8,128)(2,1)} custom-call(bf16[4,576,768]{2,1,0:T(8,128)(2,1)} %mlp_weights.1.refs_2_.comb_m, bf16[3,576,768]{2,1,0:T(8,128)(2,1)} %get-tuple-element.167.got_m, bf16[4,320,768]{2,1,0:T(8,128)(2,1)} %qkv_weights.1.refs_0_.comb_q, bf16[3,320,768]{2,1,0:T(8,128)(2,1)} %scatter.1.got_q), custom_call_target="tpu_custom_call" | custom-call | tf_op jit(solution)/shard_map/finish/pallas_call | solution.py:431
  412.9 0.0 copy-start.1
  412.9 0.0 copy-start.2
  412.9 4.3 %assemble.1 = (f32[192,2304]{1,0:T(8,128)}, f32[192,768]{1,0:T(8,128)}, f32[288,768]{1,0:T(8,128)}, f32[192,2304]{1,0:T(8,128)}, f32[16,768]{1,0:T(8,128)}) custom-call(bf16[2,896,768]{2,1,0:T(8,128)(2,1)} %finish.1.fin_ref), custom_call_target="tpu_custom_call" | custom-call | tf_op jit(solution)/shard_map/assemble/pallas_call | solution.py:42
  417.2 0.7 slice.41
  417.9 0.6 fusion
  418.6 0.7 copy.20
  419.3 0.7 copy.21
  (10 shorter events, 0.1 us)
Async XLA Ops:
  0.6 143.1 %copy-start = (bf16[2,1,128,768]{3,2,1,0:T(8,128)(2,1)S(1)}, bf16[2,1,128,768]{3,2,1,0:T(8,128)(2,1)}, u32[]{:S(2)}) copy-start(bf16[2,1,128,768]{3,2,1,0:T(8,128)(2,1)} %refs_2_.1) | copy-start | bytes 1179652
  0.6 143.1 %copy-start.3 = (bf16[2,1,128,768]{3,2,1,0:T(8,128)(2,1)S(1)}, bf16[2,1,128,768]{3,2,1,0:T(8,128)(2,1)}, u32[]{:S(2)}) copy-start(bf16[2,1,128,768]{3,2,1,0:T(8,128)(2,1)} %param.9) | copy-start | bytes 1179652
  412.9 5.7 %copy-start.1 = (bf16[2,128,768]{2,1,0:T(8,128)(2,1)S(1)}, bf16[2,128,768]{2,1,0:T(8,128)(2,1)}, u32[]{:S(2)}) copy-start(bf16[2,128,768]{2,1,0:T(8,128)(2,1)} %get-tuple-element.111) | copy-start | bytes 1179652
  412.9 6.4 %copy-start.2 = (bf16[2,128,768]{2,1,0:T(8,128)(2,1)S(1)}, bf16[2,128,768]{2,1,0:T(8,128)(2,1)}, u32[]{:S(2)}) copy-start(bf16[2,128,768]{2,1,0:T(8,128)(2,1)} %get-tuple-element.166) | copy-start | bytes 1179652

commit v5 on v4

v5 whole, which is shorter than its diff:
```python
import functools

import jax
import jax.numpy as jnp
from jax import lax
from jax.experimental import pallas as pl
from jax.experimental.pallas import tpu as pltpu
from jax.sharding import PartitionSpec as P

D = 768
HEADS = 12
HEAD_DIM = 64
FF = 1152
ROWS = 128
GROUPS = 4
GH = HEADS // GROUPS
GW = GH * HEAD_DIM
CTX = 16
SCALE = HEAD_DIM ** (-0.5)
F32 = jnp.float32
BF16 = jnp.bfloat16
MESH = pl.DeviceIdType.MESH
DMA = pltpu.SemaphoreType.DMA
ANY = pl.BlockSpec(memory_space=pl.ANY)
VM = pl.BlockSpec(memory_space=pltpu.VMEM)
VMEM_LIMIT = 60 * 1024 * 1024


def dot(a, b):
    return jnp.dot(a, b, preferred_element_type=F32)


def dot_nt(a, b):
    return lax.dot_general(a, b, (((1,), (1,)), ((), ())), preferred_element_type=F32)


def sds(shape, dtype):
    return jax.ShapeDtypeStruct(shape, dtype)


def compute_call(kernel, args, outs, name):
    return pl.pallas_call(
        kernel,
        out_shape=outs,
        in_specs=[VM] * len(args),
        out_specs=jax.tree.map(lambda _: VM, outs),
        compiler_params=pltpu.CompilerParams(vmem_limit_bytes=VMEM_LIMIT),
        name=name,
    )(*args)


def fetch(src, dst, sem):
    copy = pltpu.make_async_copy(src, dst, sem)
    copy.start()
    return copy


def turned_low(x):
    return x.astype(F32).T.astype(BF16)


def norm_parts(source):
    centered = source - jnp.mean(source, axis=-1, keepdims=True)
    variance = jnp.mean(centered * centered, axis=-1, keepdims=True)
    rstd = lax.rsqrt(variance + 1e-05)
    return centered * rstd, rstd


def norm_back(grad, normalized, rstd, gain):
    inner = grad * gain
    mean_one = jnp.mean(inner, axis=-1, keepdims=True)
    mean_two = jnp.mean(inner * normalized, axis=-1, keepdims=True)
    grad_gain = jnp.sum(grad * normalized, axis=0, keepdims=True)
    return rstd * (inner - mean_one - normalized * mean_two), grad_gain


def split_refs(refs, *counts):
    refs = list(refs)
    out = []
    for count in counts:
        out.append(refs[:count])
        refs = refs[count:]
    return out


def project(x_ref, gain, cos_ref, sin_ref, w_ref, loaded, qkv_ref, normed_ref):
    normalized, _ = norm_parts(x_ref[...].astype(F32))
    normed = (normalized * gain).astype(BF16)
    normed_ref[...] = turned_low(normed)
    loaded()
    cos = cos_ref[...]
    sin = sin_ref[...]
    for part in range(3):
        for block in range(3):
            at = part * D + block * 256
            turned = dot(normed, w_ref[:, at : at + 256]).T
            for head_at in range(4):
                head = block * 4 + head_at
                one = turned[head_at * 64 : head_at * 64 + 32]
                two = turned[head_at * 64 + 32 : head_at * 64 + 64]
                if part < 2:
                    one, two = one * cos - two * sin, two * cos + one * sin
                if part == 0:
                    one, two = one * SCALE, two * SCALE
                row = part * GW + (head % GH) * HEAD_DIM
                qkv_ref[head // GH, row : row + 32, :] = one.astype(BF16)
                qkv_ref[head // GH, row + 32 : row + 64, :] = two.astype(BF16)


CHUNK = 256
CHUNKS = 2048 // CHUNK
PAIR = CHUNK // ROWS


def attend(q_ref, kv_ref, low_ref, wide_ref, totals_ref, s_ref):
    @pl.loop(0, GH)
    def _(h):
        at = pl.multiple_of(h * HEAD_DIM, HEAD_DIM)
        value_at = pl.multiple_of(h * HEAD_DIM + GW, HEAD_DIM)
        qt = jnp.concatenate([q_ref[i, pl.ds(at, HEAD_DIM), :] for i in range(4)], axis=1)
        top = jnp.full((8, 512), -jnp.inf, F32)
        for c in range(CHUNKS):
            keys = jnp.concatenate(
                [kv_ref[c * PAIR + i, pl.ds(at, HEAD_DIM), :].T for i in range(PAIR)], axis=0
            )
            scores = dot(keys, qt)
            s_ref[c * CHUNK : (c + 1) * CHUNK, :] = scores
            top = jnp.maximum(top, jnp.max(scores.reshape(CHUNK // 8, 8, 512), axis=0))
        top = jnp.max(top, axis=0, keepdims=True)
        total = jnp.zeros((8, 512), F32)
        acc = jnp.zeros((HEAD_DIM, 512), F32)
        for c in range(CHUNKS):
            p = jnp.exp(s_ref[c * CHUNK : (c + 1) * CHUNK, :] - top)
            total = total + jnp.sum(p.reshape(CHUNK // 8, 8, 512), axis=0)
            values = jnp.concatenate(
                [kv_ref[c * PAIR + i, pl.ds(value_at, HEAD_DIM), :] for i in range(PAIR)], axis=1
            )
            acc = acc + dot(values, p.astype(BF16))
        total = jnp.sum(total, axis=0, keepdims=True)
        out = acc / total
        totals_ref[h] = jnp.broadcast_to(top + jnp.log(total), (8, 512))
        for i in range(4):
            piece = out[:, i * ROWS : (i + 1) * ROWS]
            wide_ref[i, pl.ds(at, HEAD_DIM), :] = piece
            low_ref[i, pl.ds(at, HEAD_DIM), :] = piece.astype(BF16)


def attend_back(start, stop, q_ref, kv_ref, wide_ref, totals_ref, do_ref, dq_ref, dkv_ref):
    @pl.loop(start, stop)
    def _(h):
        at = pl.multiple_of(h * HEAD_DIM, HEAD_DIM)
        value_at = pl.multiple_of(h * HEAD_DIM + GW, HEAD_DIM)
        out_at = pl.multiple_of(h * ROWS, ROWS)
        qt = jnp.concatenate([q_ref[i, pl.ds(at, HEAD_DIM), :] for i in range(4)], axis=1)
        dot_t = jnp.concatenate([do_ref[i, pl.ds(at, HEAD_DIM), :] for i in range(4)], axis=1)
        wide = jnp.concatenate([wide_ref[i, pl.ds(at, HEAD_DIM), :] for i in range(4)], axis=1)
        delta = jnp.sum(wide * dot_t.astype(F32), axis=0, keepdims=True)
        totals = totals_ref[h, 0:1, :]
        zero = jnp.zeros((512, HEAD_DIM), BF16)
        sides = jnp.concatenate(
            [
                jnp.concatenate([qt.T, zero], axis=1),
                jnp.concatenate([zero, dot_t.T], axis=1),
            ],
            axis=0,
        )

        def step(c, acc):
            keys_t = [kv_ref[c * PAIR + i, pl.ds(at, HEAD_DIM), :] for i in range(PAIR)]
            values_t = [kv_ref[c * PAIR + i, pl.ds(value_at, HEAD_DIM), :] for i in range(PAIR)]
            keys = jnp.concatenate([k.T for k in keys_t], axis=0)
            values = jnp.concatenate([v.T for v in values_t], axis=0)
            p = jnp.exp(dot(keys, qt) - totals)
            ds = (p * (dot(values, dot_t) - delta)).astype(BF16)
            both = jnp.concatenate([ds, p.astype(BF16)], axis=1)
            grads = dot(both, sides).astype(BF16)
            for i in range(PAIR):
                dkv_ref[c * PAIR + i, pl.ds(out_at, ROWS), :] = grads[i * ROWS : (i + 1) * ROWS]
            return acc + dot(jnp.concatenate(keys_t, axis=1), ds)

        acc = lax.fori_loop(0, CHUNKS, step, jnp.zeros((HEAD_DIM, 512), F32)) * SCALE
        for i in range(4):
            dq_ref[i, pl.ds(at, HEAD_DIM), :] = acc[:, i * ROWS : (i + 1) * ROWS].astype(BF16)


def mlp(
    ot_ref, x_ref, gain, wo_ref, wu_ref, wd_ref, loaded,
    out_ref, hidden_ref, gate_up_ref, normed_ref, product_ref,
):
    attended = turned_low(ot_ref[...].reshape(D, ROWS))
    loaded(0)
    hidden = x_ref[...].astype(F32) + dot(attended, wo_ref[...])
    hidden_ref[...] = hidden
    normalized, _ = norm_parts(hidden)
    normed = (normalized * gain).astype(BF16)
    normed_ref[...] = turned_low(normed)
    loaded(1)
    gate_up = dot(normed, wu_ref[...])
    gate_up_ref[...] = gate_up
    gate = gate_up[:, :FF]
    phi = 0.5 * (1.0 + lax.erf(gate * 0.5**0.5))
    product = (gate * phi * gate_up[:, FF:]).astype(BF16)
    product_ref[...] = turned_low(product)
    loaded(2)
    out_ref[...] = (hidden + dot(product, wd_ref[...])).astype(BF16)


def mlp_back(
    grad_ref, hidden_ref, gate_up_ref, gain, wo_ref, wu_ref, wd_ref, loaded,
    dot_ref, grad_hidden_ref, gg_ref, branch_ref, d_gain_ref,
):
    grad = grad_ref[...]
    loaded(2)
    grad_product = dot_nt(grad, wd_ref[...])
    gate = gate_up_ref[:, :FF]
    up = gate_up_ref[:, FF:]
    phi = 0.5 * (1.0 + lax.erf(gate * 0.5**0.5))
    density = jnp.exp(-0.5 * gate * gate) * 0.3989422804014327
    grad_gate = (grad_product * up * (phi + gate * density)).astype(BF16)
    grad_up = (grad_product * gate * phi).astype(BF16)
    gg_ref[:, :FF] = grad_gate
    gg_ref[:, FF:] = grad_up
    loaded(1)
    grad_normed = dot_nt(grad_gate, wu_ref[:, :FF]) + dot_nt(grad_up, wu_ref[:, FF:])
    normalized, rstd = norm_parts(hidden_ref[...])
    part, d_gain = norm_back(grad_normed, normalized, rstd, gain)
    d_gain_ref[...] = d_gain
    grad_hidden = grad.astype(F32) + part
    grad_hidden_ref[...] = grad_hidden
    branch = grad_hidden.astype(BF16)
    branch_ref[...] = branch
    loaded(0)
    turned = dot_nt(branch, wo_ref[...]).T.astype(BF16)
    for group in range(GROUPS):
        dot_ref[group] = turned[group * GW : (group + 1) * GW]


def qkv_back(
    dq_ref, dkv_ref, x_ref, gain, cos_ref, sin_ref, grad_hidden_ref, gain_two_ref, w_ref, loaded,
    grad_x_refs, gp_out_ref, gains_ref, gp_ref,
):
    cos = cos_ref[...]
    sin = sin_ref[...]

    def back(one, two):
        return one * cos + two * sin, two * cos - one * sin

    for head in range(HEADS):
        group, inner = head // GH, head % GH
        at = inner * HEAD_DIM
        one = dq_ref[group, at : at + 32, :].astype(F32)
        two = dq_ref[group, at + 32 : at + 64, :].astype(F32)
        gq = back(one, two)
        rows = slice(inner * ROWS, (inner + 1) * ROWS)
        kv = (dkv_ref[2 * group, rows, :].astype(F32) + dkv_ref[2 * group + 1, rows, :].astype(F32)).T
        gk = back(kv[:32], kv[32:64])
        base = head * HEAD_DIM
        gp_ref[base : base + 32, :] = gq[0]
        gp_ref[base + 32 : base + 64, :] = gq[1]
        gp_ref[D + base : D + base + 32, :] = gk[0]
        gp_ref[D + base + 32 : D + base + 64, :] = gk[1]
        gp_ref[2 * D + base : 2 * D + base + 64, :] = kv[64:]
    loaded()
    grad_normed = jnp.zeros((ROWS, D), F32)
    for block in range(9):
        cols = slice(block * 256, (block + 1) * 256)
        gp = gp_ref[cols, :].T.astype(BF16)
        gp_out_ref[:, cols] = gp
        grad_normed = grad_normed + dot_nt(gp, w_ref[:, cols])
    normalized, rstd = norm_parts(x_ref[...].astype(F32))
    part, d_gain = norm_back(grad_normed, normalized, rstd, gain)
    gains_ref[...] = jnp.concatenate(
        [d_gain, gain_two_ref[...], jnp.zeros((14, D), F32)], axis=0
    ).astype(BF16)
    for ref in grad_x_refs:
        ref[...] = (grad_hidden_ref[...] + part).astype(BF16)


MLP_ROWS = 576
QKV_ROWS = 320
SUM_ROWS = MLP_ROWS + QKV_ROWS


def weight_product(out_ref, at, left, lefts, right, rights):
    section = lax.axis_index("section")
    core = lax.rem(lax.axis_index("ctx"), 2)
    (a_sib, a_far, a_both), (g_sib, g_far, g_both) = lefts, rights
    height = a_sib.shape[1]
    for block in range(g_sib.shape[1] // D):
        cols = slice(block * D, (block + 1) * D)
        g = [right[section, :, cols], g_sib[:, cols], g_far[:, cols], g_both[:, cols]]
        g = jnp.concatenate(g, axis=0)
        for shard in range(4):
            a = [left[section, shard, core], a_sib[shard], a_far[shard, core], a_both[shard]]
            row = at + block * height
            both = dot(jnp.concatenate(a, axis=1), g)
            out_ref[shard, row : row + height, :] = both.astype(BF16)


def assemble_kernel(mlp_ref, qkv_in_ref, up_ref, out_ref, down_ref, qkv_ref, gains_ref):
    for half in range(2):
        rows = slice(half * 96, half * 96 + 96)
        for block in range(3):
            cols = slice(block * D, (block + 1) * D)
            at = slice(block * 96, block * 96 + 96)
            up_ref[rows, cols] = mlp_ref[half, at, :].astype(F32)
            qkv_ref[rows, cols] = qkv_in_ref[half, at, :].astype(F32)
        out_ref[rows, :] = mlp_ref[half, 288:384, :].astype(F32)
        down_ref[half * 144 : half * 144 + 144, :] = mlp_ref[half, 384:528, :].astype(F32)
    gains_ref[...] = qkv_in_ref[0, 288:304, :].astype(F32) + qkv_in_ref[1, 288:304, :].astype(F32)


def here():
    return lax.axis_index("section"), lax.axis_index("ctx"), lax.axis_index("wshard")


def flip(index, delta):
    for bit in (1, 2, 4, 8):
        if delta & bit:
            index = index + bit - 2 * bit * lax.rem(index // bit, 2)
    return index


def greet(peers):
    barrier = pltpu.get_barrier_semaphore()
    for peer in peers:
        pl.semaphore_signal(barrier, inc=1, device_id=peer, device_id_type=MESH)
    pl.semaphore_wait(barrier, len(peers))


def remote(src, dst, send, recv, peer):
    return pltpu.make_async_remote_copy(
        src_ref=src, dst_ref=dst, send_sem=send, recv_sem=recv, device_id=peer, device_id_type=MESH
    )


class Lines:
    count = 192

    def __init__(self, send, recv):
        self.send, self.recv, self.used, self.waits = send, recv, 0, []

    def make(self, src, dst, peer):
        at = self.used
        self.used += 1
        assert at < self.count
        return remote(src, dst, self.send.at[at], self.recv.at[at], peer)

    def put(self, src, dst, peer):
        copy = self.make(src, dst, peer)
        copy.start()
        return copy

    def keep(self, src, dst):
        at = self.used
        self.used += 1
        assert at < self.count
        copy = pltpu.make_async_copy(src, dst, self.send.at[at])
        copy.start()
        return copy


ids = iter(range(1, 64))


def sibling_of(s, c, z):
    return (s, flip(c, 1), z)


def z_peers():
    s, c, z = here()
    return [(s, c, lax.rem(z + r, 4)) for r in (1, 3, 2)]


def beside_peers():
    s, c, z = here()
    return [(1 - s, c, z), (1 - s, flip(c, 8), z)]


class Gather:
    def __init__(self, lines, own, full):
        s, c, z = here()
        rows, cols = full.shape[2] // 2, full.shape[3] // 2
        self.rows = pl.ds(pl.multiple_of(lax.rem(c, 2) * rows, 16), rows)
        self.cols = [
            pl.ds(pl.multiple_of(side * cols, 128), cols) for side in (c // 8, 1 - c // 8)
        ]
        self.halves = [pl.ds(0, cols), pl.ds(cols, cols)]
        self.lines, self.full = lines, full
        self.sibling = sibling_of(s, c, z)
        after, before, _ = z_peers()
        self.step = []
        for cut, order in ((0, (after, before)), (1, (after, before))):
            where = full.at[s, z, self.rows, self.halves[cut]]
            piece = own.at[self.rows, self.halves[cut]]
            self.step.append([lines.put(piece, where, peer) for peer in order])
        self.peers = (after, before)
        self.aside = [self.beside(own.at[self.rows, self.cols[0]], z)]
        whole = full.at[s, z, self.rows]
        self.passed = [lines.put(own.at[self.rows], whole, self.sibling)]
        self.kept = lines.keep(own.at[self.rows], whole)
        self.sent = []

    def beside(self, src, z):
        s, _, _ = here()
        where = self.full.at[s, z, self.rows, self.cols[0]]
        return [self.lines.put(src, where, peer) for peer in beside_peers()]

    def from_neighbours(self):
        s, _, z = here()
        self.sources = [lax.rem(z + 3, 4), lax.rem(z + 1, 4)]
        self.second = []
        for side in (0, 1):
            self.step[side][side].wait_recv()
            block = self.full.at[s, self.sources[side], self.rows, self.halves[side]]
            self.second.append(self.lines.put(block, block, self.peers[side]))
        for side in (0, 1):
            self.step[1 - side][side].wait_recv()
            self.onward(self.sources[side])

    def onward(self, z):
        s, _, _ = here()
        block = self.full.at[s, z, self.rows]
        self.passed.append(self.lines.put(block, block, self.sibling))
        self.aside.append(self.beside(block.at[:, self.cols[0]], z))

    def from_opposite(self):
        _, _, z = here()
        for copy in self.second:
            copy.wait_recv()
        self.onward(lax.rem(z + 2, 4))

    def from_beside(self):
        s, _, z = here()
        for copies, source in zip(self.aside, (z, *self.sources, lax.rem(z + 2, 4))):
            for i, copy in enumerate(copies):
                copy.wait_recv()
                block = self.full.at[1 - s, source, self.rows, self.cols[i]]
                self.passed.append(self.lines.put(block, block, self.sibling))

    def finish(self):
        self.kept.wait()
        for copies in (*self.step, *self.aside, self.second):
            for copy in copies:
                copy.wait_send()
        for copy in self.passed:
            copy.wait()


def run_gathers(gathers):
    for gather in gathers:
        gather.from_neighbours()
    for gather in gathers:
        gather.from_opposite()
    for gather in gathers:
        gather.from_beside()
    for gather in gathers:
        gather.finish()


def full_shapes(weights):
    return [sds((2, 4, *w.shape), BF16) for w in weights]


def gather_peers():
    return [sibling_of(*here()), *z_peers()[:2], *beside_peers()]


def shard_loads(full, layer, dst, sems):
    rows = full.shape[2]
    return [
        pltpu.make_async_copy(full.at[layer, i], dst.at[pl.ds(i * rows, rows)], sems.at[i])
        for i in range(4)
    ]


class Spread:
    order = [14, 10, 12, 8, 6, 4, 2]

    def __init__(self, lines, qkv_ref, q_ref, kv_ref):
        s, c, z = here()
        self.lines, self.kv_ref = lines, kv_ref
        self.sibling = sibling_of(s, c, z)
        kv_rows = pl.ds(GW, 2 * GW)
        q_rows = pl.ds(0, GW)
        self.kv_sends, self.q_sends = {}, []
        for delta in self.order:
            peer = (s, flip(c, delta), z)
            self.kv_sends[delta] = lines.put(qkv_ref.at[peer[1] // 4, kv_rows], kv_ref.at[c], peer)
            if delta % 4 == 0:
                self.q_sends.append(lines.put(qkv_ref.at[peer[1] // 4, q_rows], q_ref.at[c // 4], peer))
        self.passed = [lines.put(qkv_ref.at[c // 4, kv_rows], kv_ref.at[c], self.sibling)]
        self.kept = [
            lines.keep(qkv_ref.at[c // 4, kv_rows], kv_ref.at[c]),
            lines.keep(qkv_ref.at[c // 4, q_rows], q_ref.at[c // 4]),
        ]

    def finish(self):
        _, c, _ = here()
        for delta in reversed(self.order):
            self.kv_sends[delta].wait_recv()
            block = self.kv_ref.at[flip(c, delta)]
            self.passed.append(self.lines.put(block, block, self.sibling))
        for copy in self.kept + self.q_sends + self.passed:
            copy.wait()
        for copy in self.kv_sends.values():
            copy.wait_send()


class Turn:
    def __init__(self, lines, x_ref, o_ref):
        s, c, z = here()
        peers = [(s, flip(c, delta), z) for delta in (4, 8, 12)]
        self.copies = [lines.put(x_ref.at[peer[1] // 4], o_ref.at[c // 4], peer) for peer in peers]
        self.copies.append(lines.keep(x_ref.at[c // 4], o_ref.at[c // 4]))

    def finish(self):
        for copy in self.copies:
            copy.wait()


def forward_kernel(*refs):
    (cos, sin, inputs, gain), own, per_layer, full, (gains,), scratch = split_refs(refs, 4, 4, 11, 4, 1, 14)
    x_s, w_q, w_o, w_u, w_d, qkv_s, low_s, s_ref, got_gain, load_sem, in_sem, send, recv, gain_s = scratch
    s, c, z = here()
    lines = Lines(send, recv)
    x_load = fetch(inputs.at[s, 0], x_s, in_sem.at[0])
    across = [(1 - s, c, lax.rem(z + r, 4)) for r in (1, 3, 2)]
    ctx_peers = [(s, flip(c, delta), z) for delta in range(2, CTX, 2)]
    greet([*gather_peers(), z_peers()[2], *across, *ctx_peers])

    first = Gather(lines, own[0], full[0])
    gain_copies = [
        lines.put(gain, got_gain.at[s, z], peer) for peer in (*z_peers(), beside_peers()[0], *across)
    ]
    gain_copies.append(lines.keep(gain, got_gain.at[s, z]))
    run_gathers([first])
    rest = [Gather(lines, own[i], full[i]) for i in (2, 1, 3)]

    targets = (w_q, w_o, w_u, w_d)
    loads = [
        [shard_loads(full[i], layer, targets[i], load_sem.at[layer, i]) for i in range(4)]
        for layer in range(2)
    ]

    def begin(layer, which):
        for i in which:
            for copy in loads[layer][i]:
                copy.start()

    def loaded(layer, i):
        for copy in loads[layer][i]:
            copy.wait()

    begin(0, [0])
    for copy in gain_copies:
        copy.wait()
    for layer in range(2):
        total = got_gain[layer, 0].astype(F32) + got_gain[layer, 1].astype(F32)
        gain_s[layer] = total + got_gain[layer, 2].astype(F32) + got_gain[layer, 3].astype(F32)
    gains[...] = gain_s[...]
    x_load.wait()
    source = x_s
    for layer in range(2):
        q, kv, wide, totals, ot, out, hidden, gate_up, normed_two, product, normed = [
            ref.at[layer] for ref in per_layer
        ]
        project(
            source, gain_s[layer, 0:1, :], cos, sin, w_q, lambda: loaded(layer, 0), qkv_s.at[layer], normed
        )
        if layer == 0:
            begin(1, [0])
        spread = Spread(lines, qkv_s.at[layer], q, kv)
        spread.finish()
        if layer == 0:
            for gather in rest:
                gather.from_neighbours()
        attend(q, kv, low_s.at[layer], wide, totals, s_ref)
        if layer == 0:
            for gather in rest:
                gather.from_opposite()
        turn = Turn(lines, low_s.at[layer], ot)
        turn.finish()
        if layer == 0:
            for gather in rest:
                gather.from_beside()
            for gather in rest:
                gather.finish()
            begin(0, [1, 2, 3])
        mlp(
            ot, source, gain_s[layer, 1:2, :], w_o, w_u, w_d, lambda i: loaded(layer, i + 1),
            out, hidden, gate_up, normed_two, product,
        )
        if layer == 0:
            begin(1, [1, 2, 3])
        source = out


LAYER_SHAPES = (
    sds((4, GW, ROWS), BF16),
    sds((CTX, 2 * GW, ROWS), BF16),
    sds((4, GW, ROWS), F32),
    sds((GH, 8, 512), F32),
    sds((4, GW, ROWS), BF16),
    sds((ROWS, D), BF16),
    sds((ROWS, D), F32),
    sds((ROWS, 2 * FF), F32),
    sds((D, ROWS), BF16),
    sds((FF, ROWS), BF16),
    sds((D, ROWS), BF16),
)


def forward(inputs, gain, weights, tables):
    per_layer = [sds((2, *a.shape), a.dtype) for a in LAYER_SHAPES]
    full = full_shapes(weights)
    scratch = [
        pltpu.VMEM((ROWS, D), BF16),
        *[pltpu.VMEM((4 * w.shape[0], w.shape[1]), BF16) for w in weights],
        pltpu.VMEM((2, 4, 3 * GW, ROWS), BF16),
        pltpu.VMEM((2, 4, GW, ROWS), BF16),
        pltpu.VMEM((2048, 512), F32),
        pltpu.VMEM((2, 4, 16, D), BF16),
        DMA((2, 4, 4)),
        DMA((1,)),
        DMA((Lines.count,)),
        DMA((Lines.count,)),
        pltpu.VMEM((2, 16, D), F32),
    ]
    res = pl.pallas_call(
        forward_kernel,
        out_shape=[*per_layer, *full, sds((2, 16, D), F32)],
        in_specs=[VM, VM, ANY, ANY] + [ANY] * 4,
        out_specs=[VM] * 11 + [ANY] * 4 + [VM],
        scratch_shapes=scratch,
        compiler_params=pltpu.CompilerParams(
            collective_id=next(ids), has_side_effects=True, vmem_limit_bytes=VMEM_LIMIT
        ),
        name="forward",
    )(*tables, inputs, gain, *weights)
    return res[:11], res[11:15], res[15]


class Meet:
    def __init__(self, lines, layers, sib, far, both):
        s, c, z = here()
        self.core = core = lax.rem(c, 2)
        self.lines, self.far, self.both = lines, far, both
        self.sibling = sibling_of(s, c, z)
        peer = (1 - s, flip(c, 8) * core + c * (1 - core), z)
        self.apart = lines.put(layers.at[1 - s], far, peer)
        if sib is not None:
            self.close = lines.put(self.half(layers.at[s]), sib, self.sibling)

    def half(self, ref):
        return ref.at[:, 1 - self.core] if len(ref.shape) == 4 else ref

    def forward(self):
        self.apart.wait_recv()
        if self.both is not None:
            self.passed = self.lines.put(self.half(self.far), self.both, self.sibling)

    def finish(self):
        self.apart.wait_send()
        if self.both is not None:
            self.close.wait()
            self.passed.wait()


def meet_buffers(shape):
    half = (shape[0], *shape[2:]) if len(shape) == 4 else shape
    return [pltpu.VMEM(each, BF16) for each in (half, shape, half)]


class Show:
    def __init__(self, lines, layers, out):
        s, c, z = here()
        self.copy = lines.put(layers.at[1 - s], out.at[s], (1 - s, c, z))
        self.kept = lines.keep(layers.at[s], out.at[s])

    def finish(self):
        self.copy.wait()
        self.kept.wait()


class GiveBack:
    order = [14, 10, 12, 8, 6, 4, 2, 0]

    def __init__(self, lines, dq_ref, dkv_ref, dqo_ref, theirs):
        s, c, z = here()
        self.lines, self.dkv, self.theirs = lines, dkv_ref, theirs
        sibling = sibling_of(s, c, z)
        self.passed = {
            delta: lines.put(dkv_ref.at[flip(flip(c, 1), delta)], theirs.at[delta // 2], sibling)
            for delta in self.order
        }
        self.turn = Turn(lines, dq_ref, dqo_ref)

    def finish(self, total, sums):
        s, c, z = here()
        sends = []
        for delta in self.order:
            self.passed[delta].wait_recv()
            at = delta // 2
            both = self.dkv[flip(c, delta)].astype(F32) + self.theirs[at].astype(F32)
            total[at] = both.astype(BF16)
            if delta:
                peer = (s, flip(c, delta), z)
                sends.append(self.lines.put(total.at[at], sums.at[c // 2], peer))
            else:
                sends.append(self.lines.keep(total.at[at], sums.at[c // 2]))
        for copy in self.passed.values():
            copy.wait_send()
        for copy in sends:
            copy.wait()
        self.turn.finish()


class Reduce:
    order = [14, 10, 12, 8, 6, 4, 2]

    def __init__(self, lines, comb, got, own_sum, parts, red, fin):
        self.lines, self.comb, self.got, self.own_sum = lines, comb, got, own_sum
        self.parts, self.red, self.fin = parts, red, fin
        self.quarter = comb.shape[1] // 4
        s, c, z = here()
        self.peers = {delta: (s, flip(c, delta), z) for delta in self.order}
        self.sibling = sibling_of(s, c, z)

    def block(self, at):
        rows = pl.ds(pl.multiple_of(lax.rem(at // 2, 4) * self.quarter, 16), self.quarter)
        return rows, pl.ds(pl.multiple_of(at // 8 * (D // 2), 128), D // 2)

    def along(self):
        self.scatter = [
            self.lines.put(self.comb.at[peer[2]], self.got.at[i], peer) for i, peer in enumerate(z_peers())
        ]

    def plane(self):
        _, c, z = here()
        for copy in self.scatter:
            copy.wait()
        for at in range(0, self.comb.shape[1], 64):
            rows = slice(at, at + 64)
            both = self.comb[z, rows].astype(F32) + self.got[0, rows].astype(F32)
            both += self.got[1, rows].astype(F32) + self.got[2, rows].astype(F32)
            self.own_sum[rows] = both.astype(BF16)
        self.sends = [
            self.lines.put(self.own_sum.at[self.block(peer[1])], self.parts.at[c // 2], peer)
            for peer in self.peers.values()
        ]
        self.sends.append(self.lines.keep(self.own_sum.at[self.block(c)], self.parts.at[c // 2]))

    def spread(self):
        _, c, _ = here()
        for copy in self.sends:
            copy.wait()
        for at in range(0, self.quarter, 16):
            rows = slice(at, at + 16)
            total = self.parts[0, rows].astype(F32)
            for i in range(1, 8):
                total += self.parts[i, rows].astype(F32)
            self.red[rows] = total.astype(BF16)
        self.target = self.fin.at[lax.rem(c, 2)]
        place = self.target.at[self.block(c)]
        self.shown = {delta: self.lines.put(self.red, place, peer) for delta, peer in self.peers.items()}
        self.kept = self.lines.keep(self.red, place)
        self.passed = [self.lines.put(self.red, place, self.sibling)]

    def forward(self):
        _, c, _ = here()
        for delta in reversed(self.order):
            self.shown[delta].wait_recv()
            piece = self.target.at[self.block(flip(c, delta))]
            self.passed.append(self.lines.put(piece, piece, self.sibling))

    def finish(self):
        self.kept.wait()
        for copy in self.shown.values():
            copy.wait_send()
        for copy in self.passed:
            copy.wait()


def reduce_buffers(rows):
    return [
        pltpu.VMEM((4, rows, D), BF16),
        pltpu.VMEM((3, rows, D), BF16),
        pltpu.VMEM((rows, D), BF16),
        pltpu.VMEM((8, rows // 4, D // 2), BF16),
        pltpu.VMEM((rows // 4, D // 2), BF16),
    ]


LEFT_SHAPES = ((4, 2, 96, ROWS), (4, 2, 144, ROWS), (4, 2, 96, ROWS), (4, 2, 96, ROWS))
RIGHT_SHAPES = ((ROWS, 2 * FF), (ROWS, D), (ROWS, D))
HELD_SHAPES = (
    ((2, 4, GW, ROWS), BF16),
    ((2, CTX, 2 * GW, ROWS), BF16),
    ((2, 4, GW, ROWS), F32),
    ((2, GH, 8, 512), F32),
    ((2, ROWS, D), F32),
    ((2, ROWS, 2 * FF), F32),
    ((2, ROWS, D), BF16),
)


def backward_kernel(*refs):
    (
        (cos, sin, gains, cotangent, inputs, outs), full, far_held, lefts,
        (activations, input_grads, fin_m, fin_q), weights, held, left_meets, right_meets, gp_meets,
        reduce_m, reduce_q, scratch,
    ) = split_refs(refs, 6, 4, 6, 4, 4, 4, 7, 12, 9, 3, 5, 5, 21)
    (
        d_ot, d_o, gg, branch, grads, gp, starts, gain_sums, gains_far, grad_hidden, d_gain, gp_f32,
        dq, dkv, dqo, theirs, total, sums, load_sem, held_sem, lines_sem,
    ) = scratch
    s, c, z = here()
    lines = Lines(lines_sem.at[0], lines_sem.at[1])
    w_q, w_o, w_u, w_d = weights
    loads = [
        [
            shard_loads(full[i], layer, weights[i], load_sem.at[layer, i]) for i in range(4)
        ]
        for layer in range(2)
    ]

    def begin(layer, which):
        for i in which:
            for copy in loads[layer][i]:
                copy.start()

    def loaded(layer, i):
        for copy in loads[layer][i]:
            copy.wait()

    cot_load = fetch(cotangent.at[s, 0], grads.at[1], held_sem.at[2, 0])
    q, kv, wide, totals, hidden, gate_up, x = held
    hold = {}
    for layer in (1, 0):
        for i in (5, 4, 0, 1, 2, 3):
            hold[layer, i] = fetch(far_held[i].at[layer], held[i].at[layer], held_sem.at[layer, i])
        begin(1, [3, 2, 1, 0] if layer == 1 else [])
    x_loads = [fetch(inputs.at[s, 0], x.at[0], held_sem.at[0, 6]), fetch(outs.at[0], x.at[1], held_sem.at[1, 6])]
    greet(
        [sibling_of(s, c, z), *z_peers(), *beside_peers()]
        + [(s, flip(c, delta), z) for delta in range(2, CTX, 2)]
    )
    meets = [Meet(lines, left, *left_meets[3 * i : 3 * i + 3]) for i, left in enumerate(lefts)]
    shown = [Show(lines, outs, activations)]
    cot_load.wait()

    def run_mlp_back(layer):
        hold[layer, 5].wait()
        hold[layer, 4].wait()
        mlp_back(
            grads.at[layer], hidden.at[layer], gate_up.at[layer], gains[layer, 1:2, :], w_o, w_u, w_d,
            lambda i: loaded(layer, i + 1),
            d_ot.at[layer], grad_hidden, gg.at[layer], branch.at[layer], d_gain,
        )

    def run_attend_back(layer, start, stop):
        if start == 0:
            for i in range(4):
                hold[layer, i].wait()
        attend_back(
            start, stop, q.at[layer], kv.at[layer], wide.at[layer], totals.at[layer], d_o.at[layer], dq, dkv
        )

    def run_give_back(layer):
        work = GiveBack(lines, dq, dkv, dqo.at[layer], theirs.at[layer])
        work.finish(total, sums.at[layer])

    def run_qkv_back(layer):
        x_loads[layer].wait()
        qkv_back(
            dqo.at[layer], sums.at[layer], x.at[layer], gains[layer, 0:1, :], cos, sin, grad_hidden, d_gain,
            w_q, lambda: loaded(layer, 0),
            [starts.at[1], grads.at[0]] if layer else [starts.at[0]],
            gp.at[layer], gain_sums.at[layer], gp_f32,
        )

    run_mlp_back(1)
    begin(0, [3, 2, 1])
    turn = Turn(lines, d_ot.at[1], d_o.at[1])
    for work in meets:
        work.forward()
    turn.finish()
    run_attend_back(1, 0, GH)
    for work in meets + shown:
        work.finish()
    run_give_back(1)
    run_qkv_back(1)
    begin(0, [0])
    run_mlp_back(0)
    turn = Turn(lines, d_ot.at[0], d_o.at[0])
    rights = (gg, grads, branch)
    meets = [Meet(lines, right, *right_meets[3 * i : 3 * i + 3]) for i, right in enumerate(rights)]
    turn.finish()
    run_attend_back(0, 0, 1)
    for work in meets:
        work.forward()
    run_attend_back(0, 1, 2)
    for work in meets:
        work.finish()
    part_m = Reduce(lines, *reduce_m, fin_m)
    part_q = Reduce(lines, *reduce_q, fin_q)
    comb_m, comb_q = reduce_m[0], reduce_q[0]
    for i, at in ((0, 0), (2, 288), (1, 384)):
        weight_product(
            comb_m, at, lefts[i], left_meets[3 * i : 3 * i + 3],
            (gg, grads, branch)[i], right_meets[3 * i : 3 * i + 3],
        )
    comb_m[:, 528:, :] = jnp.zeros((4, 48, D), BF16)
    part_m.along()
    run_attend_back(0, 2, GH)
    run_give_back(0)
    run_qkv_back(0)
    meets = [
        Meet(lines, gp, *gp_meets),
        Meet(lines, gain_sums, None, gains_far, None),
    ]
    shown = [Show(lines, starts, input_grads)]
    for work in meets:
        work.forward()
    for work in meets:
        work.finish()
    weight_product(comb_q, 0, lefts[3], left_meets[9:], gp, gp_meets)
    gain_rows = (gain_sums[s].astype(F32) + gains_far[...].astype(F32)).astype(BF16)
    for shard in range(4):
        comb_q[shard, 288:304, :] = gain_rows
        comb_q[shard, 304:, :] = jnp.zeros((16, D), BF16)
    part_q.along()
    part_m.plane()
    part_q.plane()
    part_m.spread()
    part_q.spread()
    part_m.forward()
    part_q.forward()
    for work in [part_m, part_q, *shown]:
        work.finish()


def backward(tables, gains, cotangent, inputs, full, stored):
    q, kv, wide, totals, ot, outs, hidden, gate_up, normed_two, product, normed = stored
    lefts = [
        a.reshape(2, *shape) for a, shape in zip((normed_two, product, ot, normed), LEFT_SHAPES)
    ]
    scratch = [
        *[pltpu.VMEM((4 * w.shape[2], w.shape[3]), BF16) for w in full],
        *[pltpu.VMEM(*held) for held in HELD_SHAPES],
        *[buffer for shape in LEFT_SHAPES for buffer in meet_buffers(shape)],
        *[buffer for shape in RIGHT_SHAPES for buffer in meet_buffers(shape)],
        *meet_buffers((ROWS, 3 * D)),
        *reduce_buffers(MLP_ROWS),
        *reduce_buffers(QKV_ROWS),
        pltpu.VMEM((2, 4, GW, ROWS), BF16),
        pltpu.VMEM((2, 4, GW, ROWS), BF16),
        pltpu.VMEM((2, ROWS, 2 * FF), BF16),
        pltpu.VMEM((2, ROWS, D), BF16),
        pltpu.VMEM((2, ROWS, D), BF16),
        pltpu.VMEM((2, ROWS, 3 * D), BF16),
        pltpu.VMEM((2, ROWS, D), BF16),
        pltpu.VMEM((2, 16, D), BF16),
        pltpu.VMEM((16, D), BF16),
        pltpu.VMEM((ROWS, D), F32),
        pltpu.VMEM((1, D), F32),
        pltpu.VMEM((3 * D, ROWS), F32),
        pltpu.VMEM((4, GW, ROWS), BF16),
        pltpu.VMEM((CTX, 2 * GW, ROWS), BF16),
        pltpu.VMEM((2, 4, GW, ROWS), BF16),
        pltpu.VMEM((2, 8, 2 * GW, ROWS), BF16),
        pltpu.VMEM((8, 2 * GW, ROWS), BF16),
        pltpu.VMEM((2, 8, 2 * GW, ROWS), BF16),
        DMA((2, 4, 4)),
        DMA((3, 7)),
        DMA((2, Lines.count)),
    ]
    return pl.pallas_call(
        backward_kernel,
        out_shape=[
            sds((2, ROWS, D), BF16), sds((2, ROWS, D), BF16),
            sds((2, MLP_ROWS, D), BF16), sds((2, QKV_ROWS, D), BF16),
        ],
        in_specs=[VM] * 3 + [ANY] * 3 + [ANY] * 4 + [ANY] * 6 + [VM] * 4,
        out_specs=[ANY, ANY, VM, VM],
        scratch_shapes=scratch,
        compiler_params=pltpu.CompilerParams(
            collective_id=next(ids), has_side_effects=True, vmem_limit_bytes=VMEM_LIMIT
        ),
        name="backward",
    )(*tables, gains, cotangent, inputs, outs, *full, q, kv, wide, totals, hidden, gate_up, *lefts)


def rope_tables():
    positions = (lax.axis_index("ctx") * ROWS + lax.iota(jnp.int32, ROWS)).astype(F32)
    frequency = 1.0 / 160000.0 ** (jnp.arange(HEAD_DIM // 2, dtype=F32) * 2.0 / HEAD_DIM)
    angles = frequency[:, None] * positions[None, :]
    return jnp.cos(angles), jnp.sin(angles)


def local(inputs, cotangent, attn_gain, qkv_weight, out_weight, mlp_gain, up_weight, down_weight):
    z = lax.axis_index("wshard")
    gain = jnp.concatenate([attn_gain, mlp_gain], axis=0)
    lanes = lax.broadcasted_iota(jnp.int32, (2, 4, 192), 1) == z
    gain = jnp.where(lanes, gain[:, None, :], jnp.zeros((), BF16)).reshape(2, D)
    gain = jnp.pad(gain, ((0, 14), (0, 0)))
    tables = rope_tables()
    stored, full, gains = forward(
        inputs, gain, [w[0] for w in (qkv_weight, out_weight, up_weight, down_weight)], tables
    )
    activations, input_grads, fin_m, fin_q = backward(tables, gains, cotangent, inputs, full, stored)
    grad_up, grad_out, grad_down, grad_qkv, gain_sums = compute_call(
        assemble_kernel,
        (fin_m, fin_q),
        [sds(shape, F32) for shape in ((192, 3 * D), (192, D), (288, D), (192, 3 * D), (16, D))],
        name="assemble",
    )
    gain_sums = lax.dynamic_slice_in_dim(gain_sums[:2], z * 192, 192, 1)
    return (
        activations[None, :, None],
        input_grads[None, :, None],
        gain_sums[0:1],
        grad_qkv[None],
        grad_out[None],
        gain_sums[1:2],
        grad_up[None],
        grad_down[None],
    )


def solution(mesh):
    global ids
    ids = iter(range(1, 64))
    placed = (
        P(None, "wshard", "ctx", None),
        P(None, "wshard", "ctx", None),
        P("section", "wshard"),
        P("section", "wshard", None),
        P("section", "wshard", None),
        P("section", "wshard"),
        P("section", "wshard", None),
        P("section", "wshard", None),
    )
    return jax.shard_map(
        local,
        mesh=mesh,
        in_specs=placed,
        out_specs=(
            P("section", None, "wshard", "ctx", None),
            P("section", None, "wshard", "ctx", None),
            P("section", "wshard"),
            P("section", "wshard", None),
            P("section", "wshard", None),
            P("section", "wshard"),
            P("section", "wshard", None),
            P("section", "wshard", None),
        ),
        check_vma=False,
    )
```

time: 424 us -> 322 us (0.76)
  Pallas kernels: 412 us -> 314 us
    pallas_call x16 -> x2, Pallas kernels: 273 us -> 174 us  [the longest x1 170 us: backward(): pl.pallas_call(backward_kernel, out_shape=[sds((2, ROWS, D), BF16), sds((...]
where the time goes in v5:
time: 322 us; the launch traced here: 319 us
  Pallas kernels  314 us (98%)
  local copies, waits for them, and re-layouts  3.75 us (1%)
    pallas_call x1, Pallas kernels, backward(): pl.pallas_call(backward_kernel, out_shape=[sds((2, ROWS, D), BF16), sds((...  170 us
    pallas_call x1, Pallas kernels, forward(): pl.pallas_call(forward_kernel, out_shape=[*per_layer, *full, sds((2, 16,...  139 us

profile of v5, /device:TPU:25, one launch (start us, length us, event | category | flops | bytes accessed | tf_op | source)
XLA Modules:
  0.0 319.5 jit_solution(5774263763202040891)
XLA Ops:
  0.7 0.8 multiply_sine_fusion
  1.4 0.1 iota.23
  1.5 0.1 iota.24
  1.6 0.7 pad_maximum_fusion
  2.3 0.1 broadcast_in_dim.36
  2.4 0.6 pad.4.refs_3_
  3.0 139.3 %forward.1 = (bf16[2,4,192,128]{3,2,1,0:T(8,128)(2,1)}, bf16[2,16,384,128]{3,2,1,0:T(8,128)(2,1)}, f32[2,4,192,128]{3,2,1,0:T(8,128)}, f32[2,3,8,512]{3,2,1,0:T(...) custom-call(f32[32,128]{1,0:T(8,128)} %get-tuple-element.69.refs_0_,, ...), custom_call_target="tpu_custom_call" | custom-call | tf_op jit(solution)/shard_map/forward/pallas_call | solution.py:630
  142.3 170.0 %backward.1 = (bf16[2,128,768]{2,1,0:T(8,128)(2,1)}, bf16[2,128,768]{2,1,0:T(8,128)(2,1)}, bf16[2,576,768]{2,1,0:T(8,128)(2,1)}, bf16[2,320,768]{2,1,0:T(8,128)(2,1)}) custom-call(f32[32,128]{1,0:T(8,128)} %get-tuple-element.69.refs_0_, f32[32,128]{1,0:T(8,128)} %get-tuple-element.68.refs_1_, f32[2,16,768]{2,1,0:T(8,128)} %get-tuple-element.33.refs_2_, ...), custom_call_target="tpu_custom_call" | custom-call | tf_op jit(solution)/shard_map/backward/pallas_call | solution.py:979
  312.3 0.0 copy-start.1
  312.4 0.0 copy-start
  312.4 4.2 %assemble.1 = (f32[192,2304]{1,0:T(8,128)}, f32[192,768]{1,0:T(8,128)}, f32[288,768]{1,0:T(8,128)}, f32[192,2304]{1,0:T(8,128)}, f32[16,768]{1,0:T(8,128)}) custom-call(bf16[2,576,768]{2,1,0:T(8,128)(2,1)} %get-tuple-element.51.mlp_ref, bf16[2,320,768]{2,1,0:T(8,128)(2,1)} %get-tuple-element.52.qkv_in_ref), custom_call_target="tpu_custom_call" | custom-call | tf_op jit(solution)/shard_map/assemble/pallas_call | solution.py:42
  316.6 0.7 slice.9
  317.3 0.6 fusion
  318.0 0.0 copy-done.1
  318.0 0.7 copy.20
  318.7 0.0 copy-done
  318.7 0.7 copy.21
  (5 shorter events, 0.0 us)
Async XLA Ops:
  312.3 5.6 %copy-start.1 = (bf16[2,128,768]{2,1,0:T(8,128)(2,1)S(1)}, bf16[2,128,768]{2,1,0:T(8,128)(2,1)}, u32[]{:S(2)}) copy-start(bf16[2,128,768]{2,1,0:T(8,128)(2,1)} %get-tuple-element.49) | copy-start | bytes 1179652
  312.4 6.4 %copy-start = (bf16[2,128,768]{2,1,0:T(8,128)(2,1)S(1)}, bf16[2,128,768]{2,1,0:T(8,128)(2,1)}, u32[]{:S(2)}) copy-start(bf16[2,128,768]{2,1,0:T(8,128)(2,1)} %get-tuple-element.50) | copy-start | bytes 1179652
